TPU v7x, 256 devices: a whole 4x4x8 slice. The times are simulated.
256 devices in a mesh: row: 32 (over y, z), col: 8 (over x, core).
Axes of the slice: x: 4, y: 4, z: 8, core: 2. Of those that a mesh axis runs over, the one named last changes fastest.
Arguments:
- kernel_configs: float32 [8, 2048, 16384], P(None, 'row', 'col'), may hold values from -1 to 2, as said below
- epoch_kernel: float32 [256, 256], replicated, may hold values from -1 to 2, as said below
- lengths: int32 [16384], P(('col', 'row')), may hold values from 1 to 256
- noise: float32 [16384], P(('col', 'row')), may hold values from 0.1 to 1
- curves: float32 [16384, 256], P(('col', 'row')), may hold values from -33 to 33
Outputs:
- solution: float32 [16384, 256], P(('col', 'row'))
- residual: float32 [16384, 256], P(('col', 'row'))
Inputs may be any that keep to these rules, and one draw needn't show every extreme that they name: `kernel_configs`: reshaped to 16384 x 16384 by merging the first two dimensions, the matrix is symmetric positive definite. `epoch_kernel`: symmetric positive definite.
All inputs are finite; a program needn't handle non-finite values.
Results may differ from a plain program's by a relative error of at most 0.00026.
Values sent between devices are 32-bit elements; how exact they have to be, the bound alone decides.
No kernel may reach another device: no remote copies, remote signals or barrier semaphores. Data moves between devices by JAX's collectives and lax.ppermute only.
A program may use at most 64 MiB of HBM per device.

v0:
```python
import jax
import jax.numpy as jnp
from jax import lax
from jax.sharding import PartitionSpec as P

ITERS = 2


def per_device(kernel_configs, epoch_kernel, lengths, noise, curves):
    row_count = curves.shape[0]
    epochs = curves.shape[1]
    epoch_index = lax.broadcasted_iota(jnp.int32, (row_count, epochs), 1)
    curve_mask = (epoch_index < lengths[:, None]).astype(jnp.float32)
    local_tile = kernel_configs.reshape(-1, kernel_configs.shape[2])

    def squares(residual):
        return lax.psum(jnp.sum(residual * residual), ("row", "col"))

    solution = jnp.zeros_like(curves)
    residual = curves * curve_mask
    direction = residual
    norm_now = squares(residual)
    for iteration in range(ITERS):
        masked = direction * curve_mask
        partial_value = jnp.dot(
            local_tile,
            lax.all_gather(masked, "row", axis=0, tiled=True),
            precision=lax.Precision.HIGHEST,
            preferred_element_type=jnp.float32,
        )
        summed = lax.psum_scatter(partial_value, "col", scatter_dimension=0, tiled=True)
        smoothed = jnp.dot(
            summed,
            epoch_kernel,
            precision=lax.Precision.HIGHEST,
            preferred_element_type=jnp.float32,
        )
        applied = curve_mask * smoothed + noise[:, None] * direction
        step_size = norm_now / lax.psum(jnp.sum(direction * applied), ("row", "col"))
        solution = solution + step_size * direction
        residual = residual - step_size * applied
        norm_next = squares(residual)
        direction = residual + norm_next / norm_now * direction
        norm_now = norm_next
    return (solution, residual)


def solution(mesh):
    in_specs = (
        P(None, "row", "col"),
        P(),
        P(("col", "row")),
        P(("col", "row")),
        P(("col", "row"), None),
    )
    out_specs = (P(("col", "row"), None), P(("col", "row"), None))
    return jax.shard_map(
        per_device, mesh=mesh, in_specs=in_specs, out_specs=out_specs, check_vma=False
    )
```

profile of v0, /device:TPU:6, one launch (start us, length us, event | category | flops | bytes accessed | tf_op | source)
XLA Modules:
  0.0 488.0 jit_solution(11808340311915801537)
XLA Ops:
  7.2 0.0 copy-start
  7.2 0.0 all-gather.3.cloned.1.call-start
  7.2 1.6 fusion.3
  8.8 0.0 all-gather.3.cloned.1.call-update
  8.8 0.0 reduce-scatter.7.cloned.1.call-start
  8.9 83.2 %all-gather.3.cloned.1.call-done = f32[2048,256]{1,0:T(8,128)} async-done(((f32[64,256]{1,0:T(8,128)}), f32[2048,256]{1,0:T(8,128)}) %all-gather.3.cloned.1.call-update) | async-done | bytes 2097168 | tf_op jit(solution)/shard_map/all_gather | solution.py:27
  92.1 0.0 copy-start.1
  92.1 0.0 copy-start.2
  92.1 9.3 %convolution_bitcast_fusion.1 = f32[512,256]{0,1:T(8,128)S(1)} fusion(f32[2048,256]{1,0:T(8,128)} %all-gather.3.cloned.1.call-done, f32[512,2048]{1,0:T(8,128)} %bitcast.15), kind=kOutput, calls=%fused_computation.1 | convolution fusion | flops 3221225472 | bytes 6815744 | tf_op jit(solution)/shard_map/dot_general | solution.py:25
  101.4 1.0 copy.7
  102.4 0.0 reduce-scatter.7.cloned.1.call-update
  102.4 0.0 all-gather.5.cloned.1.call-start
  102.5 27.7 %reduce-scatter.7.cloned.1.call-done = f32[64,256]{1,0:T(8,128)} async-done(((f32[512,256]{1,0:T(8,128)}), f32[64,256]{1,0:T(8,128)}) %reduce-scatter.7.cloned.1.call-update) | async-done | bytes 65552
  130.2 0.0 copy-done
  130.2 0.0 copy-done.1
  130.2 0.0 copy-done.2
  130.2 0.0 copy-done.3
  130.2 1.7 multiply_reduce_fusion.2
  131.9 77.3 %all-reduce = (f32[]{:T(128)}, f32[]{:T(128)}) all-reduce(f32[]{:T(128)} %get-tuple-element.3, f32[]{:T(128)} %get-tuple-element.2), channel_id=1, replica_groups=mesh['row'=32,'col'=8] {'row','col'}, use_global_device_ids=true, to_apply=%region_1.0 | all-reduce | flops 2 | bytes 16 | tf_op jit(solution)/shard_map/psum | solution.py:17
  210.5 0.7 multiply_reduce_fusion.1
  211.2 74.2 %psum.30 = f32[]{:T(128)} all-reduce(f32[]{:T(128)} %multiply_reduce_fusion.1), channel_id=1, replica_groups=mesh['row'=32,'col'=8] {'row','col'}, use_global_device_ids=true, to_apply=%region_6.0 | all-reduce | flops 1 | bytes 8 | tf_op jit(solution)/shard_map/psum | solution.py:17
  286.7 0.7 fusion.2
  287.4 0.0 all-gather.5.cloned.1.call-update
  287.5 0.0 reduce-scatter.9.cloned.1.call-start
  287.5 75.0 %all-gather.5.cloned.1.call-done = f32[2048,256]{1,0:T(8,128)} async-done(((f32[64,256]{1,0:T(8,128)}), f32[2048,256]{1,0:T(8,128)}) %all-gather.5.cloned.1.call-update) | async-done | bytes 2097168 | tf_op jit(solution)/shard_map/all_gather | solution.py:27
  362.5 9.3 %convolution_bitcast_fusion = f32[512,256]{0,1:T(8,128)S(1)} fusion(f32[2048,256]{1,0:T(8,128)} %all-gather.5.cloned.1.call-done, f32[512,2048]{1,0:T(8,128)} %bitcast.16), kind=kOutput, calls=%fused_computation | convolution fusion | flops 3221225472 | bytes 6815744 | tf_op jit(solution)/shard_map/dot_general | solution.py:25
  371.8 1.0 copy.9
  372.8 0.0 reduce-scatter.9.cloned.1.call-update
  372.8 27.7 %reduce-scatter.9.cloned.1.call-done = f32[64,256]{1,0:T(8,128)} async-done(((f32[512,256]{1,0:T(8,128)}), f32[64,256]{1,0:T(8,128)}) %reduce-scatter.9.cloned.1.call-update) | async-done | bytes 65552
  400.6 1.7 multiply_reduce_fusion
  402.3 77.2 %psum.31 = f32[]{:T(128)} all-reduce(f32[]{:T(128)} %get-tuple-element.11), channel_id=1, replica_groups=mesh['row'=32,'col'=8] {'row','col'}, use_global_device_ids=true, to_apply=%region_9.0 | all-reduce | flops 1 | bytes 8 | tf_op jit(solution)/shard_map/psum | solution.py:39
  480.7 0.7 multiply_subtract_fusion
  (1 shorter events, 0.0 us)
Async XLA Ops:
  7.2 123.0 %copy-start = (f32[256,256]{1,0:T(8,128)S(1)}, f32[256,256]{1,0:T(8,128)}, u32[]{:S(2)}) copy-start(f32[256,256]{1,0:T(8,128)} %param.6) | copy-start | bytes 786436
  7.2 84.9 %all-gather.3.cloned.1.call-start = ((), (), s32[]{:S(2)}) async-start(), calls=%async_computation.2 | async-start | bytes 2162688 | tf_op jit(solution)/shard_map/all_gather | solution.py:27
  8.8 121.3 %reduce-scatter.7.cloned.1.call-start = ((), (), s32[]{:S(2)}) async-start(), calls=%async_computation.4 | async-start | bytes 589824
  92.1 38.1 %copy-start.1 = (f32[64,256]{1,0:T(8,128)S(1)}, f32[64,256]{1,0:T(8,128)}, u32[]{:S(2)}) copy-start(f32[64,256]{1,0:T(8,128)} %param.9) | copy-start | bytes 196612
  92.1 38.1 %copy-start.2 = (s32[64]{0:T(128)S(1)}, s32[64]{0:T(128)}, u32[]{:S(2)}) copy-start(s32[64]{0:T(128)} %param.7) | copy-start | bytes 772
  92.1 38.1 %copy-start.3 = (f32[64]{0:T(128)S(1)}, f32[64]{0:T(128)}, u32[]{:S(2)}) copy-start(f32[64]{0:T(128)} %param.8) | copy-start | bytes 772
  102.4 260.0 %all-gather.5.cloned.1.call-start = ((), (), s32[]{:S(2)}) async-start(), calls=%async_computation.3 | async-start | bytes 2162688 | tf_op jit(solution)/shard_map/all_gather | solution.py:27
  287.5 113.1 %reduce-scatter.9.cloned.1.call-start = ((), (), s32[]{:S(2)}) async-start(), calls=%async_computation.5 | async-start | bytes 589824
Sparse Core Ops, SparseCore 0:
  11.2 80.8 all-gather.2
  102.6 27.5 reduce-scatter.6
  287.6 74.8 all-gather.4
  372.9 27.5 reduce-scatter.8
where the time goes:
time: 492 us; the launch traced here: 488 us
  blocking collectives  229 us (47%)
  waiting for transfers between devices  214 us (43%)
  matrix products  22.1 us (4%)
  between operations  17.8 us (4%)
    all_gather x2, waiting for transfers between devices, per_device(): lax.all_gather(masked, 'row', axis=0, tiled=True)  158 us
    psum x2, blocking collectives, squares(): return lax.psum(jnp.sum(residual * residual), ('row', 'col'))  151 us
    psum x1, blocking collectives, per_device(): lax.psum(jnp.sum(direction * applied), ('row', 'col'))  77.2 us
    unnamed x6, waiting for transfers between devices  55.5 us
    dot_general x2, matrix products, per_device(): jnp.dot(local_tile, lax.all_gather(masked, 'row', axis=0, tiled=True), pr...  18.7 us
  transfers between devices with their start and end apart: 4, of which 4 were waited for; matrix products, arithmetic and copies ran while one was open for 0% of the time, Pallas kernels for 0%

commit v1 on v0

v1 whole, which is shorter than its diff:
```python
import jax
import jax.numpy as jnp
from jax import lax
from jax.experimental import pallas as pl
from jax.experimental.pallas import tpu as pltpu
from jax.sharding import PartitionSpec as P

NY, NZ, NX = 4, 8, 4
BLOCK = 64
EPOCHS = 256
F32 = jnp.float32
BF16 = jnp.bfloat16


def class_member(k, j):
    kh, kl, jh, jl = k // 2, k % 2, j // 4, j % 4
    return (kl + 2 * jh) * NZ + 2 * jl + (kh + jh) % 2


CLASSES = [[class_member(k, j) for j in range(8)] for k in range(4)]


def shift_y(d):
    return [(y * NZ + z, ((y + d) % NY) * NZ + z) for y in range(NY) for z in range(NZ)]


def shift_z(d):
    return [(y * NZ + z, y * NZ + (z + d) % NZ) for y in range(NY) for z in range(NZ)]


def shift_x(d):
    return [(x * 2 + c, ((x + d) % NX) * 2 + c) for x in range(NX) for c in range(2)]


SIBLING = [(c, c ^ 1) for c in range(8)]


def split(value):
    high = lax.reduce_precision(value, 8, 7)
    return high.astype(BF16), (value - high).astype(BF16)


def gather_row(block):
    copies = jnp.broadcast_to(block[None], (8, BLOCK, EPOCHS))
    own = lax.all_to_all(copies, "row", 0, 0, axis_index_groups=CLASSES)
    next_y = lax.ppermute(own, "row", shift_y(-1))
    last_y = lax.ppermute(own, "row", shift_y(1))
    next_z = lax.ppermute(own[:4], "row", shift_z(-1))
    last_z = lax.ppermute(own[4:], "row", shift_z(1))
    return own, next_y, next_z, last_z, last_y


def product_kernel(place, own, next_y, next_z, last_z, last_y, k_high, k_low, keep, send, high, low):
    colour, x, core = place[0], place[1], place[2]

    def put(ref, slot, first):
        k = lax.rem(colour + slot, 4)
        kh, kl = k // 2, lax.rem(k, 2)
        for j in range(ref.shape[0]):
            jh, jl = (j + first) // 4, (j + first) % 4
            row = (kl + 2 * jh) * NZ + 2 * jl + lax.rem(kh + jh, 2)
            at = pl.ds(pl.multiple_of(row * BLOCK, BLOCK), BLOCK)
            value = ref[j]
            top = value.astype(BF16)
            high[at, :] = top
            low[at, :] = (value - top.astype(F32)).astype(BF16)

    put(own, 0, 0)
    put(next_y, 1, 0)
    put(next_z, 2, 0)
    put(last_z, 2, 4)
    put(last_y, 3, 0)
    for b in range(8):
        rows = pl.ds(b * BLOCK, BLOCK)
        part = jnp.dot(k_high[rows, :], high[...], preferred_element_type=F32)
        part += jnp.dot(k_high[rows, :], low[...], preferred_element_type=F32)
        part += jnp.dot(k_low[rows, :], high[...], preferred_element_type=F32)
        dx = lax.rem(b // 2 - x + NX, NX)

        @pl.when(core == b % 2)
        def _():
            keep[dx] = part

        @pl.when(core != b % 2)
        def _():
            send[dx] = part


def product(place, parts, k_high, k_low):
    vmem = pl.BlockSpec(memory_space=pltpu.VMEM)
    half = jax.ShapeDtypeStruct((NX, BLOCK, EPOCHS), F32)
    return pl.pallas_call(
        product_kernel,
        out_shape=(half, half),
        in_specs=[pl.BlockSpec(memory_space=pltpu.SMEM)] + [vmem] * 7,
        out_specs=(vmem, vmem),
        scratch_shapes=[pltpu.VMEM((2048, EPOCHS), BF16), pltpu.VMEM((2048, EPOCHS), BF16)],
        compiler_params=pltpu.CompilerParams(vmem_limit_bytes=24 * 1024 * 1024),
        cost_estimate=pl.CostEstimate(
            flops=2 * 3 * 512 * 2048 * EPOCHS, bytes_accessed=7 * 1024 * 1024, transcendentals=0
        ),
    )(place, *parts, k_high, k_low)


def scatter_col(keep, send):
    total = keep + lax.ppermute(send, "col", SIBLING)
    got = [lax.ppermute(total[d], "col", shift_x(d)) for d in range(1, NX)]
    return total[0] + got[0] + got[1] + got[2]


def reduce_all(values):
    tile = jnp.zeros((8, 128), F32)
    lane = lax.broadcasted_iota(jnp.int32, (8, 128), 1)
    for i, v in enumerate(values):
        tile = jnp.where(lane == i, v, tile)
    tile = tile + lax.ppermute(tile, "col", SIBLING)
    tile = tile + sum(lax.ppermute(tile, "col", shift_x(d)) for d in range(1, NX))
    copies = jnp.broadcast_to(tile[None], (32, 8, 128))
    tile = jnp.sum(lax.all_to_all(copies, "row", 0, 0), axis=0)
    return [tile[0, i] for i in range(len(values))]


def per_device(kernel_configs, epoch_kernel, lengths, noise, curves):
    epoch_index = lax.broadcasted_iota(jnp.int32, (BLOCK, EPOCHS), 1)
    mask = (epoch_index < lengths[:, None]).astype(F32)
    row, col = lax.axis_index("row"), lax.axis_index("col")
    colour = lax.rem(row // NZ + 2 * lax.rem(row, NZ), 4)
    place = jnp.stack([colour, col // 2, lax.rem(col, 2)]).astype(jnp.int32)
    k_high, k_low = split(kernel_configs.reshape(-1, kernel_configs.shape[2]))

    def apply(field):
        parts = gather_row(field * mask)
        summed = scatter_col(*product(place, parts, k_high, k_low))
        smoothed = jnp.dot(summed, epoch_kernel, precision=lax.Precision.HIGHEST, preferred_element_type=F32)
        return mask * smoothed + noise[:, None] * field

    r0 = curves * mask
    w1 = apply(r0)
    w2 = apply(w1)
    rr, rw, ww, wv = reduce_all([jnp.sum(r0 * r0), jnp.sum(r0 * w1), jnp.sum(w1 * w1), jnp.sum(w1 * w2)])
    a0 = rr / rw
    rr1 = rr - 2.0 * a0 * rw + a0 * a0 * ww
    b0 = rr1 / rr
    c0 = 1.0 + b0
    curvature = c0 * c0 * rw - 2.0 * a0 * c0 * ww + a0 * a0 * wv
    a1 = rr1 / curvature
    r1 = r0 - a0 * w1
    p1 = r1 + b0 * r0
    return a0 * r0 + a1 * p1, r1 - a1 * (c0 * w1 - a0 * w2)


def solution(mesh):
    in_specs = (
        P(None, "row", "col"),
        P(),
        P(("col", "row")),
        P(("col", "row")),
        P(("col", "row"), None),
    )
    out_specs = (P(("col", "row"), None), P(("col", "row"), None))
    return jax.shard_map(
        per_device, mesh=mesh, in_specs=in_specs, out_specs=out_specs, check_vma=False
    )
```

time: 492 us -> 160 us (0.33)
  waiting for transfers between devices: 214 us -> 32.6 us
  blocking collectives: 229 us -> 64.5 us
  matrix products: 22.1 us -> 1.18 us
  starting transfers between devices: 0.16 us -> 20.4 us
  Pallas kernels: 0 us -> 18.6 us
  between operations: 17.8 us -> 6.64 us
  other arithmetic: 3.74 us -> 12.6 us
    psum x3 -> x0, blocking collectives: 229 us -> none  [the longest x2 151 us: squares(): return lax.psum(jnp.sum(residual * residual), ('row', 'col'))]
    all_gather x2 -> x0, waiting for transfers between devices: 158 us -> none  [per_device(): lax.all_gather(masked, 'row', axis=0, tiled=True)]
    all_to_all x0 -> x3, blocking collectives: none -> 64.5 us  [the longest x2 49.5 us: gather_row(): own = lax.all_to_all(copies, 'row', 0, 0, axis_index_groups=CLASSES)]
    unnamed x6 -> x0, waiting for transfers between devices: 55.5 us -> none
    ppermute x0 -> x20, waiting for transfers between devices: none -> 32.6 us  [the longest x6 7.54 us: scatter_col(): got = [lax.ppermute(total[d], 'col', shift_x(d)) for d in range(1, NX)]]
    dot_general x4 -> x2, matrix products: 22.1 us -> 1.18 us  [apply(): jnp.dot(summed, epoch_kernel, precision=lax.Precision.HIGHEST, preferred_...]
    ppermute x0 -> x20, starting transfers between devices: none -> 20.4 us  [the longest x6 8.33 us: scatter_col(): got = [lax.ppermute(total[d], 'col', shift_x(d)) for d in range(1, NX)]]
    pallas_call x0 -> x2, Pallas kernels: none -> 18.6 us  [product(): pl.pallas_call(product_kernel, out_shape=(half, half), in_specs=[pl.Block...]
  transfers between devices with their start and end apart: 4 -> 20, of which waited for: 4 -> 17; matrix products, arithmetic and copies ran while one was open for 0% -> 3% of each run, Pallas kernels for 0% -> 0%
where the time goes in v1:
time: 160 us
  blocking collectives  64.5 us (40%)
  waiting for transfers between devices  32.6 us (20%)
  starting transfers between devices  20.4 us (13%)
  Pallas kernels  18.6 us (12%)
  other arithmetic  12.6 us (8%)
  between operations  6.64 us (4%)
  local copies, waits for them, and re-layouts  3.23 us (2%)
    all_to_all x2, blocking collectives, gather_row(): own = lax.all_to_all(copies, 'row', 0, 0, axis_index_groups=CLASSES)  49.5 us
    pallas_call x2, Pallas kernels, product(): pl.pallas_call(product_kernel, out_shape=(half, half), in_specs=[pl.Block...  18.6 us
    all_to_all x1, blocking collectives, reduce_all(): tile = jnp.sum(lax.all_to_all(copies, 'row', 0, 0), axis=0)  15 us
    ppermute x6, starting transfers between devices, scatter_col(): got = [lax.ppermute(total[d], 'col', shift_x(d)) for d in range(1, NX)]  8.33 us
    ppermute x6, waiting for transfers between devices, scatter_col(): got = [lax.ppermute(total[d], 'col', shift_x(d)) for d in range(1, NX)]  7.54 us
    ppermute x2, waiting for transfers between devices, gather_row(): next_y = lax.ppermute(own, 'row', shift_y(-1))  4.91 us
    ppermute x3, waiting for transfers between devices, reduce_all(): lax.ppermute(tile, 'col', shift_x(d))  4.81 us
    convert_element_type x1, other arithmetic, split(): return (high.astype(BF16), (value - high).astype(BF16))  4.38 us
  transfers between devices with their start and end apart: 20, of which 17 were waited for; matrix products, arithmetic and copies ran while one was open for 3% of the time, Pallas kernels for 0%

profile of v1, /device:TPU:6, one launch (start us, length us, event | category | flops | bytes accessed | tf_op | source)
XLA Modules:
  0.0 159.9 jit_solution(12600895640792110548)
XLA Ops:
  1.7 28.3 %all_to_all.15.own = f32[8,64,256]{2,1,0:T(8,128)S(1)} all-to-all(f32[8,64,256]{2,1,0:T(8,128)S(1)} %broadcast_in_dim.37), channel_id=1, replica_groups={{0,16,32,48,136,152,168,184},{64,80,96,112,200,216,232,248},{8,24,40,56..., dimensions={0} | all-to-all | bytes 1048576 | tf_op jit(solution)/shard_map/all_to_all | solution.py:45
  31.8 1.1 collective-permute-start.2
  33.4 1.5 collective-permute-start.3
  34.9 4.4 %fusion = (bf16[512,2048]{1,0:T(8,128)(2,1)S(1)}, bf16[512,2048]{1,0:T(8,128)(2,1)}) fusion(f32[8,64,2048]{2,1,0:T(8,128)} %param.5), kind=kLoop, calls=%fused_computation.2 | loop fusion | flops 4194304 | bytes 8388608 | tf_op jit(solution)/shard_map/convert_element_type | solution.py:40
  39.7 3.9 %collective-permute-done.next_y = f32[8,64,256]{2,1,0:T(8,128)S(1)} collective-permute-done((f32[8,64,256]{2,1,0:T(8,128)S(1)}, f32[8,64,256]{2,1,0:T(8,128)S(1)}, u32[]{:S(2)}, u32[]{:S(2)}) %collective-permute-start) | collective-permute-done | bytes 524320 | tf_op jit(solution)/shard_map/ppermute | solution.py:46
  43.6 2.9 %collective-permute-done.3.last_y = f32[8,64,256]{2,1,0:T(8,128)} collective-permute-done((f32[8,64,256]{2,1,0:T(8,128)S(1)}, f32[8,64,256]{2,1,0:T(8,128)}, u32[]{:S(2)}, u32[]{:S(2)}) %collective-permute-start.3) | collective-permute-done | bytes 524320 | tf_op jit(solution)/shard_map/ppermute | solution.py:47
  46.5 1.6 copy-done.1
  48.1 9.6 %shard_map.68 = (f32[4,64,256]{2,1,0:T(8,128)S(1)}, f32[4,64,256]{2,1,0:T(8,128)S(1)}) custom-call(s32[3]{0:T(128)S(1)} %pad_add_fusion.place, f32[8,64,256]{2,1,0:T(8,128)S(1)} %all_to_all.15.own, f32[8,64,256]{2,1,0:T(8,128)S(1)} %collective-permute-done.next_y, f32[4,64,256]{2,1,0:T(8,128)} %collective-permute-done.1.next_z, ...), custom_call_target="tpu_custom_call" | custom-call | flops 1610612736 | bytes 7340032 | tf_op jit(solution)/shard_map/pallas_call | solution.py:92
  57.8 1.5 collective-permute-done.4
  60.3 1.1 collective-permute-start.6
  61.4 2.1 %collective-permute-start.5 = (f32[64,256]{1,0:T(8,128)S(1)}, f32[64,256]{1,0:T(8,128)S(1)}, u32[]{:S(2)}, u32[]{:S(2)}) collective-permute-start(f32[64,256]{1,0:T(8,128)S(1)} %get-tuple-element.23), channel_id=1, source_target_pairs={{0,2},{1,3},{2,4},{3,5},{4,6},{5,7},{6,0},{7,1},{8,10},{9,11},{10,... | collective-permute-start | bytes 196616 | tf_op jit(solution)/shard_map/ppermute | solution.py:107
  63.5 2.8 %collective-permute-done.7 = f32[64,256]{1,0:T(8,128)S(1)} collective-permute-done((f32[64,256]{1,0:T(8,128)S(1)}, f32[64,256]{1,0:T(8,128)S(1)}, u32[]{:S(2)}, u32[]{:S(2)}) %collective-permute-start.7) | collective-permute-done | bytes 65568 | tf_op jit(solution)/shard_map/ppermute | solution.py:107
  67.1 21.2 %all_to_all.16.own = f32[8,64,256]{2,1,0:T(8,128)S(1)} all-to-all(f32[8,64,256]{2,1,0:T(8,128)S(1)} %broadcast_in_dim.38), channel_id=1, replica_groups={{0,16,32,48,136,152,168,184},{64,80,96,112,200,216,232,248},{8,24,40,56..., dimensions={0} | all-to-all | bytes 1048576 | tf_op jit(solution)/shard_map/all_to_all | solution.py:45
  88.3 2.0 %collective-permute-start.11 = (f32[8,64,256]{2,1,0:T(8,128)S(1)}, f32[8,64,256]{2,1,0:T(8,128)S(1)}, u32[]{:S(2)}, u32[]{:S(2)}) collective-permute-start(f32[8,64,256]{2,1,0:T(8,128)S(1)} %all_to_all.16.own), channel_id=1, source_target_pairs={{0,64},{8,72},{16,80},{24,88},{32,96},{40,104},{48,112},{56,120},{... | collective-permute-start | bytes 1572872 | tf_op jit(solution)/shard_map/ppermute | solution.py:47
  90.4 1.3 collective-permute-start.9
  92.5 4.3 %collective-permute-done.9.next_z = f32[4,64,256]{2,1,0:T(8,128)S(1)} collective-permute-done((f32[4,64,256]{2,1,0:T(8,128)S(1)}, f32[4,64,256]{2,1,0:T(8,128)S(1)}, u32[]{:S(2)}, u32[]{:S(2)}) %collective-permute-start.9) | collective-permute-done | bytes 262176 | tf_op jit(solution)/shard_map/ppermute | solution.py:48
  96.8 2.4 %collective-permute-done.10.last_z = f32[4,64,256]{2,1,0:T(8,128)S(1)} collective-permute-done((f32[4,64,256]{2,1,0:T(8,128)S(1)}, f32[4,64,256]{2,1,0:T(8,128)S(1)}, u32[]{:S(2)}, u32[]{:S(2)}) %collective-permute-start.10) | collective-permute-done | bytes 262176 | tf_op jit(solution)/shard_map/ppermute | solution.py:49
  100.2 1.2 collective-permute-done.11.last_y
  101.4 9.0 %shard_map.69 = (f32[4,64,256]{2,1,0:T(8,128)S(1)}, f32[4,64,256]{2,1,0:T(8,128)S(1)}) custom-call(s32[3]{0:T(128)S(1)} %pad_add_fusion.place, f32[8,64,256]{2,1,0:T(8,128)S(1)} %all_to_all.16.own, f32[8,64,256]{2,1,0:T(8,128)S(1)} %collective-permute-done.8.next_y, f32[4,64,256]{2,1,0:T(8,128)S(1)} %collective-permute-done.9.next_z, ...), custom_call_target="tpu_custom_call" | custom-call | flops 1610612736 | bytes 7340032 | tf_op jit(solution)/shard_map/pallas_call | solution.py:92
  110.5 1.5 collective-permute-done.12
  112.1 1.4 collective-permute-start.15
  113.6 2.8 %collective-permute-start.14 = (f32[64,256]{1,0:T(8,128)S(1)}, f32[64,256]{1,0:T(8,128)S(1)}, u32[]{:S(2)}, u32[]{:S(2)}) collective-permute-start(f32[64,256]{1,0:T(8,128)S(1)} %get-tuple-element.22), channel_id=1, source_target_pairs={{0,4},{1,5},{2,6},{3,7},{4,0},{5,1},{6,2},{7,3},{8,12},{9,13},{10,... | collective-permute-start | bytes 196616 | tf_op jit(solution)/shard_map/ppermute | solution.py:107
  116.3 1.3 collective-permute-done.15
  117.7 2.2 %collective-permute-done.14 = f32[64,256]{1,0:T(8,128)S(1)} collective-permute-done((f32[64,256]{1,0:T(8,128)S(1)}, f32[64,256]{1,0:T(8,128)S(1)}, u32[]{:S(2)}, u32[]{:S(2)}) %collective-permute-start.14) | collective-permute-done | bytes 65568 | tf_op jit(solution)/shard_map/ppermute | solution.py:107
  122.2 1.9 %select_select_fusion = f32[8,128]{1,0:T(8,128)S(1)} fusion(f32[128]{0:T(128)S(1)} %compare_select_fusion, f32[]{:T(128)} %get-tuple-element.10, f32[]{:T(128)} %get-tuple-element.13, f32[]{:T(128)} %get-tuple-element.12, pred[128]{0:T(512)(128)(4,1)S(1)} %get-tuple-element.35, pred[128]{0:T(512)(128)(4,1)S(1)} %get-tuple-element.36, ...), kind=kLoop, calls=%fused_computation.33 | loop fusion | flops 3072 | bytes 5004 | tf_op jit(solution)/shard_map/jit(_where)/select_n | solution.py:115
  124.2 1.2 collective-permute-done.16
  125.3 1.9 %fusion.14 = f32[8,128]{1,0:T(8,128)S(1)} fusion(f32[8,128]{1,0:T(8,128)S(1)} %collective-permute-done.16, f32[128]{0:T(128)S(1)} %compare_select_fusion, f32[]{:T(128)} %get-tuple-element.10, pred[128]{0:T(512)(128)(4,1)S(1)} %get-tuple-element.35, f32[]{:T(128)} %get-tuple-element.13, pred[128]{0:T(512)(128)(4,1)S(1)} %get-tuple-element.36, ...), kind=kLoop, calls=%fused_computation.39 | loop fusion | flops 4096 | bytes 9100 | tf_op jit(solution)/shard_map/add | solution.py:116
  127.4 3.1 %collective-permute-start.17 = (f32[8,128]{1,0:T(8,128)S(1)}, f32[8,128]{1,0:T(8,128)S(1)}, u32[]{:S(2)}, u32[]{:S(2)}) collective-permute-start(f32[8,128]{1,0:T(8,128)S(1)} %fusion.14), channel_id=1, source_target_pairs={{0,2},{1,3},{2,4},{3,5},{4,6},{5,7},{6,0},{7,1},{8,10},{9,11},{10,... | collective-permute-start | bytes 12296 | tf_op jit(solution)/shard_map/ppermute | solution.py:117
  130.9 1.3 collective-permute-done.19
  132.1 3.5 %collective-permute-done.18 = f32[8,128]{1,0:T(8,128)S(1)} collective-permute-done((f32[8,128]{1,0:T(8,128)S(1)}, f32[8,128]{1,0:T(8,128)S(1)}, u32[]{:S(2)}, u32[]{:S(2)}) %collective-permute-start.18) | collective-permute-done | bytes 4128 | tf_op jit(solution)/shard_map/ppermute | solution.py:117
  135.7 1.9 %add_add_fusion = f32[8,128]{1,0:T(8,128)S(1)} fusion(f32[8,128]{1,0:T(8,128)S(1)} %collective-permute-done.19, f32[8,128]{1,0:T(8,128)S(1)} %collective-permute-done.17, f32[8,128]{1,0:T(8,128)S(1)} %collective-permute-done.18, f32[8,128]{1,0:T(8,128)S(1)} %collective-permute-done.16, f32[128]{0:T(128)S(1)} %compare_select_fusion, f32[]{:T(128)} %get-tuple-element.10, ...), kind=kLoop, calls=%fused_computation.32 | loop fusion | flops 7168 | bytes 21388 | tf_op jit(solution)/shard_map/add | solution.py:117
  137.6 15.0 %all_to_all.17 = f32[32,8,128]{2,1,0:T(8,128)S(1)} all-to-all(f32[32,8,128]{2,1,0:T(8,128)S(1)} %broadcast_in_dim.44), channel_id=1, replica_groups=mesh['row'=32,'col'=8] {'row'}, dimensions={0} | all-to-all | bytes 262144 | tf_op jit(solution)/shard_map/all_to_all | solution.py:119
  (46 shorter events, 11.8 us)
Async XLA Ops:
  0.6 66.2 %copy-start = (f32[256,256]{1,0:T(8,128)S(1)}, f32[256,256]{1,0:T(8,128)}, u32[]{:S(2)}) copy-start(f32[256,256]{1,0:T(8,128)} %param.6) | copy-start | bytes 786436
  30.8 8.5 %collective-permute-start.1 = (f32[4,64,256]{2,1,0:T(8,128)}, f32[4,64,256]{2,1,0:T(8,128)}, u32[]{:S(2)}, u32[]{:S(2)}) collective-permute-start(f32[4,64,256]{2,1,0:T(8,128)} %get-tuple-element.19), channel_id=1, source_target_pairs={{0,56},{8,0},{16,8},{24,16},{32,24},{40,32},{48,40},{56,48},{64,12... | collective-permute-start | bytes 786440 | tf_op jit(solution)/shard_map/ppermute | solution.py:48
  31.8 7.9 %collective-permute-start.2 = (f32[4,64,256]{2,1,0:T(8,128)}, f32[4,64,256]{2,1,0:T(8,128)}, u32[]{:S(2)}, u32[]{:S(2)}) collective-permute-start(f32[4,64,256]{2,1,0:T(8,128)} %get-tuple-element.18), channel_id=1, source_target_pairs={{0,8},{8,16},{16,24},{24,32},{32,40},{40,48},{48,56},{56,0},{64,72... | collective-permute-start | bytes 786440 | tf_op jit(solution)/shard_map/ppermute | solution.py:49
  32.9 10.7 %collective-permute-start = (f32[8,64,256]{2,1,0:T(8,128)S(1)}, f32[8,64,256]{2,1,0:T(8,128)S(1)}, u32[]{:S(2)}, u32[]{:S(2)}) collective-permute-start(f32[8,64,256]{2,1,0:T(8,128)S(1)} %all_to_all.15.own), channel_id=1, source_target_pairs={{0,192},{8,200},{16,208},{24,216},{32,224},{40,232},{48,240},{56,2... | collective-permute-start | bytes 1572872 | tf_op jit(solution)/shard_map/ppermute | solution.py:46
  33.4 13.1 %collective-permute-start.3 = (f32[8,64,256]{2,1,0:T(8,128)S(1)}, f32[8,64,256]{2,1,0:T(8,128)}, u32[]{:S(2)}, u32[]{:S(2)}) collective-permute-start(f32[8,64,256]{2,1,0:T(8,128)S(1)} %all_to_all.15.own), channel_id=1, source_target_pairs={{0,64},{8,72},{16,80},{24,88},{32,96},{40,104},{48,112},{56,120},{... | collective-permute-start | bytes 1572872 | tf_op jit(solution)/shard_map/ppermute | solution.py:47
  39.3 27.5 %copy-start.2 = (f32[64,256]{1,0:T(8,128)S(1)}, f32[64,256]{1,0:T(8,128)}, u32[]{:S(2)}) copy-start(f32[64,256]{1,0:T(8,128)} %param.9) | copy-start | bytes 196612
  39.3 27.5 %copy-start.3 = (s32[64]{0:T(128)S(1)}, s32[64]{0:T(128)}, u32[]{:S(2)}) copy-start(s32[64]{0:T(128)} %param.7) | copy-start | bytes 772
  39.3 27.5 %copy-start.4 = (f32[64]{0:T(128)S(1)}, f32[64]{0:T(128)}, u32[]{:S(2)}) copy-start(f32[64]{0:T(128)} %param.8) | copy-start | bytes 772
  46.5 1.6 copy-start.1
  57.7 1.6 %collective-permute-start.4 = (f32[4,64,256]{2,1,0:T(8,128)S(1)}, f32[4,64,256]{2,1,0:T(8,128)S(1)}, u32[]{:S(2)}, u32[]{:S(2)}) collective-permute-start(f32[4,64,256]{2,1,0:T(8,128)S(1)} %get-tuple-element.7), channel_id=1, source_target_pairs={{0,1},{1,0},{2,3},{3,2},{4,5},{5,4},{6,7},{7,6},{8,9},{9,8},{10,11... | collective-permute-start | bytes 786440 | tf_op jit(solution)/shard_map/ppermute | solution.py:106
  59.4 7.0 %collective-permute-start.7 = (f32[64,256]{1,0:T(8,128)S(1)}, f32[64,256]{1,0:T(8,128)S(1)}, u32[]{:S(2)}, u32[]{:S(2)}) collective-permute-start(f32[64,256]{1,0:T(8,128)S(1)} %get-tuple-element.24), channel_id=1, source_target_pairs={{0,6},{1,7},{2,0},{3,1},{4,2},{5,3},{6,4},{7,5},{8,14},{9,15},{10,... | collective-permute-start | bytes 196616 | tf_op jit(solution)/shard_map/ppermute | solution.py:107
  60.3 6.1 %collective-permute-start.6 = (f32[64,256]{1,0:T(8,128)S(1)}, f32[64,256]{1,0:T(8,128)S(1)}, u32[]{:S(2)}, u32[]{:S(2)}) collective-permute-start(f32[64,256]{1,0:T(8,128)S(1)} %get-tuple-element.25), channel_id=1, source_target_pairs={{0,4},{1,5},{2,6},{3,7},{4,0},{5,1},{6,2},{7,3},{8,12},{9,13},{10,... | collective-permute-start | bytes 196616 | tf_op jit(solution)/shard_map/ppermute | solution.py:107
  61.4 5.4 %collective-permute-start.5 = (f32[64,256]{1,0:T(8,128)S(1)}, f32[64,256]{1,0:T(8,128)S(1)}, u32[]{:S(2)}, u32[]{:S(2)}) collective-permute-start(f32[64,256]{1,0:T(8,128)S(1)} %get-tuple-element.23), channel_id=1, source_target_pairs={{0,2},{1,3},{2,4},{3,5},{4,6},{5,7},{6,0},{7,1},{8,10},{9,11},{10,... | collective-permute-start | bytes 196616 | tf_op jit(solution)/shard_map/ppermute | solution.py:107
  88.3 11.9 %collective-permute-start.8 = (f32[8,64,256]{2,1,0:T(8,128)S(1)}, f32[8,64,256]{2,1,0:T(8,128)S(1)}, u32[]{:S(2)}, u32[]{:S(2)}) collective-permute-start(f32[8,64,256]{2,1,0:T(8,128)S(1)} %all_to_all.16.own), channel_id=1, source_target_pairs={{0,192},{8,200},{16,208},{24,216},{32,224},{40,232},{48,240},{56,2... | collective-permute-start | bytes 1572872 | tf_op jit(solution)/shard_map/ppermute | solution.py:46
  88.3 13.1 %collective-permute-start.11 = (f32[8,64,256]{2,1,0:T(8,128)S(1)}, f32[8,64,256]{2,1,0:T(8,128)S(1)}, u32[]{:S(2)}, u32[]{:S(2)}) collective-permute-start(f32[8,64,256]{2,1,0:T(8,128)S(1)} %all_to_all.16.own), channel_id=1, source_target_pairs={{0,64},{8,72},{16,80},{24,88},{32,96},{40,104},{48,112},{56,120},{... | collective-permute-start | bytes 1572872 | tf_op jit(solution)/shard_map/ppermute | solution.py:47
  90.4 6.5 %collective-permute-start.9 = (f32[4,64,256]{2,1,0:T(8,128)S(1)}, f32[4,64,256]{2,1,0:T(8,128)S(1)}, u32[]{:S(2)}, u32[]{:S(2)}) collective-permute-start(f32[4,64,256]{2,1,0:T(8,128)S(1)} %get-tuple-element.17), channel_id=1, source_target_pairs={{0,56},{8,0},{16,8},{24,16},{32,24},{40,32},{48,40},{56,48},{64,12... | collective-permute-start | bytes 786440 | tf_op jit(solution)/shard_map/ppermute | solution.py:48
  91.7 7.6 %collective-permute-start.10 = (f32[4,64,256]{2,1,0:T(8,128)S(1)}, f32[4,64,256]{2,1,0:T(8,128)S(1)}, u32[]{:S(2)}, u32[]{:S(2)}) collective-permute-start(f32[4,64,256]{2,1,0:T(8,128)S(1)} %get-tuple-element.16), channel_id=1, source_target_pairs={{0,8},{8,16},{16,24},{24,32},{32,40},{40,48},{48,56},{56,0},{64,72... | collective-permute-start | bytes 786440 | tf_op jit(solution)/shard_map/ppermute | solution.py:49
  110.4 1.6 %collective-permute-start.12 = (f32[4,64,256]{2,1,0:T(8,128)S(1)}, f32[4,64,256]{2,1,0:T(8,128)S(1)}, u32[]{:S(2)}, u32[]{:S(2)}) collective-permute-start(f32[4,64,256]{2,1,0:T(8,128)S(1)} %get-tuple-element.9), channel_id=1, source_target_pairs={{0,1},{1,0},{2,3},{3,2},{4,5},{5,4},{6,7},{7,6},{8,9},{9,8},{10,11... | collective-permute-start | bytes 786440 | tf_op jit(solution)/shard_map/ppermute | solution.py:106
  112.1 5.6 %collective-permute-start.15 = (f32[64,256]{1,0:T(8,128)S(1)}, f32[64,256]{1,0:T(8,128)S(1)}, u32[]{:S(2)}, u32[]{:S(2)}) collective-permute-start(f32[64,256]{1,0:T(8,128)S(1)} %get-tuple-element.21), channel_id=1, source_target_pairs={{0,6},{1,7},{2,0},{3,1},{4,2},{5,3},{6,4},{7,5},{8,14},{9,15},{10,... | collective-permute-start | bytes 196616 | tf_op jit(solution)/shard_map/ppermute | solution.py:107
  113.6 6.3 %collective-permute-start.14 = (f32[64,256]{1,0:T(8,128)S(1)}, f32[64,256]{1,0:T(8,128)S(1)}, u32[]{:S(2)}, u32[]{:S(2)}) collective-permute-start(f32[64,256]{1,0:T(8,128)S(1)} %get-tuple-element.22), channel_id=1, source_target_pairs={{0,4},{1,5},{2,6},{3,7},{4,0},{5,1},{6,2},{7,3},{8,12},{9,13},{10,... | collective-permute-start | bytes 196616 | tf_op jit(solution)/shard_map/ppermute | solution.py:107
  116.3 4.3 %collective-permute-start.13 = (f32[64,256]{1,0:T(8,128)S(1)}, f32[64,256]{1,0:T(8,128)S(1)}, u32[]{:S(2)}, u32[]{:S(2)}) collective-permute-start(f32[64,256]{1,0:T(8,128)S(1)} %get-tuple-element.20), channel_id=1, source_target_pairs={{0,2},{1,3},{2,4},{3,5},{4,6},{5,7},{6,0},{7,1},{8,10},{9,11},{10,... | collective-permute-start | bytes 196616 | tf_op jit(solution)/shard_map/ppermute | solution.py:107
  124.1 1.3 collective-permute-start.16
  127.2 4.9 %collective-permute-start.19 = (f32[8,128]{1,0:T(8,128)S(1)}, f32[8,128]{1,0:T(8,128)S(1)}, u32[]{:S(2)}, u32[]{:S(2)}) collective-permute-start(f32[8,128]{1,0:T(8,128)S(1)} %fusion.14), channel_id=1, source_target_pairs={{0,6},{1,7},{2,0},{3,1},{4,2},{5,3},{6,4},{7,5},{8,14},{9,15},{10,... | collective-permute-start | bytes 12296 | tf_op jit(solution)/shard_map/ppermute | solution.py:117
  127.4 4.7 %collective-permute-start.17 = (f32[8,128]{1,0:T(8,128)S(1)}, f32[8,128]{1,0:T(8,128)S(1)}, u32[]{:S(2)}, u32[]{:S(2)}) collective-permute-start(f32[8,128]{1,0:T(8,128)S(1)} %fusion.14), channel_id=1, source_target_pairs={{0,2},{1,3},{2,4},{3,5},{4,6},{5,7},{6,0},{7,1},{8,10},{9,11},{10,... | collective-permute-start | bytes 12296 | tf_op jit(solution)/shard_map/ppermute | solution.py:117
  130.6 5.1 %collective-permute-start.18 = (f32[8,128]{1,0:T(8,128)S(1)}, f32[8,128]{1,0:T(8,128)S(1)}, u32[]{:S(2)}, u32[]{:S(2)}) collective-permute-start(f32[8,128]{1,0:T(8,128)S(1)} %fusion.14), channel_id=1, source_target_pairs={{0,4},{1,5},{2,6},{3,7},{4,0},{5,1},{6,2},{7,3},{8,12},{9,13},{10,... | collective-permute-start | bytes 12296 | tf_op jit(solution)/shard_map/ppermute | solution.py:117

commit v2 on v1

v2 whole, which is shorter than its diff:
```python
import functools

import jax
import jax.numpy as jnp
from jax import lax
from jax.experimental import pallas as pl
from jax.experimental.pallas import tpu as pltpu
from jax.sharding import PartitionSpec as P

NY, NZ, NX = 4, 8, 4
BLOCK = 64
EPOCHS = 256
F32 = jnp.float32
BF16 = jnp.bfloat16


def class_member(k, j):
    kh, kl, jh, jl = k // 2, k % 2, j // 4, j % 4
    return (kl + 2 * jh) * NZ + 2 * jl + (kh + jh) % 2


CLASSES = [[class_member(k, j) for j in range(8)] for k in range(4)]


def shift_y(d):
    return [(y * NZ + z, ((y + d) % NY) * NZ + z) for y in range(NY) for z in range(NZ)]


def shift_z(d):
    return [(y * NZ + z, y * NZ + (z + d) % NZ) for y in range(NY) for z in range(NZ)]


def shift_x(d):
    return [(x * 2 + c, ((x + d) % NX) * 2 + c) for x in range(NX) for c in range(2)]


SIBLING = [(c, c ^ 1) for c in range(8)]


def split(value):
    high = lax.reduce_precision(value, 8, 7)
    return high.astype(BF16), (value - high).astype(BF16)


def gather_class(copies):
    return lax.all_to_all(copies, "row", 0, 0, axis_index_groups=CLASSES)


def gather_rest(own):
    next_y = lax.ppermute(own, "row", shift_y(-1))
    last_y = lax.ppermute(own, "row", shift_y(1))
    next_z = lax.ppermute(own[:4], "row", shift_z(-1))
    last_z = lax.ppermute(own[4:], "row", shift_z(1))
    return own, next_y, next_z, last_z, last_y


def put_parts(colour, parts, high, low):
    for ref, slot, first in zip(parts, (0, 1, 2, 2, 3), (0, 0, 0, 4, 0)):
        k = lax.rem(colour + slot, 4)
        kh, kl = k // 2, lax.rem(k, 2)
        for j in range(ref.shape[0]):
            jh, jl = (j + first) // 4, (j + first) % 4
            row = (kl + 2 * jh) * NZ + 2 * jl + lax.rem(kh + jh, 2)
            at = pl.ds(pl.multiple_of(row * BLOCK, BLOCK), BLOCK)
            value = ref[j]
            top = value.astype(BF16)
            high[at, :] = top
            low[at, :] = (value - top.astype(F32)).astype(BF16)


def product_kernel(with_sums, place, *refs):
    parts, (k_high, k_low), refs = refs[:5], refs[5:7], refs[7:]
    if with_sums:
        images, sums, refs = refs[:4], refs[4], refs[5:]
    keep, send, high, low = refs
    put_parts(place[0], parts, high, low)
    x, even_core = place[1], place[2] == 0
    value = jnp.dot(k_high[...], high[...], preferred_element_type=F32)
    value += jnp.dot(k_low[...], high[...], preferred_element_type=F32)
    value += jnp.dot(k_high[...], low[...], preferred_element_type=F32)
    for p in range(NX):
        even = value[2 * p * BLOCK : (2 * p + 1) * BLOCK]
        odd = value[(2 * p + 1) * BLOCK : (2 * p + 2) * BLOCK]
        dx = lax.rem(p - x + NX, NX)
        keep[dx, :BLOCK] = jnp.where(even_core, even, odd)
        send[dx, :BLOCK] = jnp.where(even_core, odd, even)
    if with_sums:
        form = jnp.zeros((BLOCK, EPOCHS), F32)
        for d in range(NX):
            form += keep[d, :BLOCK] * images[d][0] + send[d, :BLOCK] * images[d][1]
        lane = lax.broadcasted_iota(jnp.int32, (8, EPOCHS), 1)
        row = lax.broadcasted_iota(jnp.int32, (8, EPOCHS), 0)
        tile = sums[...] + jnp.where((lane == 3) & (row == 0), jnp.sum(form), 0.0)
        for d in range(NX):
            keep[d, BLOCK:] = tile
            send[d, BLOCK:] = tile


VMEM_SPEC = pl.BlockSpec(memory_space=pltpu.VMEM)


def product(place, parts, k_high, k_low, extra=()):
    half = jax.ShapeDtypeStruct((NX, BLOCK + (8 if extra else 0), EPOCHS), F32)
    return pl.pallas_call(
        functools.partial(product_kernel, bool(extra)),
        out_shape=(half, half),
        in_specs=[pl.BlockSpec(memory_space=pltpu.SMEM)] + [VMEM_SPEC] * (7 + len(extra)),
        out_specs=(VMEM_SPEC, VMEM_SPEC),
        scratch_shapes=[pltpu.VMEM((2048, EPOCHS), BF16), pltpu.VMEM((2048, EPOCHS), BF16)],
        compiler_params=pltpu.CompilerParams(vmem_limit_bytes=24 * 1024 * 1024),
        cost_estimate=pl.CostEstimate(
            flops=2 * 3 * 512 * 2048 * EPOCHS, bytes_accessed=7 * 1024 * 1024, transcendentals=0
        ),
    )(place, *parts, k_high, k_low, *extra)


def dot(a, b):
    return jnp.dot(a, b, precision=lax.Precision.HIGHEST, preferred_element_type=F32)


def small_call(kernel, outs, *args):
    return pl.pallas_call(
        kernel,
        out_shape=[jax.ShapeDtypeStruct(o, F32) for o in outs],
        in_specs=[VMEM_SPEC] * len(args),
        out_specs=[VMEM_SPEC] * len(outs),
        compiler_params=pltpu.CompilerParams(vmem_limit_bytes=8 * 1024 * 1024),
        cost_estimate=pl.CostEstimate(
            flops=2 * 6 * BLOCK * EPOCHS * EPOCHS, bytes_accessed=1024 * 1024, transcendentals=0
        ),
    )(*args)


def tile_of(values, shape):
    lane = lax.broadcasted_iota(jnp.int32, shape, 1)
    row = lax.broadcasted_iota(jnp.int32, shape, 0)
    tile = jnp.zeros(shape, F32)
    for i, v in enumerate(values):
        tile = jnp.where((lane == i) & (row == 0), v, tile)
    return tile


def first_kernel(t0, t1, t2, t3, kernel, mask, noise, r0, w1, copies, image, sums):
    smoothed = dot(t0[...] + t1[...] + t2[...] + t3[...], kernel[...])
    start = r0[...]
    value = mask[...] * smoothed + noise[...] * start
    w1[...] = value
    masked = mask[...] * value
    for j in range(8):
        copies[j] = masked
    image[...] = lax.dot_general(
        masked, kernel[...], (((1,), (1,)), ((), ())),
        precision=lax.Precision.HIGHEST, preferred_element_type=F32,
    )
    sums[...] = tile_of(
        [
            jnp.sum(start * start),
            jnp.sum(start * value),
            jnp.sum(value * value),
            jnp.sum(noise[...] * value * value),
        ],
        (8, EPOCHS),
    )


def second_kernel(t0, t1, t2, t3, kernel, mask, noise, w1, w2, copies):
    total = t0[...] + t1[...] + t2[...] + t3[...]
    for j in range(32):
        copies[j] = total[BLOCK:, :128]
    w2[...] = mask[...] * dot(total[:BLOCK], kernel[...]) + noise[...] * w1[...]


def last_kernel(tiles, r0, w1, w2, out, residual):
    tile = jnp.sum(tiles[...], axis=0)
    lane = lax.broadcasted_iota(jnp.int32, (8, 128), 1)

    def pick(i):
        return jnp.sum(jnp.where(lane == i, tile, 0.0), keepdims=True)

    rr, rw, ww, wv = pick(0), pick(1), pick(2), pick(3)
    a0 = rr / rw
    rr1 = rr - 2.0 * a0 * rw + a0 * a0 * ww
    b0 = rr1 / rr
    c0 = 1.0 + b0
    a1 = rr1 / (c0 * c0 * rw - 2.0 * a0 * c0 * ww + a0 * a0 * wv)
    r1 = r0[...] - a0 * w1[...]
    out[...] = a0 * r0[...] + a1 * (r1 + b0 * r0[...])
    residual[...] = r1 - a1 * (c0 * w1[...] - a0 * w2[...])


def scatter_col(keep, send):
    other = lax.ppermute(send, "col", SIBLING)
    total = [keep[d] + other[d] for d in range(NX)]
    return total[0], *[lax.ppermute(total[d], "col", shift_x(d)) for d in range(1, NX)]


def gather_col(image):
    pair = jnp.stack([image, lax.ppermute(image, "col", SIBLING)])
    return pair, *[lax.ppermute(pair, "col", shift_x(-d)) for d in range(1, NX)]


def per_device(kernel_configs, epoch_kernel, lengths, noise, curves):
    epoch_index = lax.broadcasted_iota(jnp.int32, (BLOCK, EPOCHS), 1)
    mask = (epoch_index < lengths[:, None]).astype(F32)
    noise = jnp.broadcast_to(noise[:, None], (BLOCK, EPOCHS))
    row, col = lax.axis_index("row"), lax.axis_index("col")
    colour = lax.rem(row // NZ + 2 * lax.rem(row, NZ), 4)
    place = jnp.stack([colour, col // 2, lax.rem(col, 2)]).astype(jnp.int32)
    k_high, k_low = split(kernel_configs.reshape(-1, kernel_configs.shape[2]))
    block = (BLOCK, EPOCHS)

    r0 = curves * mask
    parts = gather_rest(gather_class(jnp.broadcast_to(r0[None], (8, BLOCK, EPOCHS))))
    pieces = scatter_col(*product(place, parts, k_high, k_low))
    w1, copies, image, sums = small_call(
        first_kernel, [block, (8, *block), block, (8, EPOCHS)], *pieces, epoch_kernel, mask, noise, r0
    )
    own, images = lax.optimization_barrier((gather_class(copies), gather_col(image)))
    parts = gather_rest(own)
    pieces = scatter_col(*product(place, parts, k_high, k_low, (*images, sums)))
    w2, copies = small_call(
        second_kernel, [block, (32, 8, 128)], *pieces, epoch_kernel, mask, noise, w1
    )
    tiles = lax.all_to_all(copies, "row", 0, 0)
    return tuple(small_call(last_kernel, [block, block], tiles, r0, w1, w2))


def solution(mesh):
    in_specs = (
        P(None, "row", "col"),
        P(),
        P(("col", "row")),
        P(("col", "row")),
        P(("col", "row"), None),
    )
    out_specs = (P(("col", "row"), None), P(("col", "row"), None))
    return jax.shard_map(
        per_device, mesh=mesh, in_specs=in_specs, out_specs=out_specs, check_vma=False
    )
```

time: 160 us -> 136 us (0.85); the launches traced: 160 us -> 134 us
  blocking collectives: 64.5 us -> 47.1 us
  starting transfers between devices: 20.4 us -> 31.6 us
  Pallas kernels: 18.6 us -> 8.04 us
  other arithmetic: 12.6 us -> 5.62 us
  between operations: 6.64 us -> 0.76 us
  local copies, waits for them, and re-layouts: 3.23 us -> 6.55 us
  waiting for transfers between devices: 32.6 us -> 34.5 us
    all_to_all x3 -> x2, blocking collectives: 64.5 us -> 47.1 us  [the longest x1 28.3 us: gather_class(): return lax.all_to_all(copies, 'row', 0, 0, axis_index_groups=CLASSES)]
    pallas_call x2 -> x5, Pallas kernels: 18.6 us -> 8.04 us  [the longest x2 6.17 us: product(): pl.pallas_call(functools.partial(product_kernel, bool(extra)), out_shape=...]
    all_to_all x0 -> x1, starting transfers between devices: none -> 6.27 us  [gather_class(): return lax.all_to_all(copies, 'row', 0, 0, axis_index_groups=CLASSES)]
    ppermute x20, starting transfers between devices: 20.4 us -> 25.3 us  [the longest x6 7.42 us: scatter_col(): lax.ppermute(total[d], 'col', shift_x(d))]
    unnamed x10 -> x16, local copies, waits for them, and re-layouts: 1.61 us -> 5.55 us
    add x4 -> x2, other arithmetic: 3.88 us -> 0.07 us  [scatter_col(): total = [keep[d] + other[d] for d in range(NX)]]
    select_n x2 -> x0, other arithmetic: 2.55 us -> none  [reduce_all(): tile = jnp.where(lane == i, v, tile)]
    all_to_all x0 -> x1, waiting for transfers between devices: none -> 1.84 us  [gather_class(): return lax.all_to_all(copies, 'row', 0, 0, axis_index_groups=CLASSES)]
  transfers between devices with their start and end apart: 20 -> 21, of which waited for: 17 -> 15; matrix products, arithmetic and copies ran while one was open for 3% -> 3% of each run, Pallas kernels for 0% -> 0%
where the time goes in v2:
time: 136 us; the launch traced here: 134 us
  blocking collectives  47.1 us (35%)
  waiting for transfers between devices  34.5 us (25%)
  starting transfers between devices  31.6 us (23%)
  Pallas kernels  8.04 us (6%)
  local copies, waits for them, and re-layouts  6.55 us (5%)
  other arithmetic  5.62 us (4%)
    all_to_all x1, blocking collectives, gather_class(): return lax.all_to_all(copies, 'row', 0, 0, axis_index_groups=CLASSES)  28.3 us
    all_to_all x1, blocking collectives, per_device(): tiles = lax.all_to_all(copies, 'row', 0, 0)  18.7 us
    ppermute x3, waiting for transfers between devices, gather_col(): lax.ppermute(pair, 'col', shift_x(-d))  8.5 us
    ppermute x6, waiting for transfers between devices, scatter_col(): lax.ppermute(total[d], 'col', shift_x(d))  7.64 us
    ppermute x6, starting transfers between devices, scatter_col(): lax.ppermute(total[d], 'col', shift_x(d))  7.42 us
    ppermute x2, waiting for transfers between devices, gather_rest(): last_y = lax.ppermute(own, 'row', shift_y(1))  6.35 us
    ppermute x2, starting transfers between devices, gather_rest(): next_y = lax.ppermute(own, 'row', shift_y(-1))  6.28 us
    all_to_all x1, starting transfers between devices, gather_class(): return lax.all_to_all(copies, 'row', 0, 0, axis_index_groups=CLASSES)  6.27 us
  transfers between devices with their start and end apart: 21, of which 15 were waited for; matrix products, arithmetic and copies ran while one was open for 3% of the time, Pallas kernels for 0%

profile of v2, /device:TPU:6, one launch (start us, length us, event | category | flops | bytes accessed | tf_op | source)
XLA Modules:
  0.0 134.1 jit_solution(4392635078679264529)
XLA Ops:
  0.6 0.9 fusion.10.r0
  1.6 28.3 %all_to_all.15.refs_0_ = f32[8,64,256]{2,1,0:T(8,128)S(1)} all-to-all(f32[8,64,256]{2,1,0:T(8,128)S(1)} %broadcast_in_dim.4), channel_id=1, replica_groups={{0,16,32,48,136,152,168,184},{64,80,96,112,200,216,232,248},{8,24,40,56..., dimensions={0} | all-to-all | bytes 1048576 | tf_op jit(solution)/shard_map/all_to_all | solution.py:46
  30.8 1.5 %collective-permute-start.2 = (f32[4,64,256]{2,1,0:T(8,128)}, f32[4,64,256]{2,1,0:T(8,128)}, u32[]{:S(2)}, u32[]{:S(2)}) collective-permute-start(f32[4,64,256]{2,1,0:T(8,128)} %get-tuple-element.44), channel_id=1, source_target_pairs={{0,8},{8,16},{16,24},{24,32},{32,40},{40,48},{48,56},{56,0},{64,72... | collective-permute-start | bytes 786440 | tf_op jit(solution)/shard_map/ppermute | solution.py:53
  32.3 1.7 %collective-permute-start.1 = (f32[4,64,256]{2,1,0:T(8,128)}, f32[4,64,256]{2,1,0:T(8,128)}, u32[]{:S(2)}, u32[]{:S(2)}) collective-permute-start(f32[4,64,256]{2,1,0:T(8,128)} %get-tuple-element.45), channel_id=1, source_target_pairs={{0,56},{8,0},{16,8},{24,16},{32,24},{40,32},{48,40},{56,48},{64,12... | collective-permute-start | bytes 786440 | tf_op jit(solution)/shard_map/ppermute | solution.py:52
  34.7 2.6 %collective-permute-start = (f32[8,64,256]{2,1,0:T(8,128)S(1)}, f32[8,64,256]{2,1,0:T(8,128)}, u32[]{:S(2)}, u32[]{:S(2)}) collective-permute-start(f32[8,64,256]{2,1,0:T(8,128)S(1)} %all_to_all.15.refs_0_), channel_id=1, source_target_pairs={{0,192},{8,200},{16,208},{24,216},{32,224},{40,232},{48,240},{56,2... | collective-permute-start | bytes 1572872 | tf_op jit(solution)/shard_map/ppermute | solution.py:50
  37.2 4.5 %fusion = (bf16[512,2048]{1,0:T(8,128)(2,1)S(1)}, bf16[512,2048]{1,0:T(8,128)(2,1)}) fusion(f32[8,64,2048]{2,1,0:T(8,128)} %param.5), kind=kLoop, calls=%fused_computation.2 | loop fusion | flops 4194304 | bytes 8388608 | tf_op jit(solution)/shard_map/convert_element_type | solution.py:42
  41.8 3.6 %collective-permute-done.3.refs_4_ = f32[8,64,256]{2,1,0:T(8,128)S(1)} collective-permute-done((f32[8,64,256]{2,1,0:T(8,128)S(1)}, f32[8,64,256]{2,1,0:T(8,128)S(1)}, u32[]{:S(2)}, u32[]{:S(2)}) %collective-permute-start.3) | collective-permute-done | bytes 524320 | tf_op jit(solution)/shard_map/ppermute | solution.py:51
  45.4 1.6 %copy-done = bf16[512,2048]{1,0:T(8,128)(2,1)S(1)} copy-done((bf16[512,2048]{1,0:T(8,128)(2,1)S(1)}, bf16[512,2048]{1,0:T(8,128)(2,1)}, u32[]{:S(2)}) %copy-start) | copy-done | bytes 2097176
  47.0 3.3 %shard_map.68 = (f32[4,64,256]{2,1,0:T(8,128)S(1)}, f32[4,64,256]{2,1,0:T(8,128)S(1)}) custom-call(s32[3]{0:T(128)S(1)} %pad_add_fusion.place, f32[8,64,256]{2,1,0:T(8,128)S(1)} %all_to_all.15.refs_0_, f32[8,64,256]{2,1,0:T(8,128)} %collective-permute-done.refs_1_, f32[4,64,256]{2,1,0:T(8,128)} %collective-permute-done.1.refs_2_, ...), custom_call_target="tpu_custom_call" | custom-call | flops 1610612736 | bytes 7340032 | tf_op jit(solution)/shard_map/pallas_call | solution.py:104
  50.4 1.5 %collective-permute-done.4 = f32[4,64,256]{2,1,0:T(8,128)S(1)} collective-permute-done((f32[4,64,256]{2,1,0:T(8,128)S(1)}, f32[4,64,256]{2,1,0:T(8,128)S(1)}, u32[]{:S(2)}, u32[]{:S(2)}) %collective-permute-start.4) | collective-permute-done | bytes 262176 | tf_op jit(solution)/shard_map/ppermute | solution.py:192
  52.0 0.9 collective-permute-start.7
  52.9 1.1 collective-permute-start.6
  54.0 2.1 %collective-permute-start.5 = (f32[64,256]{1,0:T(8,128)S(1)}, f32[64,256]{1,0:T(8,128)S(1)}, u32[]{:S(2)}, u32[]{:S(2)}) collective-permute-start(f32[64,256]{1,0:T(8,128)S(1)} %get-tuple-element.42), channel_id=1, source_target_pairs={{0,2},{1,3},{2,4},{3,5},{4,6},{5,7},{6,0},{7,1},{8,10},{9,11},{10,... | collective-permute-start | bytes 196616 | tf_op jit(solution)/shard_map/ppermute | solution.py:194
  56.2 2.8 %collective-permute-done.7.t3 = f32[64,256]{1,0:T(8,128)S(1)} collective-permute-done((f32[64,256]{1,0:T(8,128)S(1)}, f32[64,256]{1,0:T(8,128)S(1)}, u32[]{:S(2)}, u32[]{:S(2)}) %collective-permute-start.7) | collective-permute-done | bytes 65568 | tf_op jit(solution)/shard_map/ppermute | solution.py:194
  61.1 6.3 %all-to-all-start.1 = ((f32[8,64,256]{2,1,0:T(8,128)}), f32[8,64,256]{2,1,0:T(8,128)S(1)}, u32[]{:S(2)}, u32[]{:S(2)}) async-start(f32[8,64,256]{2,1,0:T(8,128)} %copy-done.3), calls=%async_computation.1 | async-start | bytes 1048576 | tf_op jit(solution)/shard_map/all_to_all | solution.py:46
  67.3 1.2 collective-permute-done.8
  68.6 2.8 %collective-permute-start.11 = (f32[2,64,256]{2,1,0:T(8,128)S(1)}, f32[2,64,256]{2,1,0:T(8,128)S(1)}, u32[]{:S(2)}, u32[]{:S(2)}) collective-permute-start(f32[2,64,256]{2,1,0:T(8,128)S(1)} %pad_maximum_fusion.refs_7_), channel_id=1, source_target_pairs={{0,2},{1,3},{2,4},{3,5},{4,6},{5,7},{6,0},{7,1},{8,10},{9,11},{10,... | collective-permute-start | bytes 393224 | tf_op jit(solution)/shard_map/ppermute | solution.py:199
  72.3 5.0 %collective-permute-done.11.refs_10_ = f32[2,64,256]{2,1,0:T(8,128)S(1)} collective-permute-done((f32[2,64,256]{2,1,0:T(8,128)S(1)}, f32[2,64,256]{2,1,0:T(8,128)S(1)}, u32[]{:S(2)}, u32[]{:S(2)}) %collective-permute-start.11) | collective-permute-done | bytes 131104 | tf_op jit(solution)/shard_map/ppermute | solution.py:199
  77.3 2.0 %collective-permute-done.10.refs_9_ = f32[2,64,256]{2,1,0:T(8,128)S(1)} collective-permute-done((f32[2,64,256]{2,1,0:T(8,128)S(1)}, f32[2,64,256]{2,1,0:T(8,128)S(1)}, u32[]{:S(2)}, u32[]{:S(2)}) %collective-permute-start.10) | collective-permute-done | bytes 131104 | tf_op jit(solution)/shard_map/ppermute | solution.py:199
  79.2 1.6 %collective-permute-done.9.refs_8_ = f32[2,64,256]{2,1,0:T(8,128)S(1)} collective-permute-done((f32[2,64,256]{2,1,0:T(8,128)S(1)}, f32[2,64,256]{2,1,0:T(8,128)S(1)}, u32[]{:S(2)}, u32[]{:S(2)}) %collective-permute-start.9) | collective-permute-done | bytes 131104 | tf_op jit(solution)/shard_map/ppermute | solution.py:199
  81.4 1.8 %all-to-all-done.1.refs_0_ = f32[8,64,256]{2,1,0:T(8,128)S(1)} async-done(((f32[8,64,256]{2,1,0:T(8,128)}), f32[8,64,256]{2,1,0:T(8,128)S(1)}, u32[]{:S(2)}, u32[]{:S(2)}) %all-to-all-start.1) | async-done | bytes 524320 | tf_op jit(solution)/shard_map/all_to_all | solution.py:46
  83.8 3.7 %collective-permute-start.12 = (f32[8,64,256]{2,1,0:T(8,128)S(1)}, f32[8,64,256]{2,1,0:T(8,128)S(1)}, u32[]{:S(2)}, u32[]{:S(2)}) collective-permute-start(f32[8,64,256]{2,1,0:T(8,128)S(1)} %all-to-all-done.1.refs_0_), channel_id=1, source_target_pairs={{0,192},{8,200},{16,208},{24,216},{32,224},{40,232},{48,240},{56,2... | collective-permute-start | bytes 1572872 | tf_op jit(solution)/shard_map/ppermute | solution.py:50
  87.5 2.8 %collective-permute-start.14 = (f32[4,64,256]{2,1,0:T(8,128)S(1)}, f32[4,64,256]{2,1,0:T(8,128)S(1)}, u32[]{:S(2)}, u32[]{:S(2)}) collective-permute-start(f32[4,64,256]{2,1,0:T(8,128)S(1)} %get-tuple-element.38), channel_id=1, source_target_pairs={{0,8},{8,16},{16,24},{24,32},{32,40},{40,48},{48,56},{56,0},{64,72... | collective-permute-start | bytes 786440 | tf_op jit(solution)/shard_map/ppermute | solution.py:53
  90.8 5.8 %collective-permute-done.14.refs_3_ = f32[4,64,256]{2,1,0:T(8,128)S(1)} collective-permute-done((f32[4,64,256]{2,1,0:T(8,128)S(1)}, f32[4,64,256]{2,1,0:T(8,128)S(1)}, u32[]{:S(2)}, u32[]{:S(2)}) %collective-permute-start.14) | collective-permute-done | bytes 262176 | tf_op jit(solution)/shard_map/ppermute | solution.py:53
  96.7 2.8 %collective-permute-done.15.refs_4_ = f32[8,64,256]{2,1,0:T(8,128)S(1)} collective-permute-done((f32[8,64,256]{2,1,0:T(8,128)S(1)}, f32[8,64,256]{2,1,0:T(8,128)S(1)}, u32[]{:S(2)}, u32[]{:S(2)}) %collective-permute-start.15) | collective-permute-done | bytes 524320 | tf_op jit(solution)/shard_map/ppermute | solution.py:51
  99.4 1.6 %copy-done.1 = bf16[512,2048]{1,0:T(8,128)(2,1)S(1)} copy-done((bf16[512,2048]{1,0:T(8,128)(2,1)S(1)}, bf16[512,2048]{1,0:T(8,128)(2,1)}, u32[]{:S(2)}) %copy-start.1) | copy-done | bytes 2097176
  101.9 2.8 %shard_map.70 = (f32[4,72,256]{2,1,0:T(8,128)S(1)}, f32[4,72,256]{2,1,0:T(8,128)S(1)}) custom-call(s32[3]{0:T(128)S(1)} %pad_add_fusion.place, f32[8,64,256]{2,1,0:T(8,128)S(1)} %all-to-all-done.1.refs_0_, f32[8,64,256]{2,1,0:T(8,128)S(1)} %collective-permute-done.12.refs_1_, f32[4,64,256]{2,1,0:T(8,128)S(1)} %collective-permute-done.13.refs_2_, ...), custom_call_target="tpu_custom_call" | custom-call | flops 1610612736 | bytes 7340032 | tf_op jit(solution)/shard_map/pallas_call | solution.py:104
  104.9 1.6 %collective-permute-done.16 = f32[4,72,256]{2,1,0:T(8,128)S(1)} collective-permute-done((f32[4,72,256]{2,1,0:T(8,128)S(1)}, f32[4,72,256]{2,1,0:T(8,128)S(1)}, u32[]{:S(2)}, u32[]{:S(2)}) %collective-permute-start.16) | collective-permute-done | bytes 294944 | tf_op jit(solution)/shard_map/ppermute | solution.py:192
  106.6 1.7 %collective-permute-start.18 = (f32[72,256]{1,0:T(8,128)S(1)}, f32[72,256]{1,0:T(8,128)S(1)}, u32[]{:S(2)}, u32[]{:S(2)}) collective-permute-start(f32[72,256]{1,0:T(8,128)S(1)} %get-tuple-element.35), channel_id=1, source_target_pairs={{0,4},{1,5},{2,6},{3,7},{4,0},{5,1},{6,2},{7,3},{8,12},{9,13},{10,... | collective-permute-start | bytes 221192 | tf_op jit(solution)/shard_map/ppermute | solution.py:194
  108.3 1.5 %collective-permute-start.17 = (f32[72,256]{1,0:T(8,128)S(1)}, f32[72,256]{1,0:T(8,128)S(1)}, u32[]{:S(2)}, u32[]{:S(2)}) collective-permute-start(f32[72,256]{1,0:T(8,128)S(1)} %get-tuple-element.36), channel_id=1, source_target_pairs={{0,2},{1,3},{2,4},{3,5},{4,6},{5,7},{6,0},{7,1},{8,10},{9,11},{10,... | collective-permute-start | bytes 221192 | tf_op jit(solution)/shard_map/ppermute | solution.py:194
  109.8 3.9 %collective-permute-done.19.t3 = f32[72,256]{1,0:T(8,128)S(1)} collective-permute-done((f32[72,256]{1,0:T(8,128)S(1)}, f32[72,256]{1,0:T(8,128)S(1)}, u32[]{:S(2)}, u32[]{:S(2)}) %collective-permute-start.19) | collective-permute-done | bytes 73760 | tf_op jit(solution)/shard_map/ppermute | solution.py:194
  114.5 18.7 %all_to_all.16.tiles = f32[32,8,128]{2,1,0:T(8,128)S(1)} all-to-all(f32[32,8,128]{2,1,0:T(8,128)S(1)} %get-tuple-element.30), channel_id=1, replica_groups=mesh['row'=32,'col'=8] {'row'}, dimensions={0} | all-to-all | bytes 262144 | tf_op jit(solution)/shard_map/all_to_all | solution.py:224
  (44 shorter events, 9.5 us)
Async XLA Ops:
  30.8 11.0 %collective-permute-start.2 = (f32[4,64,256]{2,1,0:T(8,128)}, f32[4,64,256]{2,1,0:T(8,128)}, u32[]{:S(2)}, u32[]{:S(2)}) collective-permute-start(f32[4,64,256]{2,1,0:T(8,128)} %get-tuple-element.44), channel_id=1, source_target_pairs={{0,8},{8,16},{16,24},{24,32},{32,40},{40,48},{48,56},{56,0},{64,72... | collective-permute-start | bytes 786440 | tf_op jit(solution)/shard_map/ppermute | solution.py:53
  32.3 9.6 %collective-permute-start.1 = (f32[4,64,256]{2,1,0:T(8,128)}, f32[4,64,256]{2,1,0:T(8,128)}, u32[]{:S(2)}, u32[]{:S(2)}) collective-permute-start(f32[4,64,256]{2,1,0:T(8,128)} %get-tuple-element.45), channel_id=1, source_target_pairs={{0,56},{8,0},{16,8},{24,16},{32,24},{40,32},{48,40},{56,48},{64,12... | collective-permute-start | bytes 786440 | tf_op jit(solution)/shard_map/ppermute | solution.py:52
  34.0 11.4 %collective-permute-start.3 = (f32[8,64,256]{2,1,0:T(8,128)S(1)}, f32[8,64,256]{2,1,0:T(8,128)S(1)}, u32[]{:S(2)}, u32[]{:S(2)}) collective-permute-start(f32[8,64,256]{2,1,0:T(8,128)S(1)} %all_to_all.15.refs_0_), channel_id=1, source_target_pairs={{0,64},{8,72},{16,80},{24,88},{32,96},{40,104},{48,112},{56,120},{... | collective-permute-start | bytes 1572872 | tf_op jit(solution)/shard_map/ppermute | solution.py:51
  34.7 10.7 %collective-permute-start = (f32[8,64,256]{2,1,0:T(8,128)S(1)}, f32[8,64,256]{2,1,0:T(8,128)}, u32[]{:S(2)}, u32[]{:S(2)}) collective-permute-start(f32[8,64,256]{2,1,0:T(8,128)S(1)} %all_to_all.15.refs_0_), channel_id=1, source_target_pairs={{0,192},{8,200},{16,208},{24,216},{32,224},{40,232},{48,240},{56,2... | collective-permute-start | bytes 1572872 | tf_op jit(solution)/shard_map/ppermute | solution.py:50
  37.2 22.2 %copy-start.2 = (f32[256,256]{1,0:T(8,128)S(1)}, f32[256,256]{1,0:T(8,128)}, u32[]{:S(2)}) copy-start(f32[256,256]{1,0:T(8,128)} %kernel.3) | copy-start | bytes 786436
  41.7 14.4 %copy-start.6 = (s32[64]{0:T(128)S(1)}, s32[64]{0:T(128)}, u32[]{:S(2)}) copy-start(s32[64]{0:T(128)} %param.7) | copy-start | bytes 772
  41.7 17.7 %copy-start.7 = (f32[64]{0:T(128)S(1)}, f32[64]{0:T(128)}, u32[]{:S(2)}) copy-start(f32[64]{0:T(128)} %param.8) | copy-start | bytes 772
  45.4 1.6 %copy-start = (bf16[512,2048]{1,0:T(8,128)(2,1)S(1)}, bf16[512,2048]{1,0:T(8,128)(2,1)}, u32[]{:S(2)}) copy-start(bf16[512,2048]{1,0:T(8,128)(2,1)} %get-tuple-element.33.refs_5_) | copy-start | bytes 6291460
  50.3 1.6 %collective-permute-start.4 = (f32[4,64,256]{2,1,0:T(8,128)S(1)}, f32[4,64,256]{2,1,0:T(8,128)S(1)}, u32[]{:S(2)}, u32[]{:S(2)}) collective-permute-start(f32[4,64,256]{2,1,0:T(8,128)S(1)} %get-tuple-element.18), channel_id=1, source_target_pairs={{0,1},{1,0},{2,3},{3,2},{4,5},{5,4},{6,7},{7,6},{8,9},{9,8},{10,11... | collective-permute-start | bytes 786440 | tf_op jit(solution)/shard_map/ppermute | solution.py:192
  52.0 7.0 %collective-permute-start.7 = (f32[64,256]{1,0:T(8,128)S(1)}, f32[64,256]{1,0:T(8,128)S(1)}, u32[]{:S(2)}, u32[]{:S(2)}) collective-permute-start(f32[64,256]{1,0:T(8,128)S(1)} %get-tuple-element.40), channel_id=1, source_target_pairs={{0,6},{1,7},{2,0},{3,1},{4,2},{5,3},{6,4},{7,5},{8,14},{9,15},{10,... | collective-permute-start | bytes 196616 | tf_op jit(solution)/shard_map/ppermute | solution.py:194
  52.9 6.1 %collective-permute-start.6 = (f32[64,256]{1,0:T(8,128)S(1)}, f32[64,256]{1,0:T(8,128)S(1)}, u32[]{:S(2)}, u32[]{:S(2)}) collective-permute-start(f32[64,256]{1,0:T(8,128)S(1)} %get-tuple-element.41), channel_id=1, source_target_pairs={{0,4},{1,5},{2,6},{3,7},{4,0},{5,1},{6,2},{7,3},{8,12},{9,13},{10,... | collective-permute-start | bytes 196616 | tf_op jit(solution)/shard_map/ppermute | solution.py:194
  54.0 5.4 %collective-permute-start.5 = (f32[64,256]{1,0:T(8,128)S(1)}, f32[64,256]{1,0:T(8,128)S(1)}, u32[]{:S(2)}, u32[]{:S(2)}) collective-permute-start(f32[64,256]{1,0:T(8,128)S(1)} %get-tuple-element.42), channel_id=1, source_target_pairs={{0,2},{1,3},{2,4},{3,5},{4,6},{5,7},{6,0},{7,1},{8,10},{9,11},{10,... | collective-permute-start | bytes 196616 | tf_op jit(solution)/shard_map/ppermute | solution.py:194
  60.2 0.8 copy-start.3
  61.1 22.2 %all-to-all-start.1 = ((f32[8,64,256]{2,1,0:T(8,128)}), f32[8,64,256]{2,1,0:T(8,128)S(1)}, u32[]{:S(2)}, u32[]{:S(2)}) async-start(f32[8,64,256]{2,1,0:T(8,128)} %copy-done.3), calls=%async_computation.1 | async-start | bytes 1048576 | tf_op jit(solution)/shard_map/all_to_all | solution.py:46
  67.3 1.3 collective-permute-start.8
  68.6 8.7 %collective-permute-start.11 = (f32[2,64,256]{2,1,0:T(8,128)S(1)}, f32[2,64,256]{2,1,0:T(8,128)S(1)}, u32[]{:S(2)}, u32[]{:S(2)}) collective-permute-start(f32[2,64,256]{2,1,0:T(8,128)S(1)} %pad_maximum_fusion.refs_7_), channel_id=1, source_target_pairs={{0,2},{1,3},{2,4},{3,5},{4,6},{5,7},{6,0},{7,1},{8,10},{9,11},{10,... | collective-permute-start | bytes 393224 | tf_op jit(solution)/shard_map/ppermute | solution.py:199
  71.3 7.9 %collective-permute-start.10 = (f32[2,64,256]{2,1,0:T(8,128)S(1)}, f32[2,64,256]{2,1,0:T(8,128)S(1)}, u32[]{:S(2)}, u32[]{:S(2)}) collective-permute-start(f32[2,64,256]{2,1,0:T(8,128)S(1)} %pad_maximum_fusion.refs_7_), channel_id=1, source_target_pairs={{0,4},{1,5},{2,6},{3,7},{4,0},{5,1},{6,2},{7,3},{8,12},{9,13},{10,... | collective-permute-start | bytes 393224 | tf_op jit(solution)/shard_map/ppermute | solution.py:199
  71.8 9.0 %collective-permute-start.9 = (f32[2,64,256]{2,1,0:T(8,128)S(1)}, f32[2,64,256]{2,1,0:T(8,128)S(1)}, u32[]{:S(2)}, u32[]{:S(2)}) collective-permute-start(f32[2,64,256]{2,1,0:T(8,128)S(1)} %pad_maximum_fusion.refs_7_), channel_id=1, source_target_pairs={{0,6},{1,7},{2,0},{3,1},{4,2},{5,3},{6,4},{7,5},{8,14},{9,15},{10,... | collective-permute-start | bytes 393224 | tf_op jit(solution)/shard_map/ppermute | solution.py:199
  80.8 0.6 copy-start.4
  83.3 16.1 %collective-permute-start.15 = (f32[8,64,256]{2,1,0:T(8,128)S(1)}, f32[8,64,256]{2,1,0:T(8,128)S(1)}, u32[]{:S(2)}, u32[]{:S(2)}) collective-permute-start(f32[8,64,256]{2,1,0:T(8,128)S(1)} %all-to-all-done.1.refs_0_), channel_id=1, source_target_pairs={{0,64},{8,72},{16,80},{24,88},{32,96},{40,104},{48,112},{56,120},{... | collective-permute-start | bytes 1572872 | tf_op jit(solution)/shard_map/ppermute | solution.py:51
  83.8 15.7 %collective-permute-start.12 = (f32[8,64,256]{2,1,0:T(8,128)S(1)}, f32[8,64,256]{2,1,0:T(8,128)S(1)}, u32[]{:S(2)}, u32[]{:S(2)}) collective-permute-start(f32[8,64,256]{2,1,0:T(8,128)S(1)} %all-to-all-done.1.refs_0_), channel_id=1, source_target_pairs={{0,192},{8,200},{16,208},{24,216},{32,224},{40,232},{48,240},{56,2... | collective-permute-start | bytes 1572872 | tf_op jit(solution)/shard_map/ppermute | solution.py:50
  87.5 9.1 %collective-permute-start.14 = (f32[4,64,256]{2,1,0:T(8,128)S(1)}, f32[4,64,256]{2,1,0:T(8,128)S(1)}, u32[]{:S(2)}, u32[]{:S(2)}) collective-permute-start(f32[4,64,256]{2,1,0:T(8,128)S(1)} %get-tuple-element.38), channel_id=1, source_target_pairs={{0,8},{8,16},{16,24},{24,32},{32,40},{40,48},{48,56},{56,0},{64,72... | collective-permute-start | bytes 786440 | tf_op jit(solution)/shard_map/ppermute | solution.py:53
  90.3 6.4 %collective-permute-start.13 = (f32[4,64,256]{2,1,0:T(8,128)S(1)}, f32[4,64,256]{2,1,0:T(8,128)S(1)}, u32[]{:S(2)}, u32[]{:S(2)}) collective-permute-start(f32[4,64,256]{2,1,0:T(8,128)S(1)} %get-tuple-element.39), channel_id=1, source_target_pairs={{0,56},{8,0},{16,8},{24,16},{32,24},{40,32},{48,40},{56,48},{64,12... | collective-permute-start | bytes 786440 | tf_op jit(solution)/shard_map/ppermute | solution.py:52
  99.4 1.6 %copy-start.1 = (bf16[512,2048]{1,0:T(8,128)(2,1)S(1)}, bf16[512,2048]{1,0:T(8,128)(2,1)}, u32[]{:S(2)}) copy-start(bf16[512,2048]{1,0:T(8,128)(2,1)} %get-tuple-element.33.refs_5_) | copy-start | bytes 6291460
  101.0 0.9 copy-start.5
  104.8 1.7 %collective-permute-start.16 = (f32[4,72,256]{2,1,0:T(8,128)S(1)}, f32[4,72,256]{2,1,0:T(8,128)S(1)}, u32[]{:S(2)}, u32[]{:S(2)}) collective-permute-start(f32[4,72,256]{2,1,0:T(8,128)S(1)} %get-tuple-element.28), channel_id=1, source_target_pairs={{0,1},{1,0},{2,3},{3,2},{4,5},{5,4},{6,7},{7,6},{8,9},{9,8},{10,11... | collective-permute-start | bytes 884744 | tf_op jit(solution)/shard_map/ppermute | solution.py:192
  106.5 7.2 %collective-permute-start.19 = (f32[72,256]{1,0:T(8,128)S(1)}, f32[72,256]{1,0:T(8,128)S(1)}, u32[]{:S(2)}, u32[]{:S(2)}) collective-permute-start(f32[72,256]{1,0:T(8,128)S(1)} %get-tuple-element.34), channel_id=1, source_target_pairs={{0,6},{1,7},{2,0},{3,1},{4,2},{5,3},{6,4},{7,5},{8,14},{9,15},{10,... | collective-permute-start | bytes 221192 | tf_op jit(solution)/shard_map/ppermute | solution.py:194
  106.6 7.1 %collective-permute-start.18 = (f32[72,256]{1,0:T(8,128)S(1)}, f32[72,256]{1,0:T(8,128)S(1)}, u32[]{:S(2)}, u32[]{:S(2)}) collective-permute-start(f32[72,256]{1,0:T(8,128)S(1)} %get-tuple-element.35), channel_id=1, source_target_pairs={{0,4},{1,5},{2,6},{3,7},{4,0},{5,1},{6,2},{7,3},{8,12},{9,13},{10,... | collective-permute-start | bytes 221192 | tf_op jit(solution)/shard_map/ppermute | solution.py:194
  108.3 5.9 %collective-permute-start.17 = (f32[72,256]{1,0:T(8,128)S(1)}, f32[72,256]{1,0:T(8,128)S(1)}, u32[]{:S(2)}, u32[]{:S(2)}) collective-permute-start(f32[72,256]{1,0:T(8,128)S(1)} %get-tuple-element.36), channel_id=1, source_target_pairs={{0,2},{1,3},{2,4},{3,5},{4,6},{5,7},{6,0},{7,1},{8,10},{9,11},{10,... | collective-permute-start | bytes 221192 | tf_op jit(solution)/shard_map/ppermute | solution.py:194

commit v3 on v2

--- a/solution.py
+++ b/solution.py
@@ -37,11 +37,6 @@
 SIBLING = [(c, c ^ 1) for c in range(8)]
 
 
-def split(value):
-    high = lax.reduce_precision(value, 8, 7)
-    return high.astype(BF16), (value - high).astype(BF16)
-
-
 def gather_class(copies):
     return lax.all_to_all(copies, "row", 0, 0, axis_index_groups=CLASSES)
 
@@ -49,8 +44,9 @@
 def gather_rest(own):
     next_y = lax.ppermute(own, "row", shift_y(-1))
     last_y = lax.ppermute(own, "row", shift_y(1))
-    next_z = lax.ppermute(own[:4], "row", shift_z(-1))
-    last_z = lax.ppermute(own[4:], "row", shift_z(1))
+    lower, upper = small_call(halves_kernel, [(4, BLOCK, EPOCHS)] * 2, own)
+    next_z = lax.ppermute(lower, "row", shift_z(-1))
+    last_z = lax.ppermute(upper, "row", shift_z(1))
     return own, next_y, next_z, last_z, last_y
 
 
@@ -99,6 +95,25 @@
 VMEM_SPEC = pl.BlockSpec(memory_space=pltpu.VMEM)
 
 
+def split_kernel(tile, high, low):
+    value = tile[...]
+    top = value.astype(BF16)
+    high[...] = top
+    low[...] = (value - top.astype(F32)).astype(BF16)
+
+
+def split(tile):
+    half = jax.ShapeDtypeStruct(tile.shape, BF16)
+    return pl.pallas_call(
+        split_kernel,
+        out_shape=(half, half),
+        in_specs=[VMEM_SPEC],
+        out_specs=(VMEM_SPEC, VMEM_SPEC),
+        compiler_params=pltpu.CompilerParams(vmem_limit_bytes=16 * 1024 * 1024),
+        cost_estimate=pl.CostEstimate(flops=4 * tile.size, bytes_accessed=8 * tile.size, transcendentals=0),
+    )(tile)
+
+
 def product(place, parts, k_high, k_low, extra=()):
     half = jax.ShapeDtypeStruct((NX, BLOCK + (8 if extra else 0), EPOCHS), F32)
     return pl.pallas_call(
@@ -107,7 +122,7 @@
         in_specs=[pl.BlockSpec(memory_space=pltpu.SMEM)] + [VMEM_SPEC] * (7 + len(extra)),
         out_specs=(VMEM_SPEC, VMEM_SPEC),
         scratch_shapes=[pltpu.VMEM((2048, EPOCHS), BF16), pltpu.VMEM((2048, EPOCHS), BF16)],
-        compiler_params=pltpu.CompilerParams(vmem_limit_bytes=24 * 1024 * 1024),
+        compiler_params=pltpu.CompilerParams(vmem_limit_bytes=16 * 1024 * 1024),
         cost_estimate=pl.CostEstimate(
             flops=2 * 3 * 512 * 2048 * EPOCHS, bytes_accessed=7 * 1024 * 1024, transcendentals=0
         ),
@@ -118,13 +133,13 @@
     return jnp.dot(a, b, precision=lax.Precision.HIGHEST, preferred_element_type=F32)
 
 
-def small_call(kernel, outs, *args):
+def small_call(kernel, outs, *args, limit=4):
     return pl.pallas_call(
         kernel,
         out_shape=[jax.ShapeDtypeStruct(o, F32) for o in outs],
         in_specs=[VMEM_SPEC] * len(args),
         out_specs=[VMEM_SPEC] * len(outs),
-        compiler_params=pltpu.CompilerParams(vmem_limit_bytes=8 * 1024 * 1024),
+        compiler_params=pltpu.CompilerParams(vmem_limit_bytes=limit * 1024 * 1024),
         cost_estimate=pl.CostEstimate(
             flops=2 * 6 * BLOCK * EPOCHS * EPOCHS, bytes_accessed=1024 * 1024, transcendentals=0
         ),
@@ -166,13 +181,13 @@
 def second_kernel(t0, t1, t2, t3, kernel, mask, noise, w1, w2, copies):
     total = t0[...] + t1[...] + t2[...] + t3[...]
     for j in range(32):
-        copies[j] = total[BLOCK:, :128]
+        copies[j] = total[BLOCK : BLOCK + 1, :128]
     w2[...] = mask[...] * dot(total[:BLOCK], kernel[...]) + noise[...] * w1[...]
 
 
 def last_kernel(tiles, r0, w1, w2, out, residual):
     tile = jnp.sum(tiles[...], axis=0)
-    lane = lax.broadcasted_iota(jnp.int32, (8, 128), 1)
+    lane = lax.broadcasted_iota(jnp.int32, (1, 128), 1)
 
     def pick(i):
         return jnp.sum(jnp.where(lane == i, tile, 0.0), keepdims=True)
@@ -188,38 +203,61 @@
     residual[...] = r1 - a1 * (c0 * w1[...] - a0 * w2[...])
 
 
+def halves_kernel(own, lower, upper):
+    lower[...] = own[:4]
+    upper[...] = own[4:]
+
+
+def add_kernel(keep, other, *total):
+    for d in range(NX):
+        total[d][...] = keep[d] + other[d]
+
+
+def pair_kernel(image, other, pair):
+    pair[0] = image[...]
+    pair[1] = other[...]
+
+
 def scatter_col(keep, send):
     other = lax.ppermute(send, "col", SIBLING)
-    total = [keep[d] + other[d] for d in range(NX)]
+    total = small_call(add_kernel, [keep.shape[1:]] * NX, keep, other)
     return total[0], *[lax.ppermute(total[d], "col", shift_x(d)) for d in range(1, NX)]
 
 
 def gather_col(image):
-    pair = jnp.stack([image, lax.ppermute(image, "col", SIBLING)])
+    other = lax.ppermute(image, "col", SIBLING)
+    (pair,) = small_call(pair_kernel, [(2, BLOCK, EPOCHS)], image, other)
     return pair, *[lax.ppermute(pair, "col", shift_x(-d)) for d in range(1, NX)]
 
 
 def per_device(kernel_configs, epoch_kernel, lengths, noise, curves):
-    epoch_index = lax.broadcasted_iota(jnp.int32, (BLOCK, EPOCHS), 1)
-    mask = (epoch_index < lengths[:, None]).astype(F32)
-    noise = jnp.broadcast_to(noise[:, None], (BLOCK, EPOCHS))
+    block = (BLOCK, EPOCHS)
+
+    def mask_of(lengths):
+        epoch_index = lax.broadcasted_iota(jnp.int32, block, 1)
+        return (epoch_index < lengths[:, None]).astype(F32)
+
     row, col = lax.axis_index("row"), lax.axis_index("col")
     colour = lax.rem(row // NZ + 2 * lax.rem(row, NZ), 4)
     place = jnp.stack([colour, col // 2, lax.rem(col, 2)]).astype(jnp.int32)
-    k_high, k_low = split(kernel_configs.reshape(-1, kernel_configs.shape[2]))
-    block = (BLOCK, EPOCHS)
-
-    r0 = curves * mask
-    parts = gather_rest(gather_class(jnp.broadcast_to(r0[None], (8, BLOCK, EPOCHS))))
+    tile = kernel_configs.reshape(-1, kernel_configs.shape[2])
+
+    r0 = curves * mask_of(lengths)
+    own = gather_class(jnp.broadcast_to(r0[None], (8, BLOCK, EPOCHS)))
+    own, first_tile, lengths, noise = lax.optimization_barrier((own, tile, lengths, noise))
+    mask, noise = mask_of(lengths), jnp.broadcast_to(noise[:, None], block)
+    parts = gather_rest(own)
+    k_high, k_low = split(first_tile)
     pieces = scatter_col(*product(place, parts, k_high, k_low))
     w1, copies, image, sums = small_call(
         first_kernel, [block, (8, *block), block, (8, EPOCHS)], *pieces, epoch_kernel, mask, noise, r0
     )
-    own, images = lax.optimization_barrier((gather_class(copies), gather_col(image)))
+    own, images, second_tile = lax.optimization_barrier((gather_class(copies), gather_col(image), tile))
     parts = gather_rest(own)
+    k_high, k_low = split(second_tile)
     pieces = scatter_col(*product(place, parts, k_high, k_low, (*images, sums)))
     w2, copies = small_call(
-        second_kernel, [block, (32, 8, 128)], *pieces, epoch_kernel, mask, noise, w1
+        second_kernel, [block, (32, 1, 128)], *pieces, epoch_kernel, mask, noise, w1
     )
     tiles = lax.all_to_all(copies, "row", 0, 0)
     return tuple(small_call(last_kernel, [block, block], tiles, r0, w1, w2))

time: 136 us -> 124 us (0.912)
  starting transfers between devices: 31.6 us -> 26.1 us
  other arithmetic: 5.62 us -> 1.06 us
  blocking collectives: 47.1 us -> 44.6 us
  waiting for transfers between devices: 34.5 us -> 36.7 us
  local copies, waits for them, and re-layouts: 6.55 us -> 4.5 us
    convert_element_type x2 -> x1, other arithmetic: 4.55 us -> 0.07 us  [mask_of(): return (epoch_index < lengths[:, None]).astype(F32)]
    ppermute x2, waiting for transfers between devices: 6.35 us -> 2.2 us  [gather_rest(): last_y = lax.ppermute(own, 'row', shift_y(1))]
    ppermute x6, waiting for transfers between devices: 7.64 us -> 11.3 us  [scatter_col(): lax.ppermute(total[d], 'col', shift_x(d))]
    ppermute x2, starting transfers between devices: 6.28 us -> 3.57 us  [gather_rest(): next_y = lax.ppermute(own, 'row', shift_y(-1))]
    all_to_all x1, blocking collectives: 18.7 us -> 16.3 us  [per_device(): tiles = lax.all_to_all(copies, 'row', 0, 0)]
    ppermute x6, starting transfers between devices: 7.42 us -> 5.22 us  [scatter_col(): lax.ppermute(total[d], 'col', shift_x(d))]
    all_to_all x1, waiting for transfers between devices: 1.84 us -> 3.97 us  [gather_class(): return lax.all_to_all(copies, 'row', 0, 0, axis_index_groups=CLASSES)]
    ppermute x2, starting transfers between devices: 1.15 us -> 2.9 us  [gather_rest(): last_y = lax.ppermute(own, 'row', shift_y(1))]
  transfers between devices with their start and end apart: 21 -> 21, of which waited for: 15 -> 19; matrix products, arithmetic and copies ran while one was open for 3% -> 0% of each run, Pallas kernels for 0% -> 1%
where the time goes in v3:
time: 124 us; the launch traced here: 123 us
  blocking collectives  44.6 us (36%)
  waiting for transfers between devices  36.7 us (30%)
  starting transfers between devices  26.1 us (21%)
  Pallas kernels  9.39 us (8%)
  local copies, waits for them, and re-layouts  4.5 us (4%)
    all_to_all x1, blocking collectives, gather_class(): return lax.all_to_all(copies, 'row', 0, 0, axis_index_groups=CLASSES)  28.3 us
    all_to_all x1, blocking collectives, per_device(): tiles = lax.all_to_all(copies, 'row', 0, 0)  16.3 us
    ppermute x6, waiting for transfers between devices, scatter_col(): lax.ppermute(total[d], 'col', shift_x(d))  11.3 us
    ppermute x3, waiting for transfers between devices, gather_col(): lax.ppermute(pair, 'col', shift_x(-d))  8.14 us
    all_to_all x1, starting transfers between devices, gather_class(): return lax.all_to_all(copies, 'row', 0, 0, axis_index_groups=CLASSES)  6.27 us
    pallas_call x2, Pallas kernels, product(): pl.pallas_call(functools.partial(product_kernel, bool(extra)), out_shape=...  5.55 us
    ppermute x6, starting transfers between devices, scatter_col(): lax.ppermute(total[d], 'col', shift_x(d))  5.22 us
    unnamed x10, local copies, waits for them, and re-layouts  4.39 us
  transfers between devices with their start and end apart: 21, of which 19 were waited for; matrix products, arithmetic and copies ran while one was open for 0% of the time, Pallas kernels for 1%

profile of v3, /device:TPU:6, one launch (start us, length us, event | category | flops | bytes accessed | tf_op | source)
XLA Modules:
  0.0 123.1 jit_solution(12421653712283642234)
XLA Ops:
  1.6 28.3 %all_to_all.15.own.refs_0_ = f32[8,64,256]{2,1,0:T(8,128)S(1)} all-to-all(f32[8,64,256]{2,1,0:T(8,128)S(1)} %broadcast_in_dim.4), channel_id=1, replica_groups={{0,16,32,48,136,152,168,184},{64,80,96,112,200,216,232,248},{8,24,40,56..., dimensions={0} | all-to-all | bytes 1048576 | tf_op jit(solution)/shard_map/all_to_all | solution.py:41
  30.6 2.6 %collective-permute-start = (f32[8,64,256]{2,1,0:T(8,128)S(1)}, f32[8,64,256]{2,1,0:T(8,128)S(1)}, u32[]{:S(2)}, u32[]{:S(2)}) collective-permute-start(f32[8,64,256]{2,1,0:T(8,128)S(1)} %all_to_all.15.own.refs_0_), channel_id=1, source_target_pairs={{0,192},{8,200},{16,208},{24,216},{32,224},{40,232},{48,240},{56,2... | collective-permute-start | bytes 1572872 | tf_op jit(solution)/shard_map/ppermute | solution.py:45
  35.4 2.2 %copy-done = f32[8,64,2048]{2,1,0:T(8,128)S(1)} copy-done((f32[8,64,2048]{2,1,0:T(8,128)S(1)}, f32[8,64,2048]{2,1,0:T(8,128)}, u32[]{:S(2)}) %copy-start) | copy-done | bytes 4194328
  38.3 1.4 %collective-permute-done.1.refs_2_ = f32[4,64,256]{2,1,0:T(8,128)S(1)} collective-permute-done((f32[4,64,256]{2,1,0:T(8,128)S(1)}, f32[4,64,256]{2,1,0:T(8,128)S(1)}, u32[]{:S(2)}, u32[]{:S(2)}) %collective-permute-start.1) | collective-permute-done | bytes 262176 | tf_op jit(solution)/shard_map/ppermute | solution.py:48
  39.6 2.2 %collective-permute-done.2.refs_3_ = f32[4,64,256]{2,1,0:T(8,128)S(1)} collective-permute-done((f32[4,64,256]{2,1,0:T(8,128)S(1)}, f32[4,64,256]{2,1,0:T(8,128)S(1)}, u32[]{:S(2)}, u32[]{:S(2)}) %collective-permute-start.2) | collective-permute-done | bytes 262176 | tf_op jit(solution)/shard_map/ppermute | solution.py:49
  41.9 2.7 %shard_map.70 = (f32[4,64,256]{2,1,0:T(8,128)S(1)}, f32[4,64,256]{2,1,0:T(8,128)S(1)}) custom-call(s32[3]{0:T(128)S(1)} %pad_add_fusion.place, f32[8,64,256]{2,1,0:T(8,128)S(1)} %all_to_all.15.own.refs_0_, f32[8,64,256]{2,1,0:T(8,128)S(1)} %collective-permute-done.refs_1_, f32[4,64,256]{2,1,0:T(8,128)S(1)} %collective-permute-done.1.refs_2_, ...), custom_call_target="tpu_custom_call" | custom-call | flops 1610612736 | bytes 7340032 | tf_op jit(solution)/shard_map/pallas_call | solution.py:119
  44.7 1.5 %collective-permute-done.4.other = f32[4,64,256]{2,1,0:T(8,128)S(1)} collective-permute-done((f32[4,64,256]{2,1,0:T(8,128)S(1)}, f32[4,64,256]{2,1,0:T(8,128)S(1)}, u32[]{:S(2)}, u32[]{:S(2)}) %collective-permute-start.4) | collective-permute-done | bytes 262176 | tf_op jit(solution)/shard_map/ppermute | solution.py:222
  46.8 2.4 %collective-permute-start.6 = (f32[64,256]{1,0:T(8,128)S(1)}, f32[64,256]{1,0:T(8,128)S(1)}, u32[]{:S(2)}, u32[]{:S(2)}) collective-permute-start(f32[64,256]{1,0:T(8,128)S(1)} %get-tuple-element.48), channel_id=1, source_target_pairs={{0,4},{1,5},{2,6},{3,7},{4,0},{5,1},{6,2},{7,3},{8,12},{9,13},{10,... | collective-permute-start | bytes 196616 | tf_op jit(solution)/shard_map/ppermute | solution.py:224
  49.3 1.9 %collective-permute-done.5.t1 = f32[64,256]{1,0:T(8,128)S(1)} collective-permute-done((f32[64,256]{1,0:T(8,128)S(1)}, f32[64,256]{1,0:T(8,128)S(1)}, u32[]{:S(2)}, u32[]{:S(2)}) %collective-permute-start.5) | collective-permute-done | bytes 65568 | tf_op jit(solution)/shard_map/ppermute | solution.py:224
  51.1 1.4 %collective-permute-done.6.t2 = f32[64,256]{1,0:T(8,128)S(1)} collective-permute-done((f32[64,256]{1,0:T(8,128)S(1)}, f32[64,256]{1,0:T(8,128)S(1)}, u32[]{:S(2)}, u32[]{:S(2)}) %collective-permute-start.6) | collective-permute-done | bytes 65568 | tf_op jit(solution)/shard_map/ppermute | solution.py:224
  52.6 2.1 %collective-permute-done.7.t3 = f32[64,256]{1,0:T(8,128)S(1)} collective-permute-done((f32[64,256]{1,0:T(8,128)S(1)}, f32[64,256]{1,0:T(8,128)S(1)}, u32[]{:S(2)}, u32[]{:S(2)}) %collective-permute-start.7) | collective-permute-done | bytes 65568 | tf_op jit(solution)/shard_map/ppermute | solution.py:224
  54.8 1.2 shard_map.72
  55.9 6.3 %all-to-all-start.1 = ((f32[8,64,256]{2,1,0:T(8,128)}), f32[8,64,256]{2,1,0:T(8,128)S(1)}, u32[]{:S(2)}, u32[]{:S(2)}) async-start(f32[8,64,256]{2,1,0:T(8,128)} %get-tuple-element.52), calls=%async_computation.1 | async-start | bytes 1048576 | tf_op jit(solution)/shard_map/all_to_all | solution.py:41
  62.2 1.2 %collective-permute-done.8.other = f32[64,256]{1,0:T(8,128)S(1)} collective-permute-done((f32[64,256]{1,0:T(8,128)S(1)}, f32[64,256]{1,0:T(8,128)S(1)}, u32[]{:S(2)}, u32[]{:S(2)}) %collective-permute-start.8) | collective-permute-done | bytes 65568 | tf_op jit(solution)/shard_map/ppermute | solution.py:228
  64.2 1.3 %collective-permute-start.10 = (f32[2,64,256]{2,1,0:T(8,128)S(1)}, f32[2,64,256]{2,1,0:T(8,128)S(1)}, u32[]{:S(2)}, u32[]{:S(2)}) collective-permute-start(f32[2,64,256]{2,1,0:T(8,128)S(1)} %shard_map.73.refs_7_), channel_id=1, source_target_pairs={{0,4},{1,5},{2,6},{3,7},{4,0},{5,1},{6,2},{7,3},{8,12},{9,13},{10,... | collective-permute-start | bytes 393224 | tf_op jit(solution)/shard_map/ppermute | solution.py:230
  65.6 4.3 %collective-permute-done.11.refs_10_ = f32[2,64,256]{2,1,0:T(8,128)S(1)} collective-permute-done((f32[2,64,256]{2,1,0:T(8,128)S(1)}, f32[2,64,256]{2,1,0:T(8,128)S(1)}, u32[]{:S(2)}, u32[]{:S(2)}) %collective-permute-start.11) | collective-permute-done | bytes 131104 | tf_op jit(solution)/shard_map/ppermute | solution.py:230
  69.9 2.1 %collective-permute-done.10.refs_9_ = f32[2,64,256]{2,1,0:T(8,128)S(1)} collective-permute-done((f32[2,64,256]{2,1,0:T(8,128)S(1)}, f32[2,64,256]{2,1,0:T(8,128)S(1)}, u32[]{:S(2)}, u32[]{:S(2)}) %collective-permute-start.10) | collective-permute-done | bytes 131104 | tf_op jit(solution)/shard_map/ppermute | solution.py:230
  72.0 1.7 %collective-permute-done.9.refs_8_ = f32[2,64,256]{2,1,0:T(8,128)S(1)} collective-permute-done((f32[2,64,256]{2,1,0:T(8,128)S(1)}, f32[2,64,256]{2,1,0:T(8,128)S(1)}, u32[]{:S(2)}, u32[]{:S(2)}) %collective-permute-start.9) | collective-permute-done | bytes 131104 | tf_op jit(solution)/shard_map/ppermute | solution.py:230
  73.7 4.0 %all-to-all-done.1.own.refs_0_ = f32[8,64,256]{2,1,0:T(8,128)S(1)} async-done(((f32[8,64,256]{2,1,0:T(8,128)}), f32[8,64,256]{2,1,0:T(8,128)S(1)}, u32[]{:S(2)}, u32[]{:S(2)}) %all-to-all-start.1) | async-done | bytes 524320 | tf_op jit(solution)/shard_map/all_to_all | solution.py:41
  77.7 2.2 %collective-permute-start.15 = (f32[8,64,256]{2,1,0:T(8,128)S(1)}, f32[8,64,256]{2,1,0:T(8,128)S(1)}, u32[]{:S(2)}, u32[]{:S(2)}) collective-permute-start(f32[8,64,256]{2,1,0:T(8,128)S(1)} %all-to-all-done.1.own.refs_0_), channel_id=1, source_target_pairs={{0,64},{8,72},{16,80},{24,88},{32,96},{40,104},{48,112},{56,120},{... | collective-permute-start | bytes 1572872 | tf_op jit(solution)/shard_map/ppermute | solution.py:46
  81.0 2.1 %collective-permute-start.13 = (f32[4,64,256]{2,1,0:T(8,128)S(1)}, f32[4,64,256]{2,1,0:T(8,128)S(1)}, u32[]{:S(2)}, u32[]{:S(2)}) collective-permute-start(f32[4,64,256]{2,1,0:T(8,128)S(1)} %get-tuple-element.55), channel_id=1, source_target_pairs={{0,56},{8,0},{16,8},{24,16},{32,24},{40,32},{48,40},{56,48},{64,12... | collective-permute-start | bytes 786440 | tf_op jit(solution)/shard_map/ppermute | solution.py:48
  83.1 1.6 %collective-permute-start.14 = (f32[4,64,256]{2,1,0:T(8,128)S(1)}, f32[4,64,256]{2,1,0:T(8,128)S(1)}, u32[]{:S(2)}, u32[]{:S(2)}) collective-permute-start(f32[4,64,256]{2,1,0:T(8,128)S(1)} %get-tuple-element.56), channel_id=1, source_target_pairs={{0,8},{8,16},{16,24},{24,32},{32,40},{40,48},{48,56},{56,0},{64,72... | collective-permute-start | bytes 786440 | tf_op jit(solution)/shard_map/ppermute | solution.py:49
  84.7 2.2 %copy-done.1 = f32[8,64,2048]{2,1,0:T(8,128)S(1)} copy-done((f32[8,64,2048]{2,1,0:T(8,128)S(1)}, f32[8,64,2048]{2,1,0:T(8,128)}, u32[]{:S(2)}) %copy-start.1) | copy-done | bytes 4194328
  87.6 1.4 %collective-permute-done.13.refs_2_ = f32[4,64,256]{2,1,0:T(8,128)S(1)} collective-permute-done((f32[4,64,256]{2,1,0:T(8,128)S(1)}, f32[4,64,256]{2,1,0:T(8,128)S(1)}, u32[]{:S(2)}, u32[]{:S(2)}) %collective-permute-start.13) | collective-permute-done | bytes 262176 | tf_op jit(solution)/shard_map/ppermute | solution.py:48
  89.0 1.9 %collective-permute-done.14.refs_3_ = f32[4,64,256]{2,1,0:T(8,128)S(1)} collective-permute-done((f32[4,64,256]{2,1,0:T(8,128)S(1)}, f32[4,64,256]{2,1,0:T(8,128)S(1)}, u32[]{:S(2)}, u32[]{:S(2)}) %collective-permute-start.14) | collective-permute-done | bytes 262176 | tf_op jit(solution)/shard_map/ppermute | solution.py:49
  90.8 2.1 %collective-permute-done.15.refs_4_ = f32[8,64,256]{2,1,0:T(8,128)S(1)} collective-permute-done((f32[8,64,256]{2,1,0:T(8,128)S(1)}, f32[8,64,256]{2,1,0:T(8,128)S(1)}, u32[]{:S(2)}, u32[]{:S(2)}) %collective-permute-start.15) | collective-permute-done | bytes 524320 | tf_op jit(solution)/shard_map/ppermute | solution.py:46
  92.9 2.9 %shard_map.76 = (f32[4,72,256]{2,1,0:T(8,128)S(1)}, f32[4,72,256]{2,1,0:T(8,128)S(1)}) custom-call(s32[3]{0:T(128)S(1)} %pad_add_fusion.place, f32[8,64,256]{2,1,0:T(8,128)S(1)} %all-to-all-done.1.own.refs_0_, f32[8,64,256]{2,1,0:T(8,128)S(1)} %collective-permute-done.12.refs_1_, f32[4,64,256]{2,1,0:T(8,128)S(1)} %collective-permute-done.13.refs_2_, ...), custom_call_target="tpu_custom_call" | custom-call | flops 1610612736 | bytes 7340032 | tf_op jit(solution)/shard_map/pallas_call | solution.py:119
  95.9 1.6 %collective-permute-done.16.other = f32[4,72,256]{2,1,0:T(8,128)S(1)} collective-permute-done((f32[4,72,256]{2,1,0:T(8,128)S(1)}, f32[4,72,256]{2,1,0:T(8,128)S(1)}, u32[]{:S(2)}, u32[]{:S(2)}) %collective-permute-start.16) | collective-permute-done | bytes 294944 | tf_op jit(solution)/shard_map/ppermute | solution.py:222
  98.6 1.2 collective-permute-start.18
  99.8 2.9 %collective-permute-done.17.t1 = f32[72,256]{1,0:T(8,128)S(1)} collective-permute-done((f32[72,256]{1,0:T(8,128)S(1)}, f32[72,256]{1,0:T(8,128)S(1)}, u32[]{:S(2)}, u32[]{:S(2)}) %collective-permute-start.17) | collective-permute-done | bytes 73760 | tf_op jit(solution)/shard_map/ppermute | solution.py:224
  102.7 2.2 %collective-permute-done.18.t2 = f32[72,256]{1,0:T(8,128)S(1)} collective-permute-done((f32[72,256]{1,0:T(8,128)S(1)}, f32[72,256]{1,0:T(8,128)S(1)}, u32[]{:S(2)}, u32[]{:S(2)}) %collective-permute-start.18) | collective-permute-done | bytes 73760 | tf_op jit(solution)/shard_map/ppermute | solution.py:224
  105.9 16.3 %all_to_all.16.tiles = f32[32,1,128]{2,1,0:T(1,128)S(1)} all-to-all(f32[32,1,128]{2,1,0:T(1,128)S(1)} %get-tuple-element.72), channel_id=1, replica_groups=mesh['row'=32,'col'=8] {'row'}, dimensions={0} | all-to-all | bytes 32768 | tf_op jit(solution)/shard_map/all_to_all | solution.py:262
  (39 shorter events, 11.1 us)
Async XLA Ops:
  29.9 12.0 %collective-permute-start.3 = (f32[8,64,256]{2,1,0:T(8,128)S(1)}, f32[8,64,256]{2,1,0:T(8,128)S(1)}, u32[]{:S(2)}, u32[]{:S(2)}) collective-permute-start(f32[8,64,256]{2,1,0:T(8,128)S(1)} %all_to_all.15.own.refs_0_), channel_id=1, source_target_pairs={{0,64},{8,72},{16,80},{24,88},{32,96},{40,104},{48,112},{56,120},{... | collective-permute-start | bytes 1572872 | tf_op jit(solution)/shard_map/ppermute | solution.py:46
  30.6 11.3 %collective-permute-start = (f32[8,64,256]{2,1,0:T(8,128)S(1)}, f32[8,64,256]{2,1,0:T(8,128)S(1)}, u32[]{:S(2)}, u32[]{:S(2)}) collective-permute-start(f32[8,64,256]{2,1,0:T(8,128)S(1)} %all_to_all.15.own.refs_0_), channel_id=1, source_target_pairs={{0,192},{8,200},{16,208},{24,216},{32,224},{40,232},{48,240},{56,2... | collective-permute-start | bytes 1572872 | tf_op jit(solution)/shard_map/ppermute | solution.py:45
  33.2 6.5 %collective-permute-start.1 = (f32[4,64,256]{2,1,0:T(8,128)S(1)}, f32[4,64,256]{2,1,0:T(8,128)S(1)}, u32[]{:S(2)}, u32[]{:S(2)}) collective-permute-start(f32[4,64,256]{2,1,0:T(8,128)S(1)} %get-tuple-element.39), channel_id=1, source_target_pairs={{0,56},{8,0},{16,8},{24,16},{32,24},{40,32},{48,40},{56,48},{64,12... | collective-permute-start | bytes 786440 | tf_op jit(solution)/shard_map/ppermute | solution.py:48
  34.2 7.6 %collective-permute-start.2 = (f32[4,64,256]{2,1,0:T(8,128)S(1)}, f32[4,64,256]{2,1,0:T(8,128)S(1)}, u32[]{:S(2)}, u32[]{:S(2)}) collective-permute-start(f32[4,64,256]{2,1,0:T(8,128)S(1)} %get-tuple-element.40), channel_id=1, source_target_pairs={{0,8},{8,16},{16,24},{24,32},{32,40},{40,48},{48,56},{56,0},{64,72... | collective-permute-start | bytes 786440 | tf_op jit(solution)/shard_map/ppermute | solution.py:49
  35.4 2.2 %copy-start = (f32[8,64,2048]{2,1,0:T(8,128)S(1)}, f32[8,64,2048]{2,1,0:T(8,128)}, u32[]{:S(2)}) copy-start(f32[8,64,2048]{2,1,0:T(8,128)} %param.5) | copy-start | bytes 12582916
  41.9 7.3 %copy-start.3 = (s32[64]{0:T(128)S(1)}, s32[64]{0:T(128)}, u32[]{:S(2)}) copy-start(s32[64]{0:T(128)} %param.7) | copy-start | bytes 772
  41.9 12.8 %copy-start.4 = (f32[64]{0:T(128)S(1)}, f32[64]{0:T(128)}, u32[]{:S(2)}) copy-start(f32[64]{0:T(128)} %param.8) | copy-start | bytes 772
  41.9 12.9 %copy-start.2 = (f32[256,256]{1,0:T(8,128)S(1)}, f32[256,256]{1,0:T(8,128)}, u32[]{:S(2)}) copy-start(f32[256,256]{1,0:T(8,128)} %kernel.3) | copy-start | bytes 786436
  44.6 1.6 %collective-permute-start.4 = (f32[4,64,256]{2,1,0:T(8,128)S(1)}, f32[4,64,256]{2,1,0:T(8,128)S(1)}, u32[]{:S(2)}, u32[]{:S(2)}) collective-permute-start(f32[4,64,256]{2,1,0:T(8,128)S(1)} %get-tuple-element.45), channel_id=1, source_target_pairs={{0,1},{1,0},{2,3},{3,2},{4,5},{5,4},{6,7},{7,6},{8,9},{9,8},{10,11... | collective-permute-start | bytes 786440 | tf_op jit(solution)/shard_map/ppermute | solution.py:222
  46.2 4.9 %collective-permute-start.5 = (f32[64,256]{1,0:T(8,128)S(1)}, f32[64,256]{1,0:T(8,128)S(1)}, u32[]{:S(2)}, u32[]{:S(2)}) collective-permute-start(f32[64,256]{1,0:T(8,128)S(1)} %get-tuple-element.47), channel_id=1, source_target_pairs={{0,2},{1,3},{2,4},{3,5},{4,6},{5,7},{6,0},{7,1},{8,10},{9,11},{10,... | collective-permute-start | bytes 196616 | tf_op jit(solution)/shard_map/ppermute | solution.py:224
  46.8 5.8 %collective-permute-start.6 = (f32[64,256]{1,0:T(8,128)S(1)}, f32[64,256]{1,0:T(8,128)S(1)}, u32[]{:S(2)}, u32[]{:S(2)}) collective-permute-start(f32[64,256]{1,0:T(8,128)S(1)} %get-tuple-element.48), channel_id=1, source_target_pairs={{0,4},{1,5},{2,6},{3,7},{4,0},{5,1},{6,2},{7,3},{8,12},{9,13},{10,... | collective-permute-start | bytes 196616 | tf_op jit(solution)/shard_map/ppermute | solution.py:224
  49.2 5.5 %collective-permute-start.7 = (f32[64,256]{1,0:T(8,128)S(1)}, f32[64,256]{1,0:T(8,128)S(1)}, u32[]{:S(2)}, u32[]{:S(2)}) collective-permute-start(f32[64,256]{1,0:T(8,128)S(1)} %get-tuple-element.49), channel_id=1, source_target_pairs={{0,6},{1,7},{2,0},{3,1},{4,2},{5,3},{6,4},{7,5},{8,14},{9,15},{10,... | collective-permute-start | bytes 196616 | tf_op jit(solution)/shard_map/ppermute | solution.py:224
  55.9 21.8 %all-to-all-start.1 = ((f32[8,64,256]{2,1,0:T(8,128)}), f32[8,64,256]{2,1,0:T(8,128)S(1)}, u32[]{:S(2)}, u32[]{:S(2)}) async-start(f32[8,64,256]{2,1,0:T(8,128)} %get-tuple-element.52), calls=%async_computation.1 | async-start | bytes 1048576 | tf_op jit(solution)/shard_map/all_to_all | solution.py:41
  62.2 1.3 %collective-permute-start.8 = (f32[64,256]{1,0:T(8,128)S(1)}, f32[64,256]{1,0:T(8,128)S(1)}, u32[]{:S(2)}, u32[]{:S(2)}) collective-permute-start(f32[64,256]{1,0:T(8,128)S(1)} %get-tuple-element.53.image), channel_id=1, source_target_pairs={{0,1},{1,0},{2,3},{3,2},{4,5},{5,4},{6,7},{7,6},{8,9},{9,8},{10,11... | collective-permute-start | bytes 196616 | tf_op jit(solution)/shard_map/ppermute | solution.py:228
  63.5 6.4 %collective-permute-start.11 = (f32[2,64,256]{2,1,0:T(8,128)S(1)}, f32[2,64,256]{2,1,0:T(8,128)S(1)}, u32[]{:S(2)}, u32[]{:S(2)}) collective-permute-start(f32[2,64,256]{2,1,0:T(8,128)S(1)} %shard_map.73.refs_7_), channel_id=1, source_target_pairs={{0,2},{1,3},{2,4},{3,5},{4,6},{5,7},{6,0},{7,1},{8,10},{9,11},{10,... | collective-permute-start | bytes 393224 | tf_op jit(solution)/shard_map/ppermute | solution.py:230
  64.2 7.9 %collective-permute-start.10 = (f32[2,64,256]{2,1,0:T(8,128)S(1)}, f32[2,64,256]{2,1,0:T(8,128)S(1)}, u32[]{:S(2)}, u32[]{:S(2)}) collective-permute-start(f32[2,64,256]{2,1,0:T(8,128)S(1)} %shard_map.73.refs_7_), channel_id=1, source_target_pairs={{0,4},{1,5},{2,6},{3,7},{4,0},{5,1},{6,2},{7,3},{8,12},{9,13},{10,... | collective-permute-start | bytes 393224 | tf_op jit(solution)/shard_map/ppermute | solution.py:230
  65.4 8.3 %collective-permute-start.9 = (f32[2,64,256]{2,1,0:T(8,128)S(1)}, f32[2,64,256]{2,1,0:T(8,128)S(1)}, u32[]{:S(2)}, u32[]{:S(2)}) collective-permute-start(f32[2,64,256]{2,1,0:T(8,128)S(1)} %shard_map.73.refs_7_), channel_id=1, source_target_pairs={{0,6},{1,7},{2,0},{3,1},{4,2},{5,3},{6,4},{7,5},{8,14},{9,15},{10,... | collective-permute-start | bytes 393224 | tf_op jit(solution)/shard_map/ppermute | solution.py:230
  77.7 15.2 %collective-permute-start.15 = (f32[8,64,256]{2,1,0:T(8,128)S(1)}, f32[8,64,256]{2,1,0:T(8,128)S(1)}, u32[]{:S(2)}, u32[]{:S(2)}) collective-permute-start(f32[8,64,256]{2,1,0:T(8,128)S(1)} %all-to-all-done.1.own.refs_0_), channel_id=1, source_target_pairs={{0,64},{8,72},{16,80},{24,88},{32,96},{40,104},{48,112},{56,120},{... | collective-permute-start | bytes 1572872 | tf_op jit(solution)/shard_map/ppermute | solution.py:46
  79.9 13.0 %collective-permute-start.12 = (f32[8,64,256]{2,1,0:T(8,128)S(1)}, f32[8,64,256]{2,1,0:T(8,128)S(1)}, u32[]{:S(2)}, u32[]{:S(2)}) collective-permute-start(f32[8,64,256]{2,1,0:T(8,128)S(1)} %all-to-all-done.1.own.refs_0_), channel_id=1, source_target_pairs={{0,192},{8,200},{16,208},{24,216},{32,224},{40,232},{48,240},{56,2... | collective-permute-start | bytes 1572872 | tf_op jit(solution)/shard_map/ppermute | solution.py:45
  81.0 8.0 %collective-permute-start.13 = (f32[4,64,256]{2,1,0:T(8,128)S(1)}, f32[4,64,256]{2,1,0:T(8,128)S(1)}, u32[]{:S(2)}, u32[]{:S(2)}) collective-permute-start(f32[4,64,256]{2,1,0:T(8,128)S(1)} %get-tuple-element.55), channel_id=1, source_target_pairs={{0,56},{8,0},{16,8},{24,16},{32,24},{40,32},{48,40},{56,48},{64,12... | collective-permute-start | bytes 786440 | tf_op jit(solution)/shard_map/ppermute | solution.py:48
  83.1 7.7 %collective-permute-start.14 = (f32[4,64,256]{2,1,0:T(8,128)S(1)}, f32[4,64,256]{2,1,0:T(8,128)S(1)}, u32[]{:S(2)}, u32[]{:S(2)}) collective-permute-start(f32[4,64,256]{2,1,0:T(8,128)S(1)} %get-tuple-element.56), channel_id=1, source_target_pairs={{0,8},{8,16},{16,24},{24,32},{32,40},{40,48},{48,56},{56,0},{64,72... | collective-permute-start | bytes 786440 | tf_op jit(solution)/shard_map/ppermute | solution.py:49
  84.7 2.2 %copy-start.1 = (f32[8,64,2048]{2,1,0:T(8,128)S(1)}, f32[8,64,2048]{2,1,0:T(8,128)}, u32[]{:S(2)}) copy-start(f32[8,64,2048]{2,1,0:T(8,128)} %param.5) | copy-start | bytes 12582916
  95.8 1.7 %collective-permute-start.16 = (f32[4,72,256]{2,1,0:T(8,128)S(1)}, f32[4,72,256]{2,1,0:T(8,128)S(1)}, u32[]{:S(2)}, u32[]{:S(2)}) collective-permute-start(f32[4,72,256]{2,1,0:T(8,128)S(1)} %get-tuple-element.66), channel_id=1, source_target_pairs={{0,1},{1,0},{2,3},{3,2},{4,5},{5,4},{6,7},{7,6},{8,9},{9,8},{10,11... | collective-permute-start | bytes 884744 | tf_op jit(solution)/shard_map/ppermute | solution.py:222
  97.5 5.2 %collective-permute-start.17 = (f32[72,256]{1,0:T(8,128)S(1)}, f32[72,256]{1,0:T(8,128)S(1)}, u32[]{:S(2)}, u32[]{:S(2)}) collective-permute-start(f32[72,256]{1,0:T(8,128)S(1)} %get-tuple-element.68), channel_id=1, source_target_pairs={{0,2},{1,3},{2,4},{3,5},{4,6},{5,7},{6,0},{7,1},{8,10},{9,11},{10,... | collective-permute-start | bytes 221192 | tf_op jit(solution)/shard_map/ppermute | solution.py:224
  98.6 6.3 %collective-permute-start.18 = (f32[72,256]{1,0:T(8,128)S(1)}, f32[72,256]{1,0:T(8,128)S(1)}, u32[]{:S(2)}, u32[]{:S(2)}) collective-permute-start(f32[72,256]{1,0:T(8,128)S(1)} %get-tuple-element.69), channel_id=1, source_target_pairs={{0,4},{1,5},{2,6},{3,7},{4,0},{5,1},{6,2},{7,3},{8,12},{9,13},{10,... | collective-permute-start | bytes 221192 | tf_op jit(solution)/shard_map/ppermute | solution.py:224
  99.8 5.9 %collective-permute-start.19 = (f32[72,256]{1,0:T(8,128)S(1)}, f32[72,256]{1,0:T(8,128)S(1)}, u32[]{:S(2)}, u32[]{:S(2)}) collective-permute-start(f32[72,256]{1,0:T(8,128)S(1)} %get-tuple-element.70), channel_id=1, source_target_pairs={{0,6},{1,7},{2,0},{3,1},{4,2},{5,3},{6,4},{7,5},{8,14},{9,15},{10,... | collective-permute-start | bytes 221192 | tf_op jit(solution)/shard_map/ppermute | solution.py:224

commit v4 on v3

--- a/solution.py
+++ b/solution.py
@@ -14,20 +14,25 @@
 BF16 = jnp.bfloat16
 
 
-def class_member(k, j):
-    kh, kl, jh, jl = k // 2, k % 2, j // 4, j % 4
-    return (kl + 2 * jh) * NZ + 2 * jl + (kh + jh) % 2
-
-
-CLASSES = [[class_member(k, j) for j in range(8)] for k in range(4)]
-
-
-def shift_y(d):
-    return [(y * NZ + z, ((y + d) % NY) * NZ + z) for y in range(NY) for z in range(NZ)]
-
-
-def shift_z(d):
-    return [(y * NZ + z, y * NZ + (z + d) % NZ) for y in range(NY) for z in range(NZ)]
+def class_member(core, k, j):
+    if core == 0:
+        return (k + 2 * j) % 4 * NZ + j
+    return j // 2 * NZ + (k + 2 * (j // 2)) % 4 + 4 * (j % 2)
+
+
+CLASSES = [
+    [class_member(col % 2, k, j) * 8 + col for j in range(8)] for col in range(8) for k in range(4)
+]
+
+
+def shift(major, minor):
+    pairs = []
+    for row in range(NY * NZ):
+        for col in range(8):
+            dy, dz = (major, minor) if col % 2 == 0 else (minor, major)
+            target = (row // NZ + dy) % NY * NZ + (row % NZ + dz) % NZ
+            pairs.append((row * 8 + col, target * 8 + col))
+    return pairs
 
 
 def shift_x(d):
@@ -37,26 +42,32 @@
 SIBLING = [(c, c ^ 1) for c in range(8)]
 
 
+BOTH = ("row", "col")
+
+
 def gather_class(copies):
-    return lax.all_to_all(copies, "row", 0, 0, axis_index_groups=CLASSES)
+    return lax.all_to_all(copies, BOTH, 0, 0, axis_index_groups=CLASSES)
 
 
 def gather_rest(own):
-    next_y = lax.ppermute(own, "row", shift_y(-1))
-    last_y = lax.ppermute(own, "row", shift_y(1))
+    above = lax.ppermute(own, BOTH, shift(-1, 0))
+    below = lax.ppermute(own, BOTH, shift(1, 0))
     lower, upper = small_call(halves_kernel, [(4, BLOCK, EPOCHS)] * 2, own)
-    next_z = lax.ppermute(lower, "row", shift_z(-1))
-    last_z = lax.ppermute(upper, "row", shift_z(1))
-    return own, next_y, next_z, last_z, last_y
-
-
-def put_parts(colour, parts, high, low):
+    right = lax.ppermute(lower, BOTH, shift(0, -1))
+    left = lax.ppermute(upper, BOTH, shift(0, 1))
+    return own, above, right, left, below
+
+
+def put_parts(colour, first_core, parts, high, low):
     for ref, slot, first in zip(parts, (0, 1, 2, 2, 3), (0, 0, 0, 4, 0)):
         k = lax.rem(colour + slot, 4)
-        kh, kl = k // 2, lax.rem(k, 2)
         for j in range(ref.shape[0]):
-            jh, jl = (j + first) // 4, (j + first) % 4
-            row = (kl + 2 * jh) * NZ + 2 * jl + lax.rem(kh + jh, 2)
+            m = j + first
+            row = jnp.where(
+                first_core,
+                lax.rem(k + 2 * m, 4) * NZ + m,
+                m // 2 * NZ + lax.rem(k + 2 * (m // 2), 4) + 4 * (m % 2),
+            )
             at = pl.ds(pl.multiple_of(row * BLOCK, BLOCK), BLOCK)
             value = ref[j]
             top = value.astype(BF16)
@@ -69,8 +80,8 @@
     if with_sums:
         images, sums, refs = refs[:4], refs[4], refs[5:]
     keep, send, high, low = refs
-    put_parts(place[0], parts, high, low)
     x, even_core = place[1], place[2] == 0
+    put_parts(place[0], even_core, parts, high, low)
     value = jnp.dot(k_high[...], high[...], preferred_element_type=F32)
     value += jnp.dot(k_low[...], high[...], preferred_element_type=F32)
     value += jnp.dot(k_high[...], low[...], preferred_element_type=F32)
@@ -238,8 +249,9 @@
         return (epoch_index < lengths[:, None]).astype(F32)
 
     row, col = lax.axis_index("row"), lax.axis_index("col")
-    colour = lax.rem(row // NZ + 2 * lax.rem(row, NZ), 4)
-    place = jnp.stack([colour, col // 2, lax.rem(col, 2)]).astype(jnp.int32)
+    y, z, core = row // NZ, lax.rem(row, NZ), lax.rem(col, 2)
+    colour = lax.rem(jnp.where(core == 0, y + 2 * z, z + 2 * y), 4)
+    place = jnp.stack([colour, col // 2, core]).astype(jnp.int32)
     tile = kernel_configs.reshape(-1, kernel_configs.shape[2])
 
     r0 = curves * mask_of(lengths)

time: 124 us -> 121 us (0.976)
  waiting for transfers between devices: 36.7 us -> 35.3 us
    all_to_all x1, starting transfers between devices: 6.27 us -> 3.49 us  [gather_class(): return lax.all_to_all(copies, BOTH, 0, 0, axis_index_groups=CLASSES)]
    ppermute x6, starting transfers between devices: 5.22 us -> 7.83 us  [scatter_col(): lax.ppermute(total[d], 'col', shift_x(d))]
    all_to_all x1, blocking collectives: 16.3 us -> 14.5 us  [per_device(): tiles = lax.all_to_all(copies, 'row', 0, 0)]
where the time goes in v4:
time: 121 us; the launch traced here: 120 us
  blocking collectives  43.9 us (36%)
  waiting for transfers between devices  35.3 us (29%)
  starting transfers between devices  25.6 us (21%)
  Pallas kernels  9.38 us (8%)
  local copies, waits for them, and re-layouts  4.5 us (4%)
    all_to_all x1, blocking collectives, gather_class(): return lax.all_to_all(copies, BOTH, 0, 0, axis_index_groups=CLASSES)  29.5 us
    all_to_all x1, blocking collectives, per_device(): tiles = lax.all_to_all(copies, 'row', 0, 0)  14.5 us
    ppermute x6, waiting for transfers between devices, scatter_col(): lax.ppermute(total[d], 'col', shift_x(d))  11 us
    ppermute x3, waiting for transfers between devices, gather_col(): lax.ppermute(pair, 'col', shift_x(-d))  8.14 us
    ppermute x6, starting transfers between devices, scatter_col(): lax.ppermute(total[d], 'col', shift_x(d))  7.83 us
    ppermute x2, starting transfers between devices, gather_rest(): above = lax.ppermute(own, BOTH, shift(-1, 0))  6.05 us
    pallas_call x2, Pallas kernels, product(): pl.pallas_call(functools.partial(product_kernel, bool(extra)), out_shape=...  5.54 us
    unnamed x10, local copies, waits for them, and re-layouts  4.39 us
  transfers between devices with their start and end apart: 21, of which 19 were waited for; matrix products, arithmetic and copies ran while one was open for 0% of the time, Pallas kernels for 1%

profile of v4, /device:TPU:6, one launch (start us, length us, event | category | flops | bytes accessed | tf_op | source)
XLA Modules:
  0.0 120.5 jit_solution(1324865037365194569)
XLA Ops:
  1.6 29.5 %all_to_all.15.own.refs_0_ = f32[8,64,256]{2,1,0:T(8,128)S(1)} all-to-all(f32[8,64,256]{2,1,0:T(8,128)S(1)} %broadcast_in_dim.4), channel_id=1, replica_groups={{0,136,16,152,32,168,48,184},{64,200,80,216,96,232,112,248},{128,8,144,..., dimensions={0} | all-to-all | bytes 1048576 | tf_op jit(solution)/shard_map/all_to_all | solution.py:49
  31.1 3.2 %collective-permute-start = (f32[8,64,256]{2,1,0:T(8,128)S(1)}, f32[8,64,256]{2,1,0:T(8,128)S(1)}, u32[]{:S(2)}, u32[]{:S(2)}) collective-permute-start(f32[8,64,256]{2,1,0:T(8,128)S(1)} %all_to_all.15.own.refs_0_), channel_id=1, source_target_pairs={{0,192},{1,57},{2,194},{3,59},{4,196},{5,61},{6,198},{7,63},{8,200... | collective-permute-start | bytes 1572872 | tf_op jit(solution)/shard_map/ppermute | solution.py:53
  34.4 2.0 %collective-permute-start.2 = (f32[4,64,256]{2,1,0:T(8,128)S(1)}, f32[4,64,256]{2,1,0:T(8,128)S(1)}, u32[]{:S(2)}, u32[]{:S(2)}) collective-permute-start(f32[4,64,256]{2,1,0:T(8,128)S(1)} %get-tuple-element.40), channel_id=1, source_target_pairs={{0,8},{1,65},{2,10},{3,67},{4,12},{5,69},{6,14},{7,71},{8,16},{9,7... | collective-permute-start | bytes 786440 | tf_op jit(solution)/shard_map/ppermute | solution.py:57
  36.5 2.2 %copy-done = f32[8,64,2048]{2,1,0:T(8,128)S(1)} copy-done((f32[8,64,2048]{2,1,0:T(8,128)S(1)}, f32[8,64,2048]{2,1,0:T(8,128)}, u32[]{:S(2)}) %copy-start) | copy-done | bytes 4194328
  39.4 1.6 %collective-permute-done.1.refs_2_ = f32[4,64,256]{2,1,0:T(8,128)S(1)} collective-permute-done((f32[4,64,256]{2,1,0:T(8,128)S(1)}, f32[4,64,256]{2,1,0:T(8,128)S(1)}, u32[]{:S(2)}, u32[]{:S(2)}) %collective-permute-start.1) | collective-permute-done | bytes 262176 | tf_op jit(solution)/shard_map/ppermute | solution.py:56
  41.0 1.1 collective-permute-done.2.refs_3_
  42.1 2.2 %collective-permute-done.3.refs_4_ = f32[8,64,256]{2,1,0:T(8,128)S(1)} collective-permute-done((f32[8,64,256]{2,1,0:T(8,128)S(1)}, f32[8,64,256]{2,1,0:T(8,128)S(1)}, u32[]{:S(2)}, u32[]{:S(2)}) %collective-permute-start.3) | collective-permute-done | bytes 524320 | tf_op jit(solution)/shard_map/ppermute | solution.py:54
  44.3 2.7 %shard_map.70 = (f32[4,64,256]{2,1,0:T(8,128)S(1)}, f32[4,64,256]{2,1,0:T(8,128)S(1)}) custom-call(s32[3]{0:T(128)S(1)} %pad_add_fusion.place, f32[8,64,256]{2,1,0:T(8,128)S(1)} %all_to_all.15.own.refs_0_, f32[8,64,256]{2,1,0:T(8,128)S(1)} %collective-permute-done.refs_1_, f32[4,64,256]{2,1,0:T(8,128)S(1)} %collective-permute-done.1.refs_2_, ...), custom_call_target="tpu_custom_call" | custom-call | flops 1610612736 | bytes 7340032 | tf_op jit(solution)/shard_map/pallas_call | solution.py:130
  47.1 1.5 %collective-permute-done.4.other = f32[4,64,256]{2,1,0:T(8,128)S(1)} collective-permute-done((f32[4,64,256]{2,1,0:T(8,128)S(1)}, f32[4,64,256]{2,1,0:T(8,128)S(1)}, u32[]{:S(2)}, u32[]{:S(2)}) %collective-permute-start.4) | collective-permute-done | bytes 262176 | tf_op jit(solution)/shard_map/ppermute | solution.py:233
  49.2 2.4 %collective-permute-start.6 = (f32[64,256]{1,0:T(8,128)S(1)}, f32[64,256]{1,0:T(8,128)S(1)}, u32[]{:S(2)}, u32[]{:S(2)}) collective-permute-start(f32[64,256]{1,0:T(8,128)S(1)} %get-tuple-element.48), channel_id=1, source_target_pairs={{0,4},{1,5},{2,6},{3,7},{4,0},{5,1},{6,2},{7,3},{8,12},{9,13},{10,... | collective-permute-start | bytes 196616 | tf_op jit(solution)/shard_map/ppermute | solution.py:235
  51.7 1.9 %collective-permute-done.5.t1 = f32[64,256]{1,0:T(8,128)S(1)} collective-permute-done((f32[64,256]{1,0:T(8,128)S(1)}, f32[64,256]{1,0:T(8,128)S(1)}, u32[]{:S(2)}, u32[]{:S(2)}) %collective-permute-start.5) | collective-permute-done | bytes 65568 | tf_op jit(solution)/shard_map/ppermute | solution.py:235
  53.5 1.4 %collective-permute-done.6.t2 = f32[64,256]{1,0:T(8,128)S(1)} collective-permute-done((f32[64,256]{1,0:T(8,128)S(1)}, f32[64,256]{1,0:T(8,128)S(1)}, u32[]{:S(2)}, u32[]{:S(2)}) %collective-permute-start.6) | collective-permute-done | bytes 65568 | tf_op jit(solution)/shard_map/ppermute | solution.py:235
  55.0 2.1 %collective-permute-done.7.t3 = f32[64,256]{1,0:T(8,128)S(1)} collective-permute-done((f32[64,256]{1,0:T(8,128)S(1)}, f32[64,256]{1,0:T(8,128)S(1)}, u32[]{:S(2)}, u32[]{:S(2)}) %collective-permute-start.7) | collective-permute-done | bytes 65568 | tf_op jit(solution)/shard_map/ppermute | solution.py:235
  57.1 1.2 shard_map.72
  58.3 3.5 %all-to-all-start.1 = ((f32[8,64,256]{2,1,0:T(8,128)}), f32[8,64,256]{2,1,0:T(8,128)S(1)}, u32[]{:S(2)}, u32[]{:S(2)}) async-start(f32[8,64,256]{2,1,0:T(8,128)} %get-tuple-element.52), calls=%async_computation.1 | async-start | bytes 1048576 | tf_op jit(solution)/shard_map/all_to_all | solution.py:49
  61.9 1.2 %collective-permute-done.8.other = f32[64,256]{1,0:T(8,128)S(1)} collective-permute-done((f32[64,256]{1,0:T(8,128)S(1)}, f32[64,256]{1,0:T(8,128)S(1)}, u32[]{:S(2)}, u32[]{:S(2)}) %collective-permute-start.8) | collective-permute-done | bytes 65568 | tf_op jit(solution)/shard_map/ppermute | solution.py:239
  63.9 1.3 %collective-permute-start.10 = (f32[2,64,256]{2,1,0:T(8,128)S(1)}, f32[2,64,256]{2,1,0:T(8,128)S(1)}, u32[]{:S(2)}, u32[]{:S(2)}) collective-permute-start(f32[2,64,256]{2,1,0:T(8,128)S(1)} %shard_map.73.refs_7_), channel_id=1, source_target_pairs={{0,4},{1,5},{2,6},{3,7},{4,0},{5,1},{6,2},{7,3},{8,12},{9,13},{10,... | collective-permute-start | bytes 393224 | tf_op jit(solution)/shard_map/ppermute | solution.py:241
  65.3 4.3 %collective-permute-done.11.refs_10_ = f32[2,64,256]{2,1,0:T(8,128)S(1)} collective-permute-done((f32[2,64,256]{2,1,0:T(8,128)S(1)}, f32[2,64,256]{2,1,0:T(8,128)S(1)}, u32[]{:S(2)}, u32[]{:S(2)}) %collective-permute-start.11) | collective-permute-done | bytes 131104 | tf_op jit(solution)/shard_map/ppermute | solution.py:241
  69.6 2.1 %collective-permute-done.10.refs_9_ = f32[2,64,256]{2,1,0:T(8,128)S(1)} collective-permute-done((f32[2,64,256]{2,1,0:T(8,128)S(1)}, f32[2,64,256]{2,1,0:T(8,128)S(1)}, u32[]{:S(2)}, u32[]{:S(2)}) %collective-permute-start.10) | collective-permute-done | bytes 131104 | tf_op jit(solution)/shard_map/ppermute | solution.py:241
  71.7 1.7 %collective-permute-done.9.refs_8_ = f32[2,64,256]{2,1,0:T(8,128)S(1)} collective-permute-done((f32[2,64,256]{2,1,0:T(8,128)S(1)}, f32[2,64,256]{2,1,0:T(8,128)S(1)}, u32[]{:S(2)}, u32[]{:S(2)}) %collective-permute-start.9) | collective-permute-done | bytes 131104 | tf_op jit(solution)/shard_map/ppermute | solution.py:241
  73.5 3.7 %all-to-all-done.1.own.refs_0_ = f32[8,64,256]{2,1,0:T(8,128)S(1)} async-done(((f32[8,64,256]{2,1,0:T(8,128)}), f32[8,64,256]{2,1,0:T(8,128)S(1)}, u32[]{:S(2)}, u32[]{:S(2)}) %all-to-all-start.1) | async-done | bytes 524320 | tf_op jit(solution)/shard_map/all_to_all | solution.py:49
  77.6 2.8 %collective-permute-start.12 = (f32[8,64,256]{2,1,0:T(8,128)S(1)}, f32[8,64,256]{2,1,0:T(8,128)S(1)}, u32[]{:S(2)}, u32[]{:S(2)}) collective-permute-start(f32[8,64,256]{2,1,0:T(8,128)S(1)} %all-to-all-done.1.own.refs_0_), channel_id=1, source_target_pairs={{0,192},{1,57},{2,194},{3,59},{4,196},{5,61},{6,198},{7,63},{8,200... | collective-permute-start | bytes 1572872 | tf_op jit(solution)/shard_map/ppermute | solution.py:53
  81.4 2.0 %collective-permute-start.14 = (f32[4,64,256]{2,1,0:T(8,128)S(1)}, f32[4,64,256]{2,1,0:T(8,128)S(1)}, u32[]{:S(2)}, u32[]{:S(2)}) collective-permute-start(f32[4,64,256]{2,1,0:T(8,128)S(1)} %get-tuple-element.56), channel_id=1, source_target_pairs={{0,8},{1,65},{2,10},{3,67},{4,12},{5,69},{6,14},{7,71},{8,16},{9,7... | collective-permute-start | bytes 786440 | tf_op jit(solution)/shard_map/ppermute | solution.py:57
  83.4 2.2 %copy-done.1 = f32[8,64,2048]{2,1,0:T(8,128)S(1)} copy-done((f32[8,64,2048]{2,1,0:T(8,128)S(1)}, f32[8,64,2048]{2,1,0:T(8,128)}, u32[]{:S(2)}) %copy-start.1) | copy-done | bytes 4194328
  86.3 2.0 %collective-permute-done.13.refs_2_ = f32[4,64,256]{2,1,0:T(8,128)S(1)} collective-permute-done((f32[4,64,256]{2,1,0:T(8,128)S(1)}, f32[4,64,256]{2,1,0:T(8,128)S(1)}, u32[]{:S(2)}, u32[]{:S(2)}) %collective-permute-start.13) | collective-permute-done | bytes 262176 | tf_op jit(solution)/shard_map/ppermute | solution.py:56
  88.3 1.2 %collective-permute-done.14.refs_3_ = f32[4,64,256]{2,1,0:T(8,128)S(1)} collective-permute-done((f32[4,64,256]{2,1,0:T(8,128)S(1)}, f32[4,64,256]{2,1,0:T(8,128)S(1)}, u32[]{:S(2)}, u32[]{:S(2)}) %collective-permute-start.14) | collective-permute-done | bytes 262176 | tf_op jit(solution)/shard_map/ppermute | solution.py:57
  89.9 2.9 %shard_map.76 = (f32[4,72,256]{2,1,0:T(8,128)S(1)}, f32[4,72,256]{2,1,0:T(8,128)S(1)}) custom-call(s32[3]{0:T(128)S(1)} %pad_add_fusion.place, f32[8,64,256]{2,1,0:T(8,128)S(1)} %all-to-all-done.1.own.refs_0_, f32[8,64,256]{2,1,0:T(8,128)S(1)} %collective-permute-done.12.refs_1_, f32[4,64,256]{2,1,0:T(8,128)S(1)} %collective-permute-done.13.refs_2_, ...), custom_call_target="tpu_custom_call" | custom-call | flops 1610612736 | bytes 7340032 | tf_op jit(solution)/shard_map/pallas_call | solution.py:130
  93.2 1.3 %collective-permute-done.16.other = f32[4,72,256]{2,1,0:T(8,128)S(1)} collective-permute-done((f32[4,72,256]{2,1,0:T(8,128)S(1)}, f32[4,72,256]{2,1,0:T(8,128)S(1)}, u32[]{:S(2)}, u32[]{:S(2)}) %collective-permute-start.16) | collective-permute-done | bytes 294944 | tf_op jit(solution)/shard_map/ppermute | solution.py:233
  95.5 3.9 %collective-permute-start.18 = (f32[72,256]{1,0:T(8,128)S(1)}, f32[72,256]{1,0:T(8,128)S(1)}, u32[]{:S(2)}, u32[]{:S(2)}) collective-permute-start(f32[72,256]{1,0:T(8,128)S(1)} %get-tuple-element.69), channel_id=1, source_target_pairs={{0,4},{1,5},{2,6},{3,7},{4,0},{5,1},{6,2},{7,3},{8,12},{9,13},{10,... | collective-permute-start | bytes 221192 | tf_op jit(solution)/shard_map/ppermute | solution.py:235
  100.3 1.4 %collective-permute-done.18.t2 = f32[72,256]{1,0:T(8,128)S(1)} collective-permute-done((f32[72,256]{1,0:T(8,128)S(1)}, f32[72,256]{1,0:T(8,128)S(1)}, u32[]{:S(2)}, u32[]{:S(2)}) %collective-permute-start.18) | collective-permute-done | bytes 73760 | tf_op jit(solution)/shard_map/ppermute | solution.py:235
  101.7 3.2 %collective-permute-done.19.t3 = f32[72,256]{1,0:T(8,128)S(1)} collective-permute-done((f32[72,256]{1,0:T(8,128)S(1)}, f32[72,256]{1,0:T(8,128)S(1)}, u32[]{:S(2)}, u32[]{:S(2)}) %collective-permute-start.19) | collective-permute-done | bytes 73760 | tf_op jit(solution)/shard_map/ppermute | solution.py:235
  105.2 14.5 %all_to_all.16.tiles = f32[32,1,128]{2,1,0:T(1,128)S(1)} all-to-all(f32[32,1,128]{2,1,0:T(1,128)S(1)} %get-tuple-element.72), channel_id=1, replica_groups=mesh['row'=32,'col'=8] {'row'}, dimensions={0} | all-to-all | bytes 32768 | tf_op jit(solution)/shard_map/all_to_all | solution.py:274
  (39 shorter events, 9.6 us)
Async XLA Ops:
  31.1 13.2 %collective-permute-start.3 = (f32[8,64,256]{2,1,0:T(8,128)S(1)}, f32[8,64,256]{2,1,0:T(8,128)S(1)}, u32[]{:S(2)}, u32[]{:S(2)}) collective-permute-start(f32[8,64,256]{2,1,0:T(8,128)S(1)} %all_to_all.15.own.refs_0_), channel_id=1, source_target_pairs={{0,64},{1,9},{2,66},{3,11},{4,68},{5,13},{6,70},{7,15},{8,72},{9,1... | collective-permute-start | bytes 1572872 | tf_op jit(solution)/shard_map/ppermute | solution.py:54
  31.1 13.2 %collective-permute-start = (f32[8,64,256]{2,1,0:T(8,128)S(1)}, f32[8,64,256]{2,1,0:T(8,128)S(1)}, u32[]{:S(2)}, u32[]{:S(2)}) collective-permute-start(f32[8,64,256]{2,1,0:T(8,128)S(1)} %all_to_all.15.own.refs_0_), channel_id=1, source_target_pairs={{0,192},{1,57},{2,194},{3,59},{4,196},{5,61},{6,198},{7,63},{8,200... | collective-permute-start | bytes 1572872 | tf_op jit(solution)/shard_map/ppermute | solution.py:53
  34.3 6.6 %collective-permute-start.1 = (f32[4,64,256]{2,1,0:T(8,128)S(1)}, f32[4,64,256]{2,1,0:T(8,128)S(1)}, u32[]{:S(2)}, u32[]{:S(2)}) collective-permute-start(f32[4,64,256]{2,1,0:T(8,128)S(1)} %get-tuple-element.39), channel_id=1, source_target_pairs={{0,56},{1,193},{2,58},{3,195},{4,60},{5,197},{6,62},{7,199},{8,0},... | collective-permute-start | bytes 786440 | tf_op jit(solution)/shard_map/ppermute | solution.py:56
  34.4 7.7 %collective-permute-start.2 = (f32[4,64,256]{2,1,0:T(8,128)S(1)}, f32[4,64,256]{2,1,0:T(8,128)S(1)}, u32[]{:S(2)}, u32[]{:S(2)}) collective-permute-start(f32[4,64,256]{2,1,0:T(8,128)S(1)} %get-tuple-element.40), channel_id=1, source_target_pairs={{0,8},{1,65},{2,10},{3,67},{4,12},{5,69},{6,14},{7,71},{8,16},{9,7... | collective-permute-start | bytes 786440 | tf_op jit(solution)/shard_map/ppermute | solution.py:57
  36.5 2.2 %copy-start = (f32[8,64,2048]{2,1,0:T(8,128)S(1)}, f32[8,64,2048]{2,1,0:T(8,128)}, u32[]{:S(2)}) copy-start(f32[8,64,2048]{2,1,0:T(8,128)} %param.5) | copy-start | bytes 12582916
  44.3 7.3 %copy-start.3 = (s32[64]{0:T(128)S(1)}, s32[64]{0:T(128)}, u32[]{:S(2)}) copy-start(s32[64]{0:T(128)} %param.7) | copy-start | bytes 772
  44.3 12.8 %copy-start.4 = (f32[64]{0:T(128)S(1)}, f32[64]{0:T(128)}, u32[]{:S(2)}) copy-start(f32[64]{0:T(128)} %param.8) | copy-start | bytes 772
  44.3 12.9 %copy-start.2 = (f32[256,256]{1,0:T(8,128)S(1)}, f32[256,256]{1,0:T(8,128)}, u32[]{:S(2)}) copy-start(f32[256,256]{1,0:T(8,128)} %kernel.3) | copy-start | bytes 786436
  47.0 1.6 %collective-permute-start.4 = (f32[4,64,256]{2,1,0:T(8,128)S(1)}, f32[4,64,256]{2,1,0:T(8,128)S(1)}, u32[]{:S(2)}, u32[]{:S(2)}) collective-permute-start(f32[4,64,256]{2,1,0:T(8,128)S(1)} %get-tuple-element.45), channel_id=1, source_target_pairs={{0,1},{1,0},{2,3},{3,2},{4,5},{5,4},{6,7},{7,6},{8,9},{9,8},{10,11... | collective-permute-start | bytes 786440 | tf_op jit(solution)/shard_map/ppermute | solution.py:233
  48.6 4.9 %collective-permute-start.5 = (f32[64,256]{1,0:T(8,128)S(1)}, f32[64,256]{1,0:T(8,128)S(1)}, u32[]{:S(2)}, u32[]{:S(2)}) collective-permute-start(f32[64,256]{1,0:T(8,128)S(1)} %get-tuple-element.47), channel_id=1, source_target_pairs={{0,2},{1,3},{2,4},{3,5},{4,6},{5,7},{6,0},{7,1},{8,10},{9,11},{10,... | collective-permute-start | bytes 196616 | tf_op jit(solution)/shard_map/ppermute | solution.py:235
  49.2 5.8 %collective-permute-start.6 = (f32[64,256]{1,0:T(8,128)S(1)}, f32[64,256]{1,0:T(8,128)S(1)}, u32[]{:S(2)}, u32[]{:S(2)}) collective-permute-start(f32[64,256]{1,0:T(8,128)S(1)} %get-tuple-element.48), channel_id=1, source_target_pairs={{0,4},{1,5},{2,6},{3,7},{4,0},{5,1},{6,2},{7,3},{8,12},{9,13},{10,... | collective-permute-start | bytes 196616 | tf_op jit(solution)/shard_map/ppermute | solution.py:235
  51.6 5.5 %collective-permute-start.7 = (f32[64,256]{1,0:T(8,128)S(1)}, f32[64,256]{1,0:T(8,128)S(1)}, u32[]{:S(2)}, u32[]{:S(2)}) collective-permute-start(f32[64,256]{1,0:T(8,128)S(1)} %get-tuple-element.49), channel_id=1, source_target_pairs={{0,6},{1,7},{2,0},{3,1},{4,2},{5,3},{6,4},{7,5},{8,14},{9,15},{10,... | collective-permute-start | bytes 196616 | tf_op jit(solution)/shard_map/ppermute | solution.py:235
  58.3 18.8 %all-to-all-start.1 = ((f32[8,64,256]{2,1,0:T(8,128)}), f32[8,64,256]{2,1,0:T(8,128)S(1)}, u32[]{:S(2)}, u32[]{:S(2)}) async-start(f32[8,64,256]{2,1,0:T(8,128)} %get-tuple-element.52), calls=%async_computation.1 | async-start | bytes 1048576 | tf_op jit(solution)/shard_map/all_to_all | solution.py:49
  61.8 1.3 %collective-permute-start.8 = (f32[64,256]{1,0:T(8,128)S(1)}, f32[64,256]{1,0:T(8,128)S(1)}, u32[]{:S(2)}, u32[]{:S(2)}) collective-permute-start(f32[64,256]{1,0:T(8,128)S(1)} %get-tuple-element.53.image), channel_id=1, source_target_pairs={{0,1},{1,0},{2,3},{3,2},{4,5},{5,4},{6,7},{7,6},{8,9},{9,8},{10,11... | collective-permute-start | bytes 196616 | tf_op jit(solution)/shard_map/ppermute | solution.py:239
  63.2 6.4 %collective-permute-start.11 = (f32[2,64,256]{2,1,0:T(8,128)S(1)}, f32[2,64,256]{2,1,0:T(8,128)S(1)}, u32[]{:S(2)}, u32[]{:S(2)}) collective-permute-start(f32[2,64,256]{2,1,0:T(8,128)S(1)} %shard_map.73.refs_7_), channel_id=1, source_target_pairs={{0,2},{1,3},{2,4},{3,5},{4,6},{5,7},{6,0},{7,1},{8,10},{9,11},{10,... | collective-permute-start | bytes 393224 | tf_op jit(solution)/shard_map/ppermute | solution.py:241
  63.9 7.9 %collective-permute-start.10 = (f32[2,64,256]{2,1,0:T(8,128)S(1)}, f32[2,64,256]{2,1,0:T(8,128)S(1)}, u32[]{:S(2)}, u32[]{:S(2)}) collective-permute-start(f32[2,64,256]{2,1,0:T(8,128)S(1)} %shard_map.73.refs_7_), channel_id=1, source_target_pairs={{0,4},{1,5},{2,6},{3,7},{4,0},{5,1},{6,2},{7,3},{8,12},{9,13},{10,... | collective-permute-start | bytes 393224 | tf_op jit(solution)/shard_map/ppermute | solution.py:241
  65.1 8.3 %collective-permute-start.9 = (f32[2,64,256]{2,1,0:T(8,128)S(1)}, f32[2,64,256]{2,1,0:T(8,128)S(1)}, u32[]{:S(2)}, u32[]{:S(2)}) collective-permute-start(f32[2,64,256]{2,1,0:T(8,128)S(1)} %shard_map.73.refs_7_), channel_id=1, source_target_pairs={{0,6},{1,7},{2,0},{3,1},{4,2},{5,3},{6,4},{7,5},{8,14},{9,15},{10,... | collective-permute-start | bytes 393224 | tf_op jit(solution)/shard_map/ppermute | solution.py:241
  77.2 12.3 %collective-permute-start.15 = (f32[8,64,256]{2,1,0:T(8,128)S(1)}, f32[8,64,256]{2,1,0:T(8,128)S(1)}, u32[]{:S(2)}, u32[]{:S(2)}) collective-permute-start(f32[8,64,256]{2,1,0:T(8,128)S(1)} %all-to-all-done.1.own.refs_0_), channel_id=1, source_target_pairs={{0,64},{1,9},{2,66},{3,11},{4,68},{5,13},{6,70},{7,15},{8,72},{9,1... | collective-permute-start | bytes 1572872 | tf_op jit(solution)/shard_map/ppermute | solution.py:54
  77.6 12.3 %collective-permute-start.12 = (f32[8,64,256]{2,1,0:T(8,128)S(1)}, f32[8,64,256]{2,1,0:T(8,128)S(1)}, u32[]{:S(2)}, u32[]{:S(2)}) collective-permute-start(f32[8,64,256]{2,1,0:T(8,128)S(1)} %all-to-all-done.1.own.refs_0_), channel_id=1, source_target_pairs={{0,192},{1,57},{2,194},{3,59},{4,196},{5,61},{6,198},{7,63},{8,200... | collective-permute-start | bytes 1572872 | tf_op jit(solution)/shard_map/ppermute | solution.py:53
  80.5 7.9 %collective-permute-start.13 = (f32[4,64,256]{2,1,0:T(8,128)S(1)}, f32[4,64,256]{2,1,0:T(8,128)S(1)}, u32[]{:S(2)}, u32[]{:S(2)}) collective-permute-start(f32[4,64,256]{2,1,0:T(8,128)S(1)} %get-tuple-element.55), channel_id=1, source_target_pairs={{0,56},{1,193},{2,58},{3,195},{4,60},{5,197},{6,62},{7,199},{8,0},... | collective-permute-start | bytes 786440 | tf_op jit(solution)/shard_map/ppermute | solution.py:56
  81.4 8.1 %collective-permute-start.14 = (f32[4,64,256]{2,1,0:T(8,128)S(1)}, f32[4,64,256]{2,1,0:T(8,128)S(1)}, u32[]{:S(2)}, u32[]{:S(2)}) collective-permute-start(f32[4,64,256]{2,1,0:T(8,128)S(1)} %get-tuple-element.56), channel_id=1, source_target_pairs={{0,8},{1,65},{2,10},{3,67},{4,12},{5,69},{6,14},{7,71},{8,16},{9,7... | collective-permute-start | bytes 786440 | tf_op jit(solution)/shard_map/ppermute | solution.py:57
  83.4 2.2 %copy-start.1 = (f32[8,64,2048]{2,1,0:T(8,128)S(1)}, f32[8,64,2048]{2,1,0:T(8,128)}, u32[]{:S(2)}) copy-start(f32[8,64,2048]{2,1,0:T(8,128)} %param.5) | copy-start | bytes 12582916
  92.8 1.7 %collective-permute-start.16 = (f32[4,72,256]{2,1,0:T(8,128)S(1)}, f32[4,72,256]{2,1,0:T(8,128)S(1)}, u32[]{:S(2)}, u32[]{:S(2)}) collective-permute-start(f32[4,72,256]{2,1,0:T(8,128)S(1)} %get-tuple-element.66), channel_id=1, source_target_pairs={{0,1},{1,0},{2,3},{3,2},{4,5},{5,4},{6,7},{7,6},{8,9},{9,8},{10,11... | collective-permute-start | bytes 884744 | tf_op jit(solution)/shard_map/ppermute | solution.py:233
  94.5 5.8 %collective-permute-start.17 = (f32[72,256]{1,0:T(8,128)S(1)}, f32[72,256]{1,0:T(8,128)S(1)}, u32[]{:S(2)}, u32[]{:S(2)}) collective-permute-start(f32[72,256]{1,0:T(8,128)S(1)} %get-tuple-element.68), channel_id=1, source_target_pairs={{0,2},{1,3},{2,4},{3,5},{4,6},{5,7},{6,0},{7,1},{8,10},{9,11},{10,... | collective-permute-start | bytes 221192 | tf_op jit(solution)/shard_map/ppermute | solution.py:235
  95.5 6.2 %collective-permute-start.18 = (f32[72,256]{1,0:T(8,128)S(1)}, f32[72,256]{1,0:T(8,128)S(1)}, u32[]{:S(2)}, u32[]{:S(2)}) collective-permute-start(f32[72,256]{1,0:T(8,128)S(1)} %get-tuple-element.69), channel_id=1, source_target_pairs={{0,4},{1,5},{2,6},{3,7},{4,0},{5,1},{6,2},{7,3},{8,12},{9,13},{10,... | collective-permute-start | bytes 221192 | tf_op jit(solution)/shard_map/ppermute | solution.py:235
  99.4 5.6 %collective-permute-start.19 = (f32[72,256]{1,0:T(8,128)S(1)}, f32[72,256]{1,0:T(8,128)S(1)}, u32[]{:S(2)}, u32[]{:S(2)}) collective-permute-start(f32[72,256]{1,0:T(8,128)S(1)} %get-tuple-element.70), channel_id=1, source_target_pairs={{0,6},{1,7},{2,0},{3,1},{4,2},{5,3},{6,4},{7,5},{8,14},{9,15},{10,... | collective-permute-start | bytes 221192 | tf_op jit(solution)/shard_map/ppermute | solution.py:235

commit v5 on v4

--- a/solution.py
+++ b/solution.py
@@ -58,15 +58,15 @@
     return own, above, right, left, below
 
 
-def put_parts(colour, first_core, parts, high, low):
+def put_parts(place, parts, high, low):
+    colour, first_core = place[0], place[2] == 0
     for ref, slot, first in zip(parts, (0, 1, 2, 2, 3), (0, 0, 0, 4, 0)):
-        k = lax.rem(colour + slot, 4)
+        k = (colour + slot) & 3
+        shifts = (k, (k + 2) & 3)
         for j in range(ref.shape[0]):
             m = j + first
             row = jnp.where(
-                first_core,
-                lax.rem(k + 2 * m, 4) * NZ + m,
-                m // 2 * NZ + lax.rem(k + 2 * (m // 2), 4) + 4 * (m % 2),
+                first_core, shifts[m % 2] * NZ + m, shifts[m // 2 % 2] + (m // 2 * NZ + 4 * (m % 2))
             )
             at = pl.ds(pl.multiple_of(row * BLOCK, BLOCK), BLOCK)
             value = ref[j]
@@ -75,69 +75,101 @@
             low[at, :] = (value - top.astype(F32)).astype(BF16)
 
 
-def product_kernel(with_sums, place, *refs):
-    parts, (k_high, k_low), refs = refs[:5], refs[5:7], refs[7:]
-    if with_sums:
-        images, sums, refs = refs[:4], refs[4], refs[5:]
-    keep, send, high, low = refs
-    x, even_core = place[1], place[2] == 0
-    put_parts(place[0], even_core, parts, high, low)
-    value = jnp.dot(k_high[...], high[...], preferred_element_type=F32)
-    value += jnp.dot(k_low[...], high[...], preferred_element_type=F32)
-    value += jnp.dot(k_high[...], low[...], preferred_element_type=F32)
-    for p in range(NX):
-        even = value[2 * p * BLOCK : (2 * p + 1) * BLOCK]
-        odd = value[(2 * p + 1) * BLOCK : (2 * p + 2) * BLOCK]
-        dx = lax.rem(p - x + NX, NX)
-        keep[dx, :BLOCK] = jnp.where(even_core, even, odd)
-        send[dx, :BLOCK] = jnp.where(even_core, odd, even)
-    if with_sums:
-        form = jnp.zeros((BLOCK, EPOCHS), F32)
+def multiply(k_high, k_low, half, high, low):
+    top = k_high[half].reshape(NX * BLOCK, -1)
+    value = jnp.dot(top, high[...], preferred_element_type=F32)
+    value += jnp.dot(k_low[half].reshape(NX * BLOCK, -1), high[...], preferred_element_type=F32)
+    value += jnp.dot(top, low[...], preferred_element_type=F32)
+    return value.reshape(NX, BLOCK, EPOCHS)
+
+
+KEEP, SEND = 0, 1
+
+
+def send_kernel(place, own, above, right, left, below, k_high, k_low, send, high, low):
+    put_parts(place, (own, above, right, left, below), high, low)
+    send[...] = multiply(k_high, k_low, SEND, high, low)
+
+
+def keep_kernel(k_high, k_low, high, low, keep):
+    keep[...] = multiply(k_high, k_low, KEEP, high, low)
+
+
+def both_kernel(place, own, above, right, left, below, k_high, k_low, *refs):
+    images, (sums, keep, send, high, low) = refs[:4], refs[4:]
+    put_parts(place, (own, above, right, left, below), high, low)
+    form = jnp.zeros((BLOCK, EPOCHS), F32)
+    for half, out in ((SEND, send), (KEEP, keep)):
+        value = multiply(k_high, k_low, half, high, low)
         for d in range(NX):
-            form += keep[d, :BLOCK] * images[d][0] + send[d, :BLOCK] * images[d][1]
-        lane = lax.broadcasted_iota(jnp.int32, (8, EPOCHS), 1)
-        row = lax.broadcasted_iota(jnp.int32, (8, EPOCHS), 0)
-        tile = sums[...] + jnp.where((lane == 3) & (row == 0), jnp.sum(form), 0.0)
-        for d in range(NX):
-            keep[d, BLOCK:] = tile
-            send[d, BLOCK:] = tile
+            out[d, :BLOCK] = value[d]
+            form += value[d] * images[d][half]
+    lane = lax.broadcasted_iota(jnp.int32, (8, EPOCHS), 1)
+    row = lax.broadcasted_iota(jnp.int32, (8, EPOCHS), 0)
+    tile = sums[...] + jnp.where((lane == 3) & (row == 0), jnp.sum(form), 0.0)
+    for d in range(NX):
+        keep[d, BLOCK:] = tile
+        send[d, BLOCK:] = tile
 
 
 VMEM_SPEC = pl.BlockSpec(memory_space=pltpu.VMEM)
 
 
-def split_kernel(tile, high, low):
-    value = tile[...]
-    top = value.astype(BF16)
-    high[...] = top
-    low[...] = (value - top.astype(F32)).astype(BF16)
-
-
-def split(tile):
-    half = jax.ShapeDtypeStruct(tile.shape, BF16)
+SMEM_SPEC = pl.BlockSpec(memory_space=pltpu.SMEM)
+
+
+def split_kernel(place, tile, high, low):
+    x, core = place[1], place[2]
+    for b in range(2 * NX):
+        half, dx = (core + b) & 1, (b // 2 - x) & 3
+        value = tile[b]
+        top = value.astype(BF16)
+        high[half, dx] = top
+        low[half, dx] = (value - top.astype(F32)).astype(BF16)
+
+
+def large_call(kernel, outs, in_specs, flops, scratch=()):
     return pl.pallas_call(
-        split_kernel,
-        out_shape=(half, half),
-        in_specs=[VMEM_SPEC],
-        out_specs=(VMEM_SPEC, VMEM_SPEC),
+        kernel,
+        out_shape=[jax.ShapeDtypeStruct(*o) for o in outs],
+        in_specs=in_specs,
+        out_specs=[VMEM_SPEC] * len(outs),
+        scratch_shapes=scratch,
         compiler_params=pltpu.CompilerParams(vmem_limit_bytes=16 * 1024 * 1024),
-        cost_estimate=pl.CostEstimate(flops=4 * tile.size, bytes_accessed=8 * tile.size, transcendentals=0),
-    )(tile)
-
-
-def product(place, parts, k_high, k_low, extra=()):
-    half = jax.ShapeDtypeStruct((NX, BLOCK + (8 if extra else 0), EPOCHS), F32)
-    return pl.pallas_call(
-        functools.partial(product_kernel, bool(extra)),
-        out_shape=(half, half),
-        in_specs=[pl.BlockSpec(memory_space=pltpu.SMEM)] + [VMEM_SPEC] * (7 + len(extra)),
-        out_specs=(VMEM_SPEC, VMEM_SPEC),
-        scratch_shapes=[pltpu.VMEM((2048, EPOCHS), BF16), pltpu.VMEM((2048, EPOCHS), BF16)],
-        compiler_params=pltpu.CompilerParams(vmem_limit_bytes=16 * 1024 * 1024),
-        cost_estimate=pl.CostEstimate(
-            flops=2 * 3 * 512 * 2048 * EPOCHS, bytes_accessed=7 * 1024 * 1024, transcendentals=0
-        ),
-    )(place, *parts, k_high, k_low, *extra)
+        cost_estimate=pl.CostEstimate(flops=flops, bytes_accessed=7 * 1024 * 1024, transcendentals=0),
+    )
+
+
+def split(place, tile):
+    out = ((2, NX, BLOCK, tile.shape[2]), BF16)
+    return large_call(split_kernel, [out, out], [SMEM_SPEC, VMEM_SPEC], 4 * tile.size)(place, tile)
+
+
+PRODUCT_FLOPS = 2 * 3 * 512 * 2048 * EPOCHS
+FIELD = (2048, EPOCHS)
+
+
+def first_product(place, parts, k_high, k_low):
+    half = ((NX, BLOCK, EPOCHS), F32)
+    send, high, low = large_call(
+        send_kernel,
+        [half, (FIELD, BF16), (FIELD, BF16)],
+        [SMEM_SPEC] + [VMEM_SPEC] * 7,
+        PRODUCT_FLOPS // 2,
+    )(place, *parts, k_high, k_low)
+    (keep,) = large_call(keep_kernel, [half], [VMEM_SPEC] * 4, PRODUCT_FLOPS // 2)(k_high, k_low, high, low)
+    return keep, send
+
+
+def second_product(place, parts, k_high, k_low, images, sums):
+    half = ((NX, BLOCK + 8, EPOCHS), F32)
+    return large_call(
+        both_kernel,
+        [half, half],
+        [SMEM_SPEC] + [VMEM_SPEC] * 12,
+        PRODUCT_FLOPS,
+        [pltpu.VMEM(FIELD, BF16), pltpu.VMEM(FIELD, BF16)],
+    )(place, *parts, k_high, k_low, *images, sums)
 
 
 def dot(a, b):
@@ -232,7 +264,7 @@
 def scatter_col(keep, send):
     other = lax.ppermute(send, "col", SIBLING)
     total = small_call(add_kernel, [keep.shape[1:]] * NX, keep, other)
-    return total[0], *[lax.ppermute(total[d], "col", shift_x(d)) for d in range(1, NX)]
+    return total[0], *[lax.ppermute(total[d], "col", shift_x(d)) for d in (2, 1, 3)]
 
 
 def gather_col(image):
@@ -252,22 +284,22 @@
     y, z, core = row // NZ, lax.rem(row, NZ), lax.rem(col, 2)
     colour = lax.rem(jnp.where(core == 0, y + 2 * z, z + 2 * y), 4)
     place = jnp.stack([colour, col // 2, core]).astype(jnp.int32)
-    tile = kernel_configs.reshape(-1, kernel_configs.shape[2])
+    tile = kernel_configs
 
     r0 = curves * mask_of(lengths)
     own = gather_class(jnp.broadcast_to(r0[None], (8, BLOCK, EPOCHS)))
     own, first_tile, lengths, noise = lax.optimization_barrier((own, tile, lengths, noise))
     mask, noise = mask_of(lengths), jnp.broadcast_to(noise[:, None], block)
     parts = gather_rest(own)
-    k_high, k_low = split(first_tile)
-    pieces = scatter_col(*product(place, parts, k_high, k_low))
+    k_high, k_low = split(place, first_tile)
+    pieces = scatter_col(*first_product(place, parts, k_high, k_low))
     w1, copies, image, sums = small_call(
         first_kernel, [block, (8, *block), block, (8, EPOCHS)], *pieces, epoch_kernel, mask, noise, r0
     )
     own, images, second_tile = lax.optimization_barrier((gather_class(copies), gather_col(image), tile))
     parts = gather_rest(own)
-    k_high, k_low = split(second_tile)
-    pieces = scatter_col(*product(place, parts, k_high, k_low, (*images, sums)))
+    k_high, k_low = split(place, second_tile)
+    pieces = scatter_col(*second_product(place, parts, k_high, k_low, images, sums))
     w2, copies = small_call(
         second_kernel, [block, (32, 1, 128)], *pieces, epoch_kernel, mask, noise, w1
     )

time: 121 us -> 121 us (level)
  starting transfers between devices: 25.6 us -> 21.7 us
  waiting for transfers between devices: 35.3 us -> 37.2 us
  Pallas kernels: 9.38 us -> 10.8 us
    ppermute x2, starting transfers between devices: 6.05 us -> 2.06 us  [gather_rest(): above = lax.ppermute(own, BOTH, shift(-1, 0))]
    ppermute x2, waiting for transfers between devices: 2.33 us -> 4.63 us  [gather_rest(): left = lax.ppermute(upper, BOTH, shift(0, 1))]
    all_to_all x1, waiting for transfers between devices: 3.72 us -> 5.39 us  [gather_class(): return lax.all_to_all(copies, BOTH, 0, 0, axis_index_groups=CLASSES)]
    ppermute x2, starting transfers between devices: 0.43 us -> 1.99 us  [gather_rest(): below = lax.ppermute(own, BOTH, shift(1, 0))]
    pallas_call x4 -> x5, Pallas kernels: 6.95 us -> 8.35 us  [the longest x1 2.89 us: second_product(): large_call(both_kernel, [half, half], [SMEM_SPEC] + [VMEM_SPEC] * 12, PRO...]
  transfers between devices with their start and end apart: 21 -> 21, of which waited for: 19 -> 18; matrix products, arithmetic and copies ran while one was open for 0% -> 0% of each run, Pallas kernels for 1% -> 3%
where the time goes in v5:
time: 121 us
  blocking collectives  44.8 us (37%)
  waiting for transfers between devices  37.2 us (31%)
  starting transfers between devices  21.7 us (18%)
  Pallas kernels  10.8 us (9%)
  local copies, waits for them, and re-layouts  4.5 us (4%)
    all_to_all x1, blocking collectives, gather_class(): return lax.all_to_all(copies, BOTH, 0, 0, axis_index_groups=CLASSES)  29.5 us
    all_to_all x1, blocking collectives, per_device(): tiles = lax.all_to_all(copies, 'row', 0, 0)  15.4 us
    ppermute x6, waiting for transfers between devices, scatter_col(): lax.ppermute(total[d], 'col', shift_x(d))  10.6 us
    ppermute x3, waiting for transfers between devices, gather_col(): lax.ppermute(pair, 'col', shift_x(-d))  7.75 us
    ppermute x6, starting transfers between devices, scatter_col(): lax.ppermute(total[d], 'col', shift_x(d))  6.96 us
    all_to_all x1, waiting for transfers between devices, gather_class(): return lax.all_to_all(copies, BOTH, 0, 0, axis_index_groups=CLASSES)  5.39 us
    ppermute x2, waiting for transfers between devices, gather_rest(): left = lax.ppermute(upper, BOTH, shift(0, 1))  4.63 us
    unnamed x10, local copies, waits for them, and re-layouts  4.4 us
  transfers between devices with their start and end apart: 21, of which 18 were waited for; matrix products, arithmetic and copies ran while one was open for 0% of the time, Pallas kernels for 3%

profile of v5, /device:TPU:6, one launch (start us, length us, event | category | flops | bytes accessed | tf_op | source)
XLA Modules:
  0.0 120.8 jit_solution(2737053236516741315)
XLA Ops:
  1.6 29.5 %all_to_all.15.own = f32[8,64,256]{2,1,0:T(8,128)S(1)} all-to-all(f32[8,64,256]{2,1,0:T(8,128)S(1)} %broadcast_in_dim.4), channel_id=1, replica_groups={{0,136,16,152,32,168,48,184},{64,200,80,216,96,232,112,248},{128,8,144,..., dimensions={0} | all-to-all | bytes 1048576 | tf_op jit(solution)/shard_map/all_to_all | solution.py:49
  31.8 1.3 %collective-permute-start.3 = (f32[8,64,256]{2,1,0:T(8,128)S(1)}, f32[8,64,256]{2,1,0:T(8,128)S(1)}, u32[]{:S(2)}, u32[]{:S(2)}) collective-permute-start(f32[8,64,256]{2,1,0:T(8,128)S(1)} %all_to_all.15.own), channel_id=1, source_target_pairs={{0,64},{1,9},{2,66},{3,11},{4,68},{5,13},{6,70},{7,15},{8,72},{9,1... | collective-permute-start | bytes 1572872 | tf_op jit(solution)/shard_map/ppermute | solution.py:54
  33.2 2.0 %collective-permute-start.2 = (f32[4,64,256]{2,1,0:T(8,128)S(1)}, f32[4,64,256]{2,1,0:T(8,128)S(1)}, u32[]{:S(2)}, u32[]{:S(2)}) collective-permute-start(f32[4,64,256]{2,1,0:T(8,128)S(1)} %get-tuple-element.44), channel_id=1, source_target_pairs={{0,8},{1,65},{2,10},{3,67},{4,12},{5,69},{6,14},{7,71},{8,16},{9,7... | collective-permute-start | bytes 786440 | tf_op jit(solution)/shard_map/ppermute | solution.py:57
  35.3 2.2 %copy-done = f32[8,64,2048]{2,1,0:T(8,128)S(1)} copy-done((f32[8,64,2048]{2,1,0:T(8,128)S(1)}, f32[8,64,2048]{2,1,0:T(8,128)}, u32[]{:S(2)}) %copy-start) | copy-done | bytes 4194328
  37.5 1.3 %shard_map.68 = (bf16[2,4,64,2048]{3,2,1,0:T(8,128)(2,1)S(1)}, bf16[2,4,64,2048]{3,2,1,0:T(8,128)(2,1)S(1)}) custom-call(s32[3]{0:T(128)S(1)} %pad_add_fusion.place, f32[8,64,2048]{2,1,0:T(8,128)S(1)} %copy-done), custom_call_target="tpu_custom_call" | custom-call | flops 4194304 | bytes 7340032 | tf_op jit(solution)/shard_map/pallas_call | solution.py:145
  38.8 1.6 %collective-permute-done.1.right = f32[4,64,256]{2,1,0:T(8,128)S(1)} collective-permute-done((f32[4,64,256]{2,1,0:T(8,128)S(1)}, f32[4,64,256]{2,1,0:T(8,128)S(1)}, u32[]{:S(2)}, u32[]{:S(2)}) %collective-permute-start.1) | collective-permute-done | bytes 262176 | tf_op jit(solution)/shard_map/ppermute | solution.py:56
  40.4 1.2 %collective-permute-done.2.left = f32[4,64,256]{2,1,0:T(8,128)S(1)} collective-permute-done((f32[4,64,256]{2,1,0:T(8,128)S(1)}, f32[4,64,256]{2,1,0:T(8,128)S(1)}, u32[]{:S(2)}, u32[]{:S(2)}) %collective-permute-start.2) | collective-permute-done | bytes 262176 | tf_op jit(solution)/shard_map/ppermute | solution.py:57
  42.0 1.4 %collective-permute-done.3.below = f32[8,64,256]{2,1,0:T(8,128)S(1)} collective-permute-done((f32[8,64,256]{2,1,0:T(8,128)S(1)}, f32[8,64,256]{2,1,0:T(8,128)S(1)}, u32[]{:S(2)}, u32[]{:S(2)}) %collective-permute-start.3) | collective-permute-done | bytes 524320 | tf_op jit(solution)/shard_map/ppermute | solution.py:54
  43.4 1.9 %shard_map.70 = (f32[4,64,256]{2,1,0:T(8,128)S(1)}, bf16[2048,256]{1,0:T(8,128)(2,1)S(1)}, bf16[2048,256]{1,0:T(8,128)(2,1)S(1)}) custom-call(s32[3]{0:T(128)S(1)} %pad_add_fusion.place, f32[8,64,256]{2,1,0:T(8,128)S(1)} %all_to_all.15.own, f32[8,64,256]{2,1,0:T(8,128)S(1)} %collective-permute-done.above, f32[4,64,256]{2,1,0:T(8,128)S(1)} %collective-permute-done.1.right, ...), custom_call_target="tpu_custom_call" | custom-call | flops 805306368 | bytes 7340032 | tf_op jit(solution)/shard_map/pallas_call | solution.py:154
  47.0 1.5 %collective-permute-start.5 = (f32[64,256]{1,0:T(8,128)S(1)}, f32[64,256]{1,0:T(8,128)S(1)}, u32[]{:S(2)}, u32[]{:S(2)}) collective-permute-start(f32[64,256]{1,0:T(8,128)S(1)} %get-tuple-element.49), channel_id=1, source_target_pairs={{0,4},{1,5},{2,6},{3,7},{4,0},{5,1},{6,2},{7,3},{8,12},{9,13},{10,... | collective-permute-start | bytes 196616 | tf_op jit(solution)/shard_map/ppermute | solution.py:267
  48.5 2.1 %collective-permute-start.6 = (f32[64,256]{1,0:T(8,128)S(1)}, f32[64,256]{1,0:T(8,128)S(1)}, u32[]{:S(2)}, u32[]{:S(2)}) collective-permute-start(f32[64,256]{1,0:T(8,128)S(1)} %get-tuple-element.50), channel_id=1, source_target_pairs={{0,2},{1,3},{2,4},{3,5},{4,6},{5,7},{6,0},{7,1},{8,10},{9,11},{10,... | collective-permute-start | bytes 196616 | tf_op jit(solution)/shard_map/ppermute | solution.py:267
  50.7 2.3 %collective-permute-done.5.t1 = f32[64,256]{1,0:T(8,128)S(1)} collective-permute-done((f32[64,256]{1,0:T(8,128)S(1)}, f32[64,256]{1,0:T(8,128)S(1)}, u32[]{:S(2)}, u32[]{:S(2)}) %collective-permute-start.5) | collective-permute-done | bytes 65568 | tf_op jit(solution)/shard_map/ppermute | solution.py:267
  53.0 3.1 %collective-permute-done.7.t3 = f32[64,256]{1,0:T(8,128)S(1)} collective-permute-done((f32[64,256]{1,0:T(8,128)S(1)}, f32[64,256]{1,0:T(8,128)S(1)}, u32[]{:S(2)}, u32[]{:S(2)}) %collective-permute-start.7) | collective-permute-done | bytes 65568 | tf_op jit(solution)/shard_map/ppermute | solution.py:267
  57.3 4.1 %all-to-all-start.1 = ((f32[8,64,256]{2,1,0:T(8,128)}), f32[8,64,256]{2,1,0:T(8,128)S(1)}, u32[]{:S(2)}, u32[]{:S(2)}) async-start(f32[8,64,256]{2,1,0:T(8,128)} %get-tuple-element.54), calls=%async_computation.1 | async-start | bytes 1048576 | tf_op jit(solution)/shard_map/all_to_all | solution.py:49
  61.4 1.2 %collective-permute-done.8.other = f32[64,256]{1,0:T(8,128)S(1)} collective-permute-done((f32[64,256]{1,0:T(8,128)S(1)}, f32[64,256]{1,0:T(8,128)S(1)}, u32[]{:S(2)}, u32[]{:S(2)}) %collective-permute-start.8) | collective-permute-done | bytes 65568 | tf_op jit(solution)/shard_map/ppermute | solution.py:271
  62.8 1.5 %collective-permute-start.11 = (f32[2,64,256]{2,1,0:T(8,128)S(1)}, f32[2,64,256]{2,1,0:T(8,128)S(1)}, u32[]{:S(2)}, u32[]{:S(2)}) collective-permute-start(f32[2,64,256]{2,1,0:T(8,128)S(1)} %shard_map.74.refs_0_), channel_id=1, source_target_pairs={{0,2},{1,3},{2,4},{3,5},{4,6},{5,7},{6,0},{7,1},{8,10},{9,11},{10,... | collective-permute-start | bytes 393224 | tf_op jit(solution)/shard_map/ppermute | solution.py:273
  64.9 5.7 %collective-permute-done.10.refs_2_ = f32[2,64,256]{2,1,0:T(8,128)S(1)} collective-permute-done((f32[2,64,256]{2,1,0:T(8,128)S(1)}, f32[2,64,256]{2,1,0:T(8,128)S(1)}, u32[]{:S(2)}, u32[]{:S(2)}) %collective-permute-start.10) | collective-permute-done | bytes 131104 | tf_op jit(solution)/shard_map/ppermute | solution.py:273
  70.6 2.0 %collective-permute-done.9.refs_1_ = f32[2,64,256]{2,1,0:T(8,128)S(1)} collective-permute-done((f32[2,64,256]{2,1,0:T(8,128)S(1)}, f32[2,64,256]{2,1,0:T(8,128)S(1)}, u32[]{:S(2)}, u32[]{:S(2)}) %collective-permute-start.9) | collective-permute-done | bytes 131104 | tf_op jit(solution)/shard_map/ppermute | solution.py:273
  72.6 5.4 %all-to-all-done.1.own = f32[8,64,256]{2,1,0:T(8,128)S(1)} async-done(((f32[8,64,256]{2,1,0:T(8,128)}), f32[8,64,256]{2,1,0:T(8,128)S(1)}, u32[]{:S(2)}, u32[]{:S(2)}) %all-to-all-start.1) | async-done | bytes 524320 | tf_op jit(solution)/shard_map/all_to_all | solution.py:49
  78.0 1.4 %collective-permute-start.12 = (f32[8,64,256]{2,1,0:T(8,128)S(1)}, f32[8,64,256]{2,1,0:T(8,128)S(1)}, u32[]{:S(2)}, u32[]{:S(2)}) collective-permute-start(f32[8,64,256]{2,1,0:T(8,128)S(1)} %all-to-all-done.1.own), channel_id=1, source_target_pairs={{0,192},{1,57},{2,194},{3,59},{4,196},{5,61},{6,198},{7,63},{8,200... | collective-permute-start | bytes 1572872 | tf_op jit(solution)/shard_map/ppermute | solution.py:53
  81.0 1.2 %collective-permute-start.14 = (f32[4,64,256]{2,1,0:T(8,128)S(1)}, f32[4,64,256]{2,1,0:T(8,128)S(1)}, u32[]{:S(2)}, u32[]{:S(2)}) collective-permute-start(f32[4,64,256]{2,1,0:T(8,128)S(1)} %get-tuple-element.58), channel_id=1, source_target_pairs={{0,8},{1,65},{2,10},{3,67},{4,12},{5,69},{6,14},{7,71},{8,16},{9,7... | collective-permute-start | bytes 786440 | tf_op jit(solution)/shard_map/ppermute | solution.py:57
  82.2 2.2 %copy-done.1 = f32[8,64,2048]{2,1,0:T(8,128)S(1)} copy-done((f32[8,64,2048]{2,1,0:T(8,128)S(1)}, f32[8,64,2048]{2,1,0:T(8,128)}, u32[]{:S(2)}) %copy-start.1) | copy-done | bytes 4194328
  84.4 1.3 %shard_map.76 = (bf16[2,4,64,2048]{3,2,1,0:T(8,128)(2,1)S(1)}, bf16[2,4,64,2048]{3,2,1,0:T(8,128)(2,1)S(1)}) custom-call(s32[3]{0:T(128)S(1)} %pad_add_fusion.place, f32[8,64,2048]{2,1,0:T(8,128)S(1)} %copy-done.1), custom_call_target="tpu_custom_call" | custom-call | flops 4194304 | bytes 7340032 | tf_op jit(solution)/shard_map/pallas_call | solution.py:145
  85.7 1.7 %collective-permute-done.13.right = f32[4,64,256]{2,1,0:T(8,128)S(1)} collective-permute-done((f32[4,64,256]{2,1,0:T(8,128)S(1)}, f32[4,64,256]{2,1,0:T(8,128)S(1)}, u32[]{:S(2)}, u32[]{:S(2)}) %collective-permute-start.13) | collective-permute-done | bytes 262176 | tf_op jit(solution)/shard_map/ppermute | solution.py:56
  87.4 3.4 %collective-permute-done.14.left = f32[4,64,256]{2,1,0:T(8,128)S(1)} collective-permute-done((f32[4,64,256]{2,1,0:T(8,128)S(1)}, f32[4,64,256]{2,1,0:T(8,128)S(1)}, u32[]{:S(2)}, u32[]{:S(2)}) %collective-permute-start.14) | collective-permute-done | bytes 262176 | tf_op jit(solution)/shard_map/ppermute | solution.py:57
  91.1 2.9 %shard_map.77 = (f32[4,72,256]{2,1,0:T(8,128)S(1)}, f32[4,72,256]{2,1,0:T(8,128)S(1)}) custom-call(s32[3]{0:T(128)S(1)} %pad_add_fusion.place, f32[8,64,256]{2,1,0:T(8,128)S(1)} %all-to-all-done.1.own, f32[8,64,256]{2,1,0:T(8,128)S(1)} %collective-permute-done.12.above, f32[4,64,256]{2,1,0:T(8,128)S(1)} %collective-permute-done.13.right, ...), custom_call_target="tpu_custom_call" | custom-call | flops 1610612736 | bytes 7340032 | tf_op jit(solution)/shard_map/pallas_call | solution.py:166
  94.1 1.6 %collective-permute-done.16.other = f32[4,72,256]{2,1,0:T(8,128)S(1)} collective-permute-done((f32[4,72,256]{2,1,0:T(8,128)S(1)}, f32[4,72,256]{2,1,0:T(8,128)S(1)}, u32[]{:S(2)}, u32[]{:S(2)}) %collective-permute-start.16) | collective-permute-done | bytes 294944 | tf_op jit(solution)/shard_map/ppermute | solution.py:265
  95.7 1.3 %collective-permute-start.17 = (f32[72,256]{1,0:T(8,128)S(1)}, f32[72,256]{1,0:T(8,128)S(1)}, u32[]{:S(2)}, u32[]{:S(2)}) collective-permute-start(f32[72,256]{1,0:T(8,128)S(1)} %get-tuple-element.70), channel_id=1, source_target_pairs={{0,4},{1,5},{2,6},{3,7},{4,0},{5,1},{6,2},{7,3},{8,12},{9,13},{10,... | collective-permute-start | bytes 221192 | tf_op jit(solution)/shard_map/ppermute | solution.py:267
  97.1 1.7 %collective-permute-start.18 = (f32[72,256]{1,0:T(8,128)S(1)}, f32[72,256]{1,0:T(8,128)S(1)}, u32[]{:S(2)}, u32[]{:S(2)}) collective-permute-start(f32[72,256]{1,0:T(8,128)S(1)} %get-tuple-element.71), channel_id=1, source_target_pairs={{0,2},{1,3},{2,4},{3,5},{4,6},{5,7},{6,0},{7,1},{8,10},{9,11},{10,... | collective-permute-start | bytes 221192 | tf_op jit(solution)/shard_map/ppermute | solution.py:267
  99.1 2.8 %collective-permute-done.17.t1 = f32[72,256]{1,0:T(8,128)S(1)} collective-permute-done((f32[72,256]{1,0:T(8,128)S(1)}, f32[72,256]{1,0:T(8,128)S(1)}, u32[]{:S(2)}, u32[]{:S(2)}) %collective-permute-start.17) | collective-permute-done | bytes 73760 | tf_op jit(solution)/shard_map/ppermute | solution.py:267
  102.0 2.4 %collective-permute-done.19.t3 = f32[72,256]{1,0:T(8,128)S(1)} collective-permute-done((f32[72,256]{1,0:T(8,128)S(1)}, f32[72,256]{1,0:T(8,128)S(1)}, u32[]{:S(2)}, u32[]{:S(2)}) %collective-permute-start.19) | collective-permute-done | bytes 73760 | tf_op jit(solution)/shard_map/ppermute | solution.py:267
  104.6 15.4 %all_to_all.16.tiles = f32[32,1,128]{2,1,0:T(1,128)S(1)} all-to-all(f32[32,1,128]{2,1,0:T(1,128)S(1)} %get-tuple-element.74), channel_id=1, replica_groups=mesh['row'=32,'col'=8] {'row'}, dimensions={0} | all-to-all | bytes 32768 | tf_op jit(solution)/shard_map/all_to_all | solution.py:306
  (40 shorter events, 9.5 us)
Async XLA Ops:
  31.1 11.0 %collective-permute-start = (f32[8,64,256]{2,1,0:T(8,128)S(1)}, f32[8,64,256]{2,1,0:T(8,128)S(1)}, u32[]{:S(2)}, u32[]{:S(2)}) collective-permute-start(f32[8,64,256]{2,1,0:T(8,128)S(1)} %all_to_all.15.own), channel_id=1, source_target_pairs={{0,192},{1,57},{2,194},{3,59},{4,196},{5,61},{6,198},{7,63},{8,200... | collective-permute-start | bytes 1572872 | tf_op jit(solution)/shard_map/ppermute | solution.py:53
  31.8 11.7 %collective-permute-start.3 = (f32[8,64,256]{2,1,0:T(8,128)S(1)}, f32[8,64,256]{2,1,0:T(8,128)S(1)}, u32[]{:S(2)}, u32[]{:S(2)}) collective-permute-start(f32[8,64,256]{2,1,0:T(8,128)S(1)} %all_to_all.15.own), channel_id=1, source_target_pairs={{0,64},{1,9},{2,66},{3,11},{4,68},{5,13},{6,70},{7,15},{8,72},{9,1... | collective-permute-start | bytes 1572872 | tf_op jit(solution)/shard_map/ppermute | solution.py:54
  33.1 7.3 %collective-permute-start.1 = (f32[4,64,256]{2,1,0:T(8,128)S(1)}, f32[4,64,256]{2,1,0:T(8,128)S(1)}, u32[]{:S(2)}, u32[]{:S(2)}) collective-permute-start(f32[4,64,256]{2,1,0:T(8,128)S(1)} %get-tuple-element.43), channel_id=1, source_target_pairs={{0,56},{1,193},{2,58},{3,195},{4,60},{5,197},{6,62},{7,199},{8,0},... | collective-permute-start | bytes 786440 | tf_op jit(solution)/shard_map/ppermute | solution.py:56
  33.2 8.4 %collective-permute-start.2 = (f32[4,64,256]{2,1,0:T(8,128)S(1)}, f32[4,64,256]{2,1,0:T(8,128)S(1)}, u32[]{:S(2)}, u32[]{:S(2)}) collective-permute-start(f32[4,64,256]{2,1,0:T(8,128)S(1)} %get-tuple-element.44), channel_id=1, source_target_pairs={{0,8},{1,65},{2,10},{3,67},{4,12},{5,69},{6,14},{7,71},{8,16},{9,7... | collective-permute-start | bytes 786440 | tf_op jit(solution)/shard_map/ppermute | solution.py:57
  35.3 2.2 %copy-start = (f32[8,64,2048]{2,1,0:T(8,128)S(1)}, f32[8,64,2048]{2,1,0:T(8,128)}, u32[]{:S(2)}) copy-start(f32[8,64,2048]{2,1,0:T(8,128)} %tile.1) | copy-start | bytes 12582916
  45.3 1.6 %collective-permute-start.4 = (f32[4,64,256]{2,1,0:T(8,128)S(1)}, f32[4,64,256]{2,1,0:T(8,128)S(1)}, u32[]{:S(2)}, u32[]{:S(2)}) collective-permute-start(f32[4,64,256]{2,1,0:T(8,128)S(1)} %get-tuple-element.47), channel_id=1, source_target_pairs={{0,1},{1,0},{2,3},{3,2},{4,5},{5,4},{6,7},{7,6},{8,9},{9,8},{10,11... | collective-permute-start | bytes 786440 | tf_op jit(solution)/shard_map/ppermute | solution.py:265
  45.4 5.1 %copy-start.3 = (s32[64]{0:T(128)S(1)}, s32[64]{0:T(128)}, u32[]{:S(2)}) copy-start(s32[64]{0:T(128)} %param.7) | copy-start | bytes 772
  45.4 10.6 %copy-start.4 = (f32[64]{0:T(128)S(1)}, f32[64]{0:T(128)}, u32[]{:S(2)}) copy-start(f32[64]{0:T(128)} %param.8) | copy-start | bytes 772
  45.5 10.7 %copy-start.2 = (f32[256,256]{1,0:T(8,128)S(1)}, f32[256,256]{1,0:T(8,128)}, u32[]{:S(2)}) copy-start(f32[256,256]{1,0:T(8,128)} %kernel.3) | copy-start | bytes 786436
  47.0 6.0 %collective-permute-start.5 = (f32[64,256]{1,0:T(8,128)S(1)}, f32[64,256]{1,0:T(8,128)S(1)}, u32[]{:S(2)}, u32[]{:S(2)}) collective-permute-start(f32[64,256]{1,0:T(8,128)S(1)} %get-tuple-element.49), channel_id=1, source_target_pairs={{0,4},{1,5},{2,6},{3,7},{4,0},{5,1},{6,2},{7,3},{8,12},{9,13},{10,... | collective-permute-start | bytes 196616 | tf_op jit(solution)/shard_map/ppermute | solution.py:267
  48.5 4.5 %collective-permute-start.6 = (f32[64,256]{1,0:T(8,128)S(1)}, f32[64,256]{1,0:T(8,128)S(1)}, u32[]{:S(2)}, u32[]{:S(2)}) collective-permute-start(f32[64,256]{1,0:T(8,128)S(1)} %get-tuple-element.50), channel_id=1, source_target_pairs={{0,2},{1,3},{2,4},{3,5},{4,6},{5,7},{6,0},{7,1},{8,10},{9,11},{10,... | collective-permute-start | bytes 196616 | tf_op jit(solution)/shard_map/ppermute | solution.py:267
  50.6 5.5 %collective-permute-start.7 = (f32[64,256]{1,0:T(8,128)S(1)}, f32[64,256]{1,0:T(8,128)S(1)}, u32[]{:S(2)}, u32[]{:S(2)}) collective-permute-start(f32[64,256]{1,0:T(8,128)S(1)} %get-tuple-element.51), channel_id=1, source_target_pairs={{0,6},{1,7},{2,0},{3,1},{4,2},{5,3},{6,4},{7,5},{8,14},{9,15},{10,... | collective-permute-start | bytes 196616 | tf_op jit(solution)/shard_map/ppermute | solution.py:267
  57.3 20.7 %all-to-all-start.1 = ((f32[8,64,256]{2,1,0:T(8,128)}), f32[8,64,256]{2,1,0:T(8,128)S(1)}, u32[]{:S(2)}, u32[]{:S(2)}) async-start(f32[8,64,256]{2,1,0:T(8,128)} %get-tuple-element.54), calls=%async_computation.1 | async-start | bytes 1048576 | tf_op jit(solution)/shard_map/all_to_all | solution.py:49
  61.4 1.3 %collective-permute-start.8 = (f32[64,256]{1,0:T(8,128)S(1)}, f32[64,256]{1,0:T(8,128)S(1)}, u32[]{:S(2)}, u32[]{:S(2)}) collective-permute-start(f32[64,256]{1,0:T(8,128)S(1)} %get-tuple-element.55.image), channel_id=1, source_target_pairs={{0,1},{1,0},{2,3},{3,2},{4,5},{5,4},{6,7},{7,6},{8,9},{9,8},{10,11... | collective-permute-start | bytes 196616 | tf_op jit(solution)/shard_map/ppermute | solution.py:271
  62.7 7.9 %collective-permute-start.10 = (f32[2,64,256]{2,1,0:T(8,128)S(1)}, f32[2,64,256]{2,1,0:T(8,128)S(1)}, u32[]{:S(2)}, u32[]{:S(2)}) collective-permute-start(f32[2,64,256]{2,1,0:T(8,128)S(1)} %shard_map.74.refs_0_), channel_id=1, source_target_pairs={{0,4},{1,5},{2,6},{3,7},{4,0},{5,1},{6,2},{7,3},{8,12},{9,13},{10,... | collective-permute-start | bytes 393224 | tf_op jit(solution)/shard_map/ppermute | solution.py:273
  62.8 7.8 %collective-permute-start.11 = (f32[2,64,256]{2,1,0:T(8,128)S(1)}, f32[2,64,256]{2,1,0:T(8,128)S(1)}, u32[]{:S(2)}, u32[]{:S(2)}) collective-permute-start(f32[2,64,256]{2,1,0:T(8,128)S(1)} %shard_map.74.refs_0_), channel_id=1, source_target_pairs={{0,2},{1,3},{2,4},{3,5},{4,6},{5,7},{6,0},{7,1},{8,10},{9,11},{10,... | collective-permute-start | bytes 393224 | tf_op jit(solution)/shard_map/ppermute | solution.py:273
  64.2 8.4 %collective-permute-start.9 = (f32[2,64,256]{2,1,0:T(8,128)S(1)}, f32[2,64,256]{2,1,0:T(8,128)S(1)}, u32[]{:S(2)}, u32[]{:S(2)}) collective-permute-start(f32[2,64,256]{2,1,0:T(8,128)S(1)} %shard_map.74.refs_0_), channel_id=1, source_target_pairs={{0,6},{1,7},{2,0},{3,1},{4,2},{5,3},{6,4},{7,5},{8,14},{9,15},{10,... | collective-permute-start | bytes 393224 | tf_op jit(solution)/shard_map/ppermute | solution.py:273
  78.0 12.8 %collective-permute-start.12 = (f32[8,64,256]{2,1,0:T(8,128)S(1)}, f32[8,64,256]{2,1,0:T(8,128)S(1)}, u32[]{:S(2)}, u32[]{:S(2)}) collective-permute-start(f32[8,64,256]{2,1,0:T(8,128)S(1)} %all-to-all-done.1.own), channel_id=1, source_target_pairs={{0,192},{1,57},{2,194},{3,59},{4,196},{5,61},{6,198},{7,63},{8,200... | collective-permute-start | bytes 1572872 | tf_op jit(solution)/shard_map/ppermute | solution.py:53
  79.4 11.7 %collective-permute-start.15 = (f32[8,64,256]{2,1,0:T(8,128)S(1)}, f32[8,64,256]{2,1,0:T(8,128)S(1)}, u32[]{:S(2)}, u32[]{:S(2)}) collective-permute-start(f32[8,64,256]{2,1,0:T(8,128)S(1)} %all-to-all-done.1.own), channel_id=1, source_target_pairs={{0,64},{1,9},{2,66},{3,11},{4,68},{5,13},{6,70},{7,15},{8,72},{9,1... | collective-permute-start | bytes 1572872 | tf_op jit(solution)/shard_map/ppermute | solution.py:54
  80.1 7.3 %collective-permute-start.13 = (f32[4,64,256]{2,1,0:T(8,128)S(1)}, f32[4,64,256]{2,1,0:T(8,128)S(1)}, u32[]{:S(2)}, u32[]{:S(2)}) collective-permute-start(f32[4,64,256]{2,1,0:T(8,128)S(1)} %get-tuple-element.57), channel_id=1, source_target_pairs={{0,56},{1,193},{2,58},{3,195},{4,60},{5,197},{6,62},{7,199},{8,0},... | collective-permute-start | bytes 786440 | tf_op jit(solution)/shard_map/ppermute | solution.py:56
  81.0 9.8 %collective-permute-start.14 = (f32[4,64,256]{2,1,0:T(8,128)S(1)}, f32[4,64,256]{2,1,0:T(8,128)S(1)}, u32[]{:S(2)}, u32[]{:S(2)}) collective-permute-start(f32[4,64,256]{2,1,0:T(8,128)S(1)} %get-tuple-element.58), channel_id=1, source_target_pairs={{0,8},{1,65},{2,10},{3,67},{4,12},{5,69},{6,14},{7,71},{8,16},{9,7... | collective-permute-start | bytes 786440 | tf_op jit(solution)/shard_map/ppermute | solution.py:57
  82.2 2.2 %copy-start.1 = (f32[8,64,2048]{2,1,0:T(8,128)S(1)}, f32[8,64,2048]{2,1,0:T(8,128)}, u32[]{:S(2)}) copy-start(f32[8,64,2048]{2,1,0:T(8,128)} %tile.1) | copy-start | bytes 12582916
  94.0 1.7 %collective-permute-start.16 = (f32[4,72,256]{2,1,0:T(8,128)S(1)}, f32[4,72,256]{2,1,0:T(8,128)S(1)}, u32[]{:S(2)}, u32[]{:S(2)}) collective-permute-start(f32[4,72,256]{2,1,0:T(8,128)S(1)} %get-tuple-element.68), channel_id=1, source_target_pairs={{0,1},{1,0},{2,3},{3,2},{4,5},{5,4},{6,7},{7,6},{8,9},{9,8},{10,11... | collective-permute-start | bytes 884744 | tf_op jit(solution)/shard_map/ppermute | solution.py:265
  95.7 6.2 %collective-permute-start.17 = (f32[72,256]{1,0:T(8,128)S(1)}, f32[72,256]{1,0:T(8,128)S(1)}, u32[]{:S(2)}, u32[]{:S(2)}) collective-permute-start(f32[72,256]{1,0:T(8,128)S(1)} %get-tuple-element.70), channel_id=1, source_target_pairs={{0,4},{1,5},{2,6},{3,7},{4,0},{5,1},{6,2},{7,3},{8,12},{9,13},{10,... | collective-permute-start | bytes 221192 | tf_op jit(solution)/shard_map/ppermute | solution.py:267
  97.1 4.9 %collective-permute-start.18 = (f32[72,256]{1,0:T(8,128)S(1)}, f32[72,256]{1,0:T(8,128)S(1)}, u32[]{:S(2)}, u32[]{:S(2)}) collective-permute-start(f32[72,256]{1,0:T(8,128)S(1)} %get-tuple-element.71), channel_id=1, source_target_pairs={{0,2},{1,3},{2,4},{3,5},{4,6},{5,7},{6,0},{7,1},{8,10},{9,11},{10,... | collective-permute-start | bytes 221192 | tf_op jit(solution)/shard_map/ppermute | solution.py:267
  98.8 5.6 %collective-permute-start.19 = (f32[72,256]{1,0:T(8,128)S(1)}, f32[72,256]{1,0:T(8,128)S(1)}, u32[]{:S(2)}, u32[]{:S(2)}) collective-permute-start(f32[72,256]{1,0:T(8,128)S(1)} %get-tuple-element.72), channel_id=1, source_target_pairs={{0,6},{1,7},{2,0},{3,1},{4,2},{5,3},{6,4},{7,5},{8,14},{9,15},{10,... | collective-permute-start | bytes 221192 | tf_op jit(solution)/shard_map/ppermute | solution.py:267

commit v6 on v5

--- a/solution.py
+++ b/solution.py
@@ -198,7 +198,7 @@
     return tile
 
 
-def first_kernel(t0, t1, t2, t3, kernel, mask, noise, r0, w1, copies, image, sums):
+def first_kernel(t0, t1, t2, t3, kernel, mask, noise, r0, w1, copies):
     smoothed = dot(t0[...] + t1[...] + t2[...] + t3[...], kernel[...])
     start = r0[...]
     value = mask[...] * smoothed + noise[...] * start
@@ -206,8 +206,12 @@
     masked = mask[...] * value
     for j in range(8):
         copies[j] = masked
+
+
+def image_kernel(kernel, mask, noise, r0, w1, image, sums):
+    start, value = r0[...], w1[...]
     image[...] = lax.dot_general(
-        masked, kernel[...], (((1,), (1,)), ((), ())),
+        mask[...] * value, kernel[...], (((1,), (1,)), ((), ())),
         precision=lax.Precision.HIGHEST, preferred_element_type=F32,
     )
     sums[...] = tile_of(
@@ -293,9 +297,10 @@
     parts = gather_rest(own)
     k_high, k_low = split(place, first_tile)
     pieces = scatter_col(*first_product(place, parts, k_high, k_low))
-    w1, copies, image, sums = small_call(
-        first_kernel, [block, (8, *block), block, (8, EPOCHS)], *pieces, epoch_kernel, mask, noise, r0
-    )
+    w1, copies = small_call(
+        first_kernel, [block, (8, *block)], *pieces, epoch_kernel, mask, noise, r0
+    )
+    image, sums = small_call(image_kernel, [block, (8, EPOCHS)], epoch_kernel, mask, noise, r0, w1)
     own, images, second_tile = lax.optimization_barrier((gather_class(copies), gather_col(image), tile))
     parts = gather_rest(own)
     k_high, k_low = split(place, second_tile)

time: 121 us -> 121 us (level)
    pallas_call x8 -> x9, Pallas kernels: 2.43 us -> 2.69 us  [small_call(): pl.pallas_call(kernel, out_shape=[jax.ShapeDtypeStruct(o, F32) for o in o...]
  transfers between devices with their start and end apart: 21 -> 21, of which waited for: 18 -> 17; matrix products, arithmetic and copies ran while one was open for 0% -> 0% of each run, Pallas kernels for 3% -> 3%
where the time goes in v6:
time: 121 us
  blocking collectives  44.9 us (37%)
  waiting for transfers between devices  37 us (31%)
  starting transfers between devices  21.5 us (18%)
  Pallas kernels  11 us (9%)
  local copies, waits for them, and re-layouts  4.5 us (4%)
    all_to_all x1, blocking collectives, gather_class(): return lax.all_to_all(copies, BOTH, 0, 0, axis_index_groups=CLASSES)  29.5 us
    all_to_all x1, blocking collectives, per_device(): tiles = lax.all_to_all(copies, 'row', 0, 0)  15.4 us
    ppermute x6, waiting for transfers between devices, scatter_col(): lax.ppermute(total[d], 'col', shift_x(d))  10.6 us
    ppermute x3, waiting for transfers between devices, gather_col(): lax.ppermute(pair, 'col', shift_x(-d))  7.75 us
    ppermute x6, starting transfers between devices, scatter_col(): lax.ppermute(total[d], 'col', shift_x(d))  6.64 us
    all_to_all x1, waiting for transfers between devices, gather_class(): return lax.all_to_all(copies, BOTH, 0, 0, axis_index_groups=CLASSES)  4.95 us
    ppermute x2, waiting for transfers between devices, gather_rest(): left = lax.ppermute(upper, BOTH, shift(0, 1))  4.63 us
    unnamed x10, local copies, waits for them, and re-layouts  4.4 us
  transfers between devices with their start and end apart: 21, of which 17 were waited for; matrix products, arithmetic and copies ran while one was open for 0% of the time, Pallas kernels for 3%

profile of v6, /device:TPU:6, one launch (start us, length us, event | category | flops | bytes accessed | tf_op | source)
XLA Modules:
  0.0 120.8 jit_solution(13355793916483410319)
XLA Ops:
  1.6 29.5 %all_to_all.15.own = f32[8,64,256]{2,1,0:T(8,128)S(1)} all-to-all(f32[8,64,256]{2,1,0:T(8,128)S(1)} %broadcast_in_dim.4), channel_id=1, replica_groups={{0,136,16,152,32,168,48,184},{64,200,80,216,96,232,112,248},{128,8,144,..., dimensions={0} | all-to-all | bytes 1048576 | tf_op jit(solution)/shard_map/all_to_all | solution.py:49
  31.8 1.3 %collective-permute-start.3 = (f32[8,64,256]{2,1,0:T(8,128)S(1)}, f32[8,64,256]{2,1,0:T(8,128)S(1)}, u32[]{:S(2)}, u32[]{:S(2)}) collective-permute-start(f32[8,64,256]{2,1,0:T(8,128)S(1)} %all_to_all.15.own), channel_id=1, source_target_pairs={{0,64},{1,9},{2,66},{3,11},{4,68},{5,13},{6,70},{7,15},{8,72},{9,1... | collective-permute-start | bytes 1572872 | tf_op jit(solution)/shard_map/ppermute | solution.py:54
  33.2 2.0 %collective-permute-start.2 = (f32[4,64,256]{2,1,0:T(8,128)S(1)}, f32[4,64,256]{2,1,0:T(8,128)S(1)}, u32[]{:S(2)}, u32[]{:S(2)}) collective-permute-start(f32[4,64,256]{2,1,0:T(8,128)S(1)} %get-tuple-element.44), channel_id=1, source_target_pairs={{0,8},{1,65},{2,10},{3,67},{4,12},{5,69},{6,14},{7,71},{8,16},{9,7... | collective-permute-start | bytes 786440 | tf_op jit(solution)/shard_map/ppermute | solution.py:57
  35.3 2.2 %copy-done = f32[8,64,2048]{2,1,0:T(8,128)S(1)} copy-done((f32[8,64,2048]{2,1,0:T(8,128)S(1)}, f32[8,64,2048]{2,1,0:T(8,128)}, u32[]{:S(2)}) %copy-start) | copy-done | bytes 4194328
  37.5 1.3 %shard_map.68 = (bf16[2,4,64,2048]{3,2,1,0:T(8,128)(2,1)S(1)}, bf16[2,4,64,2048]{3,2,1,0:T(8,128)(2,1)S(1)}) custom-call(s32[3]{0:T(128)S(1)} %pad_add_fusion.place, f32[8,64,2048]{2,1,0:T(8,128)S(1)} %copy-done), custom_call_target="tpu_custom_call" | custom-call | flops 4194304 | bytes 7340032 | tf_op jit(solution)/shard_map/pallas_call | solution.py:145
  38.8 1.6 %collective-permute-done.1.right = f32[4,64,256]{2,1,0:T(8,128)S(1)} collective-permute-done((f32[4,64,256]{2,1,0:T(8,128)S(1)}, f32[4,64,256]{2,1,0:T(8,128)S(1)}, u32[]{:S(2)}, u32[]{:S(2)}) %collective-permute-start.1) | collective-permute-done | bytes 262176 | tf_op jit(solution)/shard_map/ppermute | solution.py:56
  40.4 1.2 %collective-permute-done.2.left = f32[4,64,256]{2,1,0:T(8,128)S(1)} collective-permute-done((f32[4,64,256]{2,1,0:T(8,128)S(1)}, f32[4,64,256]{2,1,0:T(8,128)S(1)}, u32[]{:S(2)}, u32[]{:S(2)}) %collective-permute-start.2) | collective-permute-done | bytes 262176 | tf_op jit(solution)/shard_map/ppermute | solution.py:57
  42.0 1.4 %collective-permute-done.3.below = f32[8,64,256]{2,1,0:T(8,128)S(1)} collective-permute-done((f32[8,64,256]{2,1,0:T(8,128)S(1)}, f32[8,64,256]{2,1,0:T(8,128)S(1)}, u32[]{:S(2)}, u32[]{:S(2)}) %collective-permute-start.3) | collective-permute-done | bytes 524320 | tf_op jit(solution)/shard_map/ppermute | solution.py:54
  43.4 1.9 %shard_map.70 = (f32[4,64,256]{2,1,0:T(8,128)S(1)}, bf16[2048,256]{1,0:T(8,128)(2,1)S(1)}, bf16[2048,256]{1,0:T(8,128)(2,1)S(1)}) custom-call(s32[3]{0:T(128)S(1)} %pad_add_fusion.place, f32[8,64,256]{2,1,0:T(8,128)S(1)} %all_to_all.15.own, f32[8,64,256]{2,1,0:T(8,128)S(1)} %collective-permute-done.above, f32[4,64,256]{2,1,0:T(8,128)S(1)} %collective-permute-done.1.right, ...), custom_call_target="tpu_custom_call" | custom-call | flops 805306368 | bytes 7340032 | tf_op jit(solution)/shard_map/pallas_call | solution.py:154
  47.0 1.5 %collective-permute-start.5 = (f32[64,256]{1,0:T(8,128)S(1)}, f32[64,256]{1,0:T(8,128)S(1)}, u32[]{:S(2)}, u32[]{:S(2)}) collective-permute-start(f32[64,256]{1,0:T(8,128)S(1)} %get-tuple-element.49), channel_id=1, source_target_pairs={{0,4},{1,5},{2,6},{3,7},{4,0},{5,1},{6,2},{7,3},{8,12},{9,13},{10,... | collective-permute-start | bytes 196616 | tf_op jit(solution)/shard_map/ppermute | solution.py:271
  48.5 2.1 %collective-permute-start.6 = (f32[64,256]{1,0:T(8,128)S(1)}, f32[64,256]{1,0:T(8,128)S(1)}, u32[]{:S(2)}, u32[]{:S(2)}) collective-permute-start(f32[64,256]{1,0:T(8,128)S(1)} %get-tuple-element.50), channel_id=1, source_target_pairs={{0,2},{1,3},{2,4},{3,5},{4,6},{5,7},{6,0},{7,1},{8,10},{9,11},{10,... | collective-permute-start | bytes 196616 | tf_op jit(solution)/shard_map/ppermute | solution.py:271
  50.7 2.3 %collective-permute-done.5.t1 = f32[64,256]{1,0:T(8,128)S(1)} collective-permute-done((f32[64,256]{1,0:T(8,128)S(1)}, f32[64,256]{1,0:T(8,128)S(1)}, u32[]{:S(2)}, u32[]{:S(2)}) %collective-permute-start.5) | collective-permute-done | bytes 65568 | tf_op jit(solution)/shard_map/ppermute | solution.py:271
  53.0 3.1 %collective-permute-done.7.t3 = f32[64,256]{1,0:T(8,128)S(1)} collective-permute-done((f32[64,256]{1,0:T(8,128)S(1)}, f32[64,256]{1,0:T(8,128)S(1)}, u32[]{:S(2)}, u32[]{:S(2)}) %collective-permute-start.7) | collective-permute-done | bytes 65568 | tf_op jit(solution)/shard_map/ppermute | solution.py:271
  56.1 1.1 shard_map.73
  57.2 4.1 %all-to-all-start.1 = ((f32[8,64,256]{2,1,0:T(8,128)}), f32[8,64,256]{2,1,0:T(8,128)S(1)}, u32[]{:S(2)}, u32[]{:S(2)}) async-start(f32[8,64,256]{2,1,0:T(8,128)} %get-tuple-element.54), calls=%async_computation.1 | async-start | bytes 1048576 | tf_op jit(solution)/shard_map/all_to_all | solution.py:49
  61.8 1.2 %collective-permute-done.8.other = f32[64,256]{1,0:T(8,128)S(1)} collective-permute-done((f32[64,256]{1,0:T(8,128)S(1)}, f32[64,256]{1,0:T(8,128)S(1)}, u32[]{:S(2)}, u32[]{:S(2)}) %collective-permute-start.8) | collective-permute-done | bytes 65568 | tf_op jit(solution)/shard_map/ppermute | solution.py:275
  63.1 1.5 %collective-permute-start.11 = (f32[2,64,256]{2,1,0:T(8,128)S(1)}, f32[2,64,256]{2,1,0:T(8,128)S(1)}, u32[]{:S(2)}, u32[]{:S(2)}) collective-permute-start(f32[2,64,256]{2,1,0:T(8,128)S(1)} %shard_map.75.refs_0_), channel_id=1, source_target_pairs={{0,2},{1,3},{2,4},{3,5},{4,6},{5,7},{6,0},{7,1},{8,10},{9,11},{10,... | collective-permute-start | bytes 393224 | tf_op jit(solution)/shard_map/ppermute | solution.py:277
  65.2 5.7 %collective-permute-done.10.refs_2_ = f32[2,64,256]{2,1,0:T(8,128)S(1)} collective-permute-done((f32[2,64,256]{2,1,0:T(8,128)S(1)}, f32[2,64,256]{2,1,0:T(8,128)S(1)}, u32[]{:S(2)}, u32[]{:S(2)}) %collective-permute-start.10) | collective-permute-done | bytes 131104 | tf_op jit(solution)/shard_map/ppermute | solution.py:277
  71.0 2.0 %collective-permute-done.9.refs_1_ = f32[2,64,256]{2,1,0:T(8,128)S(1)} collective-permute-done((f32[2,64,256]{2,1,0:T(8,128)S(1)}, f32[2,64,256]{2,1,0:T(8,128)S(1)}, u32[]{:S(2)}, u32[]{:S(2)}) %collective-permute-start.9) | collective-permute-done | bytes 131104 | tf_op jit(solution)/shard_map/ppermute | solution.py:277
  73.0 4.9 %all-to-all-done.1.own = f32[8,64,256]{2,1,0:T(8,128)S(1)} async-done(((f32[8,64,256]{2,1,0:T(8,128)}), f32[8,64,256]{2,1,0:T(8,128)S(1)}, u32[]{:S(2)}, u32[]{:S(2)}) %all-to-all-start.1) | async-done | bytes 524320 | tf_op jit(solution)/shard_map/all_to_all | solution.py:49
  77.9 1.4 %collective-permute-start.12 = (f32[8,64,256]{2,1,0:T(8,128)S(1)}, f32[8,64,256]{2,1,0:T(8,128)S(1)}, u32[]{:S(2)}, u32[]{:S(2)}) collective-permute-start(f32[8,64,256]{2,1,0:T(8,128)S(1)} %all-to-all-done.1.own), channel_id=1, source_target_pairs={{0,192},{1,57},{2,194},{3,59},{4,196},{5,61},{6,198},{7,63},{8,200... | collective-permute-start | bytes 1572872 | tf_op jit(solution)/shard_map/ppermute | solution.py:53
  80.0 1.3 %collective-permute-start.13 = (f32[4,64,256]{2,1,0:T(8,128)S(1)}, f32[4,64,256]{2,1,0:T(8,128)S(1)}, u32[]{:S(2)}, u32[]{:S(2)}) collective-permute-start(f32[4,64,256]{2,1,0:T(8,128)S(1)} %get-tuple-element.58), channel_id=1, source_target_pairs={{0,56},{1,193},{2,58},{3,195},{4,60},{5,197},{6,62},{7,199},{8,0},... | collective-permute-start | bytes 786440 | tf_op jit(solution)/shard_map/ppermute | solution.py:56
  82.1 2.2 %copy-done.1 = f32[8,64,2048]{2,1,0:T(8,128)S(1)} copy-done((f32[8,64,2048]{2,1,0:T(8,128)S(1)}, f32[8,64,2048]{2,1,0:T(8,128)}, u32[]{:S(2)}) %copy-start.1) | copy-done | bytes 4194328
  84.3 1.3 %shard_map.77 = (bf16[2,4,64,2048]{3,2,1,0:T(8,128)(2,1)S(1)}, bf16[2,4,64,2048]{3,2,1,0:T(8,128)(2,1)S(1)}) custom-call(s32[3]{0:T(128)S(1)} %pad_add_fusion.place, f32[8,64,2048]{2,1,0:T(8,128)S(1)} %copy-done.1), custom_call_target="tpu_custom_call" | custom-call | flops 4194304 | bytes 7340032 | tf_op jit(solution)/shard_map/pallas_call | solution.py:145
  85.6 2.2 %collective-permute-done.13.right = f32[4,64,256]{2,1,0:T(8,128)S(1)} collective-permute-done((f32[4,64,256]{2,1,0:T(8,128)S(1)}, f32[4,64,256]{2,1,0:T(8,128)S(1)}, u32[]{:S(2)}, u32[]{:S(2)}) %collective-permute-start.13) | collective-permute-done | bytes 262176 | tf_op jit(solution)/shard_map/ppermute | solution.py:56
  87.8 3.4 %collective-permute-done.14.left = f32[4,64,256]{2,1,0:T(8,128)S(1)} collective-permute-done((f32[4,64,256]{2,1,0:T(8,128)S(1)}, f32[4,64,256]{2,1,0:T(8,128)S(1)}, u32[]{:S(2)}, u32[]{:S(2)}) %collective-permute-start.14) | collective-permute-done | bytes 262176 | tf_op jit(solution)/shard_map/ppermute | solution.py:57
  91.4 2.9 %shard_map.78 = (f32[4,72,256]{2,1,0:T(8,128)S(1)}, f32[4,72,256]{2,1,0:T(8,128)S(1)}) custom-call(s32[3]{0:T(128)S(1)} %pad_add_fusion.place, f32[8,64,256]{2,1,0:T(8,128)S(1)} %all-to-all-done.1.own, f32[8,64,256]{2,1,0:T(8,128)S(1)} %collective-permute-done.12.above, f32[4,64,256]{2,1,0:T(8,128)S(1)} %collective-permute-done.13.right, ...), custom_call_target="tpu_custom_call" | custom-call | flops 1610612736 | bytes 7340032 | tf_op jit(solution)/shard_map/pallas_call | solution.py:166
  94.4 1.6 %collective-permute-done.16.other = f32[4,72,256]{2,1,0:T(8,128)S(1)} collective-permute-done((f32[4,72,256]{2,1,0:T(8,128)S(1)}, f32[4,72,256]{2,1,0:T(8,128)S(1)}, u32[]{:S(2)}, u32[]{:S(2)}) %collective-permute-start.16) | collective-permute-done | bytes 294944 | tf_op jit(solution)/shard_map/ppermute | solution.py:269
  97.0 1.7 %collective-permute-start.18 = (f32[72,256]{1,0:T(8,128)S(1)}, f32[72,256]{1,0:T(8,128)S(1)}, u32[]{:S(2)}, u32[]{:S(2)}) collective-permute-start(f32[72,256]{1,0:T(8,128)S(1)} %get-tuple-element.72), channel_id=1, source_target_pairs={{0,2},{1,3},{2,4},{3,5},{4,6},{5,7},{6,0},{7,1},{8,10},{9,11},{10,... | collective-permute-start | bytes 221192 | tf_op jit(solution)/shard_map/ppermute | solution.py:271
  99.1 3.1 %collective-permute-done.17.t1 = f32[72,256]{1,0:T(8,128)S(1)} collective-permute-done((f32[72,256]{1,0:T(8,128)S(1)}, f32[72,256]{1,0:T(8,128)S(1)}, u32[]{:S(2)}, u32[]{:S(2)}) %collective-permute-start.17) | collective-permute-done | bytes 73760 | tf_op jit(solution)/shard_map/ppermute | solution.py:271
  102.2 2.1 %collective-permute-done.19.t3 = f32[72,256]{1,0:T(8,128)S(1)} collective-permute-done((f32[72,256]{1,0:T(8,128)S(1)}, f32[72,256]{1,0:T(8,128)S(1)}, u32[]{:S(2)}, u32[]{:S(2)}) %collective-permute-start.19) | collective-permute-done | bytes 73760 | tf_op jit(solution)/shard_map/ppermute | solution.py:271
  104.5 15.4 %all_to_all.16.tiles = f32[32,1,128]{2,1,0:T(1,128)S(1)} all-to-all(f32[32,1,128]{2,1,0:T(1,128)S(1)} %get-tuple-element.74), channel_id=1, replica_groups=mesh['row'=32,'col'=8] {'row'}, dimensions={0} | all-to-all | bytes 32768 | tf_op jit(solution)/shard_map/all_to_all | solution.py:311
  (41 shorter events, 9.5 us)
Async XLA Ops:
  31.1 11.0 %collective-permute-start = (f32[8,64,256]{2,1,0:T(8,128)S(1)}, f32[8,64,256]{2,1,0:T(8,128)S(1)}, u32[]{:S(2)}, u32[]{:S(2)}) collective-permute-start(f32[8,64,256]{2,1,0:T(8,128)S(1)} %all_to_all.15.own), channel_id=1, source_target_pairs={{0,192},{1,57},{2,194},{3,59},{4,196},{5,61},{6,198},{7,63},{8,200... | collective-permute-start | bytes 1572872 | tf_op jit(solution)/shard_map/ppermute | solution.py:53
  31.8 11.7 %collective-permute-start.3 = (f32[8,64,256]{2,1,0:T(8,128)S(1)}, f32[8,64,256]{2,1,0:T(8,128)S(1)}, u32[]{:S(2)}, u32[]{:S(2)}) collective-permute-start(f32[8,64,256]{2,1,0:T(8,128)S(1)} %all_to_all.15.own), channel_id=1, source_target_pairs={{0,64},{1,9},{2,66},{3,11},{4,68},{5,13},{6,70},{7,15},{8,72},{9,1... | collective-permute-start | bytes 1572872 | tf_op jit(solution)/shard_map/ppermute | solution.py:54
  33.1 7.3 %collective-permute-start.1 = (f32[4,64,256]{2,1,0:T(8,128)S(1)}, f32[4,64,256]{2,1,0:T(8,128)S(1)}, u32[]{:S(2)}, u32[]{:S(2)}) collective-permute-start(f32[4,64,256]{2,1,0:T(8,128)S(1)} %get-tuple-element.43), channel_id=1, source_target_pairs={{0,56},{1,193},{2,58},{3,195},{4,60},{5,197},{6,62},{7,199},{8,0},... | collective-permute-start | bytes 786440 | tf_op jit(solution)/shard_map/ppermute | solution.py:56
  33.2 8.4 %collective-permute-start.2 = (f32[4,64,256]{2,1,0:T(8,128)S(1)}, f32[4,64,256]{2,1,0:T(8,128)S(1)}, u32[]{:S(2)}, u32[]{:S(2)}) collective-permute-start(f32[4,64,256]{2,1,0:T(8,128)S(1)} %get-tuple-element.44), channel_id=1, source_target_pairs={{0,8},{1,65},{2,10},{3,67},{4,12},{5,69},{6,14},{7,71},{8,16},{9,7... | collective-permute-start | bytes 786440 | tf_op jit(solution)/shard_map/ppermute | solution.py:57
  35.3 2.2 %copy-start = (f32[8,64,2048]{2,1,0:T(8,128)S(1)}, f32[8,64,2048]{2,1,0:T(8,128)}, u32[]{:S(2)}) copy-start(f32[8,64,2048]{2,1,0:T(8,128)} %tile.1) | copy-start | bytes 12582916
  45.3 1.6 %collective-permute-start.4 = (f32[4,64,256]{2,1,0:T(8,128)S(1)}, f32[4,64,256]{2,1,0:T(8,128)S(1)}, u32[]{:S(2)}, u32[]{:S(2)}) collective-permute-start(f32[4,64,256]{2,1,0:T(8,128)S(1)} %get-tuple-element.47), channel_id=1, source_target_pairs={{0,1},{1,0},{2,3},{3,2},{4,5},{5,4},{6,7},{7,6},{8,9},{9,8},{10,11... | collective-permute-start | bytes 786440 | tf_op jit(solution)/shard_map/ppermute | solution.py:269
  45.4 5.1 %copy-start.3 = (s32[64]{0:T(128)S(1)}, s32[64]{0:T(128)}, u32[]{:S(2)}) copy-start(s32[64]{0:T(128)} %param.7) | copy-start | bytes 772
  45.4 10.6 %copy-start.4 = (f32[64]{0:T(128)S(1)}, f32[64]{0:T(128)}, u32[]{:S(2)}) copy-start(f32[64]{0:T(128)} %param.8) | copy-start | bytes 772
  45.5 10.7 %copy-start.2 = (f32[256,256]{1,0:T(8,128)S(1)}, f32[256,256]{1,0:T(8,128)}, u32[]{:S(2)}) copy-start(f32[256,256]{1,0:T(8,128)} %kernel.5) | copy-start | bytes 786436
  47.0 6.0 %collective-permute-start.5 = (f32[64,256]{1,0:T(8,128)S(1)}, f32[64,256]{1,0:T(8,128)S(1)}, u32[]{:S(2)}, u32[]{:S(2)}) collective-permute-start(f32[64,256]{1,0:T(8,128)S(1)} %get-tuple-element.49), channel_id=1, source_target_pairs={{0,4},{1,5},{2,6},{3,7},{4,0},{5,1},{6,2},{7,3},{8,12},{9,13},{10,... | collective-permute-start | bytes 196616 | tf_op jit(solution)/shard_map/ppermute | solution.py:271
  48.5 4.5 %collective-permute-start.6 = (f32[64,256]{1,0:T(8,128)S(1)}, f32[64,256]{1,0:T(8,128)S(1)}, u32[]{:S(2)}, u32[]{:S(2)}) collective-permute-start(f32[64,256]{1,0:T(8,128)S(1)} %get-tuple-element.50), channel_id=1, source_target_pairs={{0,2},{1,3},{2,4},{3,5},{4,6},{5,7},{6,0},{7,1},{8,10},{9,11},{10,... | collective-permute-start | bytes 196616 | tf_op jit(solution)/shard_map/ppermute | solution.py:271
  50.6 5.5 %collective-permute-start.7 = (f32[64,256]{1,0:T(8,128)S(1)}, f32[64,256]{1,0:T(8,128)S(1)}, u32[]{:S(2)}, u32[]{:S(2)}) collective-permute-start(f32[64,256]{1,0:T(8,128)S(1)} %get-tuple-element.51), channel_id=1, source_target_pairs={{0,6},{1,7},{2,0},{3,1},{4,2},{5,3},{6,4},{7,5},{8,14},{9,15},{10,... | collective-permute-start | bytes 196616 | tf_op jit(solution)/shard_map/ppermute | solution.py:271
  57.2 20.7 %all-to-all-start.1 = ((f32[8,64,256]{2,1,0:T(8,128)}), f32[8,64,256]{2,1,0:T(8,128)S(1)}, u32[]{:S(2)}, u32[]{:S(2)}) async-start(f32[8,64,256]{2,1,0:T(8,128)} %get-tuple-element.54), calls=%async_computation.1 | async-start | bytes 1048576 | tf_op jit(solution)/shard_map/all_to_all | solution.py:49
  61.7 1.3 %collective-permute-start.8 = (f32[64,256]{1,0:T(8,128)S(1)}, f32[64,256]{1,0:T(8,128)S(1)}, u32[]{:S(2)}, u32[]{:S(2)}) collective-permute-start(f32[64,256]{1,0:T(8,128)S(1)} %get-tuple-element.56.image), channel_id=1, source_target_pairs={{0,1},{1,0},{2,3},{3,2},{4,5},{5,4},{6,7},{7,6},{8,9},{9,8},{10,11... | collective-permute-start | bytes 196616 | tf_op jit(solution)/shard_map/ppermute | solution.py:275
  63.0 7.9 %collective-permute-start.10 = (f32[2,64,256]{2,1,0:T(8,128)S(1)}, f32[2,64,256]{2,1,0:T(8,128)S(1)}, u32[]{:S(2)}, u32[]{:S(2)}) collective-permute-start(f32[2,64,256]{2,1,0:T(8,128)S(1)} %shard_map.75.refs_0_), channel_id=1, source_target_pairs={{0,4},{1,5},{2,6},{3,7},{4,0},{5,1},{6,2},{7,3},{8,12},{9,13},{10,... | collective-permute-start | bytes 393224 | tf_op jit(solution)/shard_map/ppermute | solution.py:277
  63.1 7.8 %collective-permute-start.11 = (f32[2,64,256]{2,1,0:T(8,128)S(1)}, f32[2,64,256]{2,1,0:T(8,128)S(1)}, u32[]{:S(2)}, u32[]{:S(2)}) collective-permute-start(f32[2,64,256]{2,1,0:T(8,128)S(1)} %shard_map.75.refs_0_), channel_id=1, source_target_pairs={{0,2},{1,3},{2,4},{3,5},{4,6},{5,7},{6,0},{7,1},{8,10},{9,11},{10,... | collective-permute-start | bytes 393224 | tf_op jit(solution)/shard_map/ppermute | solution.py:277
  64.6 8.4 %collective-permute-start.9 = (f32[2,64,256]{2,1,0:T(8,128)S(1)}, f32[2,64,256]{2,1,0:T(8,128)S(1)}, u32[]{:S(2)}, u32[]{:S(2)}) collective-permute-start(f32[2,64,256]{2,1,0:T(8,128)S(1)} %shard_map.75.refs_0_), channel_id=1, source_target_pairs={{0,6},{1,7},{2,0},{3,1},{4,2},{5,3},{6,4},{7,5},{8,14},{9,15},{10,... | collective-permute-start | bytes 393224 | tf_op jit(solution)/shard_map/ppermute | solution.py:277
  77.9 13.2 %collective-permute-start.12 = (f32[8,64,256]{2,1,0:T(8,128)S(1)}, f32[8,64,256]{2,1,0:T(8,128)S(1)}, u32[]{:S(2)}, u32[]{:S(2)}) collective-permute-start(f32[8,64,256]{2,1,0:T(8,128)S(1)} %all-to-all-done.1.own), channel_id=1, source_target_pairs={{0,192},{1,57},{2,194},{3,59},{4,196},{5,61},{6,198},{7,63},{8,200... | collective-permute-start | bytes 1572872 | tf_op jit(solution)/shard_map/ppermute | solution.py:53
  79.3 12.1 %collective-permute-start.15 = (f32[8,64,256]{2,1,0:T(8,128)S(1)}, f32[8,64,256]{2,1,0:T(8,128)S(1)}, u32[]{:S(2)}, u32[]{:S(2)}) collective-permute-start(f32[8,64,256]{2,1,0:T(8,128)S(1)} %all-to-all-done.1.own), channel_id=1, source_target_pairs={{0,64},{1,9},{2,66},{3,11},{4,68},{5,13},{6,70},{7,15},{8,72},{9,1... | collective-permute-start | bytes 1572872 | tf_op jit(solution)/shard_map/ppermute | solution.py:54
  80.0 7.8 %collective-permute-start.13 = (f32[4,64,256]{2,1,0:T(8,128)S(1)}, f32[4,64,256]{2,1,0:T(8,128)S(1)}, u32[]{:S(2)}, u32[]{:S(2)}) collective-permute-start(f32[4,64,256]{2,1,0:T(8,128)S(1)} %get-tuple-element.58), channel_id=1, source_target_pairs={{0,56},{1,193},{2,58},{3,195},{4,60},{5,197},{6,62},{7,199},{8,0},... | collective-permute-start | bytes 786440 | tf_op jit(solution)/shard_map/ppermute | solution.py:56
  81.3 9.8 %collective-permute-start.14 = (f32[4,64,256]{2,1,0:T(8,128)S(1)}, f32[4,64,256]{2,1,0:T(8,128)S(1)}, u32[]{:S(2)}, u32[]{:S(2)}) collective-permute-start(f32[4,64,256]{2,1,0:T(8,128)S(1)} %get-tuple-element.59), channel_id=1, source_target_pairs={{0,8},{1,65},{2,10},{3,67},{4,12},{5,69},{6,14},{7,71},{8,16},{9,7... | collective-permute-start | bytes 786440 | tf_op jit(solution)/shard_map/ppermute | solution.py:57
  82.1 2.2 %copy-start.1 = (f32[8,64,2048]{2,1,0:T(8,128)S(1)}, f32[8,64,2048]{2,1,0:T(8,128)}, u32[]{:S(2)}) copy-start(f32[8,64,2048]{2,1,0:T(8,128)} %tile.1) | copy-start | bytes 12582916
  94.3 1.7 %collective-permute-start.16 = (f32[4,72,256]{2,1,0:T(8,128)S(1)}, f32[4,72,256]{2,1,0:T(8,128)S(1)}, u32[]{:S(2)}, u32[]{:S(2)}) collective-permute-start(f32[4,72,256]{2,1,0:T(8,128)S(1)} %get-tuple-element.69), channel_id=1, source_target_pairs={{0,1},{1,0},{2,3},{3,2},{4,5},{5,4},{6,7},{7,6},{8,9},{9,8},{10,11... | collective-permute-start | bytes 884744 | tf_op jit(solution)/shard_map/ppermute | solution.py:269
  96.0 6.2 %collective-permute-start.17 = (f32[72,256]{1,0:T(8,128)S(1)}, f32[72,256]{1,0:T(8,128)S(1)}, u32[]{:S(2)}, u32[]{:S(2)}) collective-permute-start(f32[72,256]{1,0:T(8,128)S(1)} %get-tuple-element.71), channel_id=1, source_target_pairs={{0,4},{1,5},{2,6},{3,7},{4,0},{5,1},{6,2},{7,3},{8,12},{9,13},{10,... | collective-permute-start | bytes 221192 | tf_op jit(solution)/shard_map/ppermute | solution.py:271
  97.0 5.1 %collective-permute-start.18 = (f32[72,256]{1,0:T(8,128)S(1)}, f32[72,256]{1,0:T(8,128)S(1)}, u32[]{:S(2)}, u32[]{:S(2)}) collective-permute-start(f32[72,256]{1,0:T(8,128)S(1)} %get-tuple-element.72), channel_id=1, source_target_pairs={{0,2},{1,3},{2,4},{3,5},{4,6},{5,7},{6,0},{7,1},{8,10},{9,11},{10,... | collective-permute-start | bytes 221192 | tf_op jit(solution)/shard_map/ppermute | solution.py:271
  98.7 5.6 %collective-permute-start.19 = (f32[72,256]{1,0:T(8,128)S(1)}, f32[72,256]{1,0:T(8,128)S(1)}, u32[]{:S(2)}, u32[]{:S(2)}) collective-permute-start(f32[72,256]{1,0:T(8,128)S(1)} %get-tuple-element.73), channel_id=1, source_target_pairs={{0,6},{1,7},{2,0},{3,1},{4,2},{5,3},{6,4},{7,5},{8,14},{9,15},{10,... | collective-permute-start | bytes 221192 | tf_op jit(solution)/shard_map/ppermute | solution.py:271
